TPU v7x, 256 devices: a whole 4x4x8 slice. The times are simulated.
256 devices in a mesh: wide: 64 (over z, x, core), narrow: 4 (over y).
Axes of the slice: x: 4, y: 4, z: 8, core: 2. Of those that a mesh axis runs over, the one named last changes fastest.
Arguments:
- gebhart: float32 [16384, 16384], P('wide', 'narrow'), may hold values from 0 to 2
- change: float32 [16384, 128], P('narrow'), may hold values from -0.0007324219 to 0.0007324219
- moved_nodes: int32 [128], replicated, may hold values from 0 to 16383, as said below
Outputs:
- updated: float32 [16384, 16384], P('wide', 'narrow')
Inputs may be any that keep to these rules, and one draw needn't show every extreme that they name: `moved_nodes`: distinct node indices.
All inputs are finite; a program needn't handle non-finite values.
Results may differ from a plain program's by a relative error of at most 0.00005.
Values sent between devices are 32-bit elements; how exact they have to be, the bound alone decides.
No kernel may reach another device: no remote copies, remote signals or barrier semaphores. Data moves between devices by JAX's collectives and lax.ppermute only.
A program may use at most 64 MiB of HBM per device.

v0:
```python
import jax
import jax.numpy as jnp
from jax import lax
from jax.sharding import PartitionSpec as P


def body(gebhart, change, moved_nodes):
    high = lax.Precision.HIGHEST
    rows_local = gebhart.shape[0]
    moved_count = moved_nodes.shape[0]
    row_first = lax.axis_index("wide") * rows_local
    positions = row_first + lax.broadcasted_iota(jnp.int32, (moved_count, rows_local), 1)
    select = (moved_nodes[:, None] == positions).astype(jnp.float32)
    picked = jnp.dot(select, gebhart, preferred_element_type=jnp.float32, precision=high)
    rows_moved = lax.psum(picked, "wide")
    partial_value = jnp.dot(gebhart, change, preferred_element_type=jnp.float32, precision=high)
    response = lax.psum(partial_value, "narrow")
    terms = jnp.dot(select, response, preferred_element_type=jnp.float32, precision=high)
    touched = lax.psum(terms, "wide")
    capacitance = jnp.eye(moved_count, dtype=jnp.float32) - touched
    normal = jnp.dot(capacitance, capacitance.T, precision=high)
    factor = jnp.linalg.cholesky(normal)
    right = jnp.dot(capacitance, response.T, precision=high)
    solved = jax.scipy.linalg.cho_solve((factor, True), right).T
    return gebhart + jnp.dot(solved, rows_moved, preferred_element_type=jnp.float32, precision=high)


def solution(mesh):
    return jax.shard_map(
        body,
        mesh=mesh,
        in_specs=(P("wide", "narrow"), P("narrow", None), P()),
        out_specs=P("wide", "narrow"),
        check_vma=False,
    )
```

profile of v0, /device:TPU:3, one launch (start us, length us, event | category | flops | bytes accessed | tf_op | source)
XLA Modules:
  0.0 296.5 jit_solution(3329231226741725784)
XLA Ops:
  6.5 0.0 copy-start
  6.5 0.0 copy-start.1
  6.5 0.0 all-reduce.4.cloned.1.call-start
  6.5 1.6 copy-done
  8.1 5.9 %fusion.16 = f32[256,128]{1,0:T(8,128)} fusion(f32[256,4096]{1,0:T(8,128)} %param.3, f32[4096,128]{1,0:T(8,128)S(1)} %copy-done), kind=kOutput, calls=%fused_computation.25 | convolution fusion | flops 1610612736 | bytes 6422528 | tf_op jit(solution)/shard_map/dot_general | solution.py:16
  14.0 0.0 all-reduce.4.cloned.1.call-update
  14.0 0.0 all-reduce.6.cloned.1.call-start
  14.1 0.0 copy-done.1
  14.1 5.2 %fusion = f32[128,4096]{1,0:T(8,128)} fusion(f32[256,4096]{1,0:T(8,128)} %param.3, s32[256]{0:T(256)S(1)} %iota_add_fusion, s32[128]{0:T(128)S(1)} %copy-done.1), kind=kOutput, calls=%fused_computation.1 | convolution fusion | flops 1610645504 | bytes 6292992 | tf_op jit(solution)/shard_map/dot_general | solution.py:14
  19.3 42.0 %all-reduce.4.cloned.1.call-done = f32[256,128]{1,0:T(8,128)} async-done(((f32[256,128]{1,0:T(8,128)}), f32[256,128]{1,0:T(8,128)}) %all-reduce.4.cloned.1.call-update) | async-done | bytes 131088 | tf_op jit(solution)/shard_map/psum | solution.py:17
  61.4 1.8 fusion.2
  63.1 0.0 all-reduce.6.cloned.1.call-update
  63.2 193.2 %all-reduce.6.cloned.1.call-done = (f32[128,128]{1,0:T(8,128)}, f32[128,4096]{1,0:T(8,128)}) async-done(((f32[128,128]{1,0:T(8,128)}, f32[128,4096]{1,0:T(8,128)}), (f32[128,128]{1,0:T(8,128)}, f32[128,4096]{1,0:T(8,128)})) %all-reduce.6.cloned.1.call-update) | async-done | bytes 2162704 | tf_op jit(solution)/shard_map/psum | solution.py:19
  256.3 1.2 fusion.15
  257.5 0.1 copy.4
  257.6 11.7 %cholesky.17 = f32[128,128]{1,0:T(8,128)S(1)} custom-call(f32[128,128]{1,0:T(8,128)S(1)} %fusion.9), custom_call_target="Cholesky" | custom-call | tf_op jit(solution)/shard_map/jit(cholesky)/cholesky | solution.py:22
  269.4 0.6 compare_reduce_fusion
  270.0 0.7 fusion.4
  270.7 9.8 %custom-call.10 = f32[1,128,128]{1,2,0:T(8,128)S(1)} custom-call(f32[1,128,128]{2,1,0:T(8,128)S(1)} %fusion.4), custom_call_target="InvertDiagBlocksLowerTriangular" | custom-call | tf_op jit(solution)/shard_map/jit(_cho_solve)/triangular_solve | solution.py:24
  280.5 1.2 fusion.14
  281.7 0.3 fusion.7
  282.1 0.3 fusion.5
  282.3 7.4 %convolution_add_fusion = f32[256,4096]{1,0:T(8,128)} fusion(f32[256,4096]{1,0:T(8,128)} %param.3, f32[128,256]{1,0:T(8,128)S(1)} %fusion.5, f32[128,4096]{1,0:T(8,128)} %get-tuple-element.6), kind=kOutput, calls=%fused_computation | convolution fusion | flops 1611661312 | bytes 10616832 | tf_op jit(solution)/shard_map/dot_general | solution.py:25
  (3 shorter events, 0.1 us)
Async XLA Ops:
  6.5 1.6 copy-start
  6.5 7.5 %copy-start.1 = (s32[128]{0:T(128)S(1)}, s32[128]{0:T(128)}, u32[]{:S(2)}) copy-start(s32[128]{0:T(128)} %param.5) | copy-start | bytes 1540
  6.5 54.8 %all-reduce.4.cloned.1.call-start = ((), (), s32[]{:S(2)}) async-start(), calls=%async_computation | async-start | bytes 262144 | tf_op jit(solution)/shard_map/psum | solution.py:17
  14.0 242.3 %all-reduce.6.cloned.1.call-start = ((), (), s32[]{:S(2)}) async-start(), calls=%async_computation.1 | async-start | bytes 4325376 | tf_op jit(solution)/shard_map/psum | solution.py:19
Sparse Core Ops, SparseCore 0:
  14.1 47.1 all-reduce.3
  65.4 190.9 all-reduce.5
where the time goes:
time: 298 us; the launch traced here: 297 us
  waiting for transfers between devices  235 us (79%)
  matrix products  23.2 us (8%)
  other arithmetic  22.9 us (8%)
  between operations  13.5 us (5%)
    psum x1, waiting for transfers between devices, body(): touched = lax.psum(terms, 'wide')  193 us
    psum x1, waiting for transfers between devices, body(): response = lax.psum(partial_value, 'narrow')  42 us
    another operation x3, other arithmetic, body(): factor = jnp.linalg.cholesky(normal)  12.4 us
    another operation x2, other arithmetic, body(): solved = jax.scipy.linalg.cho_solve((factor, True), right).T  10.5 us
    dot_general x1, matrix products, body(): jnp.dot(solved, rows_moved, preferred_element_type=jnp.float32, precision...  7.38 us
  transfers between devices with their start and end apart: 2, of which 2 were waited for; matrix products, arithmetic and copies ran while one was open for 2% of the time, Pallas kernels for 0%

commit v1 on v0

v1 whole, which is shorter than its diff:
```python
import functools

import jax
import jax.numpy as jnp
from jax import lax
from jax.experimental import pallas as pl
from jax.experimental.pallas import tpu as pltpu
from jax.sharding import PartitionSpec as P

CORES = 2
XS = 4


def pick_kernel(moved_ref, place_ref, g_ref, keep_ref, send_ref, sem):
    rows_local = g_ref.shape[0]
    quarters, half, width = keep_ref.shape
    first = place_ref[0]
    core = place_ref[1]

    def copies(k, act):
        local = moved_ref[k] - first
        owned = jnp.logical_and(local >= 0, local < rows_local)
        side = k // half
        row = k - side * half
        for target, here in ((keep_ref, side == core), (send_ref, side != core)):
            @pl.when(jnp.logical_and(owned, here))
            def _():
                for q in range(quarters):
                    act(pltpu.make_async_copy(
                        g_ref.at[pl.ds(local, 1), pl.ds(q * width, width)],
                        target.at[q, pl.ds(row, 1), :],
                        sem,
                    ))

    def start(k, carry):
        copies(k, lambda copy: copy.start())
        return carry

    def wait(k, carry):
        copies(k, lambda copy: copy.wait())
        return carry

    lax.fori_loop(0, 2 * half, start, 0)
    lax.fori_loop(0, 2 * half, wait, 0)


def pick(gebhart, moved_nodes, place, half, width):
    shape = jax.ShapeDtypeStruct((XS, half, width), jnp.float32)
    return pl.pallas_call(
        pick_kernel,
        out_shape=(shape, shape),
        in_specs=[
            pl.BlockSpec(memory_space=pltpu.SMEM),
            pl.BlockSpec(memory_space=pltpu.SMEM),
            pl.BlockSpec(memory_space=pl.ANY),
        ],
        out_specs=(pl.BlockSpec(memory_space=pl.ANY), pl.BlockSpec(memory_space=pl.ANY)),
        scratch_shapes=[pltpu.SemaphoreType.DMA],
        name="pick_rows",
    )(moved_nodes, place, gebhart)


def split(value):
    high = value.astype(jnp.bfloat16)
    low = (value - high.astype(jnp.float32)).astype(jnp.bfloat16)
    return high, low


def update_kernel(column_ref, core_ref, solved_ref, g_ref, *refs):
    mine, theirs, out_ref = refs[:XS], refs[XS:2 * XS], refs[2 * XS]
    half = mine[0].shape[0]
    step = pl.program_id(0)
    core = core_ref[0]
    s_low_half = solved_ref[:, :half]
    s_high_half = solved_ref[:, half:]
    s_mine = jnp.where(core == 0, s_low_half, s_high_half)
    s_theirs = jnp.where(core == 0, s_high_half, s_low_half)
    s_high, s_low = split(jnp.concatenate([s_mine, s_theirs], axis=1))
    left = jnp.concatenate([s_high, s_low, s_high], axis=1)
    for j in range(XS):
        @pl.when(step == j)
        def _():
            r_high, r_low = split(jnp.concatenate([mine[j][...], theirs[j][...]], axis=0))
            right = jnp.concatenate([r_high, r_high, r_low], axis=0)
            out_ref[...] = g_ref[...] + jnp.dot(left, right, preferred_element_type=jnp.float32)


def update(gebhart, solved, mine, theirs, columns, core):
    rows, nodes = gebhart.shape
    half, width = mine[0].shape
    count = solved.shape[1]
    piece = pl.BlockSpec((half, width), lambda i, col, core: (0, 0))
    block = pl.BlockSpec((rows, width), lambda i, col, core: (0, col[i]))
    return pl.pallas_call(
        update_kernel,
        out_shape=jax.ShapeDtypeStruct((rows, nodes), jnp.float32),
        grid_spec=pltpu.PrefetchScalarGridSpec(
            num_scalar_prefetch=2,
            grid=(XS,),
            in_specs=[pl.BlockSpec((rows, count), lambda i, col, core: (0, 0)), block] + [piece] * (2 * XS),
            out_specs=block,
        ),
        compiler_params=pltpu.CompilerParams(vmem_limit_bytes=40 * 1024 * 1024),
        name="update_rows",
    )(columns, core, solved, gebhart, *mine, *theirs)


def invert(touched):
    high = lax.Precision.HIGHEST
    count = touched.shape[0]
    capacitance = jnp.eye(count, dtype=jnp.float32) - touched
    normal = jnp.dot(capacitance, capacitance.T, precision=high)
    factor = jnp.linalg.cholesky(normal)
    return jax.scipy.linalg.cho_solve((factor, True), capacitance)


def body(wide, narrow, gebhart, change, moved_nodes):
    high = lax.Precision.HIGHEST
    rows_local, width_local = gebhart.shape
    count = moved_nodes.shape[0]
    half = count // CORES
    zs = wide // (CORES * XS)
    width = width_local // XS
    group = half // zs
    me = lax.axis_index("wide")
    core = me % CORES
    x = (me // CORES) % XS
    z = me // (CORES * XS)

    def along(step):
        return [(i, step(i // (CORES * XS), (i // CORES) % XS, i % CORES)) for i in range(wide)]

    def index(z, x, c):
        return (z * XS + x) * CORES + c

    swap = along(lambda z, x, c: index(z, x, (c + 1) % CORES))
    shift_x = [along(lambda z, x, c, d=d: index(z, (x + d) % XS, c)) for d in range(XS)]
    z_groups = [[index(z, x, c) for z in range(zs)] for x in range(XS) for c in range(CORES)]

    owner = moved_nodes // rows_local
    owner_half = lax.dynamic_slice(owner, (core * half,), (half,))
    owner_core = owner_half % CORES
    owner_x = (owner_half // CORES) % XS
    owner_z = owner_half // (CORES * XS)

    place = jnp.stack([me * rows_local, core]).astype(jnp.int32)
    keep, send = pick(gebhart, moved_nodes, place, half, width)
    got = lax.ppermute(send, "wide", swap)

    partial_value = jnp.dot(gebhart, change, preferred_element_type=jnp.float32, precision=lax.Precision.HIGH)
    response = partial_value
    for d in range(1, narrow):
        response = response + lax.ppermute(partial_value, "narrow", [(i, (i + d) % narrow) for i in range(narrow)])
    positions = me * rows_local + lax.broadcasted_iota(jnp.int32, (count, rows_local), 1)
    select = (moved_nodes[:, None] == positions).astype(jnp.float32)
    terms = jnp.dot(select, response, preferred_element_type=jnp.float32, precision=high)
    terms_mine = lax.dynamic_slice(terms, (core * half, 0), (half, count))
    terms_theirs = lax.dynamic_slice(terms, ((1 - core) * half, 0), (half, count))
    terms_chip = terms_mine + lax.ppermute(terms_theirs, "wide", swap)
    terms_x = terms_chip
    for d in range(1, XS):
        terms_x = terms_x + lax.ppermute(terms_chip, "wide", shift_x[d])

    from_mine = (owner_core == core)[:, None]
    slots = []
    for d in range(XS):
        q = (x + d) % XS
        kept = lax.dynamic_index_in_dim(keep, q, 0, keepdims=False)
        other = lax.dynamic_index_in_dim(got, q, 0, keepdims=False)
        slots.append(jnp.where(from_mine, kept, other))
    rows_x = slots[0]
    far = ((x - owner_x) % XS)[:, None]
    for d in range(1, XS):
        rows_x = jnp.where(far == d, lax.ppermute(slots[d], "wide", shift_x[d]), rows_x)

    both = jnp.concatenate([rows_x, terms_x], axis=1).reshape(zs, group, width + count)
    both = lax.all_to_all(both, "wide", 0, 0, axis_index_groups=z_groups)
    owner_z_mine = lax.dynamic_slice(owner_z, (z * group,), (group,))
    chosen = owner_z_mine[None, :, None] == lax.broadcasted_iota(jnp.int32, (zs, 1, 1), 0)
    mine = jnp.sum(jnp.where(chosen, both, 0.0), axis=0)
    both = lax.all_to_all(jnp.broadcast_to(mine[None], (zs,) + mine.shape), "wide", 0, 0, axis_index_groups=z_groups)
    both = both.reshape(half, width + count)

    touched_mine = both[:, width:]
    touched_theirs = lax.ppermute(touched_mine, "wide", swap)
    touched = jnp.where(core == 0, jnp.concatenate([touched_mine, touched_theirs]), jnp.concatenate([touched_theirs, touched_mine]))

    piece = both[:, :width]
    pieces = [piece] + [lax.ppermute(piece, "wide", shift_x[d]) for d in range(1, XS)]
    theirs = [lax.ppermute(p, "wide", swap) for p in pieces]
    columns = jnp.stack([(x - d) % XS for d in range(XS)]).astype(jnp.int32)

    inverse = invert(touched)
    solved = jnp.dot(response, inverse.T, precision=high)
    return update(gebhart, solved, pieces, theirs, columns, core.reshape(1).astype(jnp.int32))


def solution(mesh):
    return jax.shard_map(
        functools.partial(body, mesh.shape["wide"], mesh.shape["narrow"]),
        mesh=mesh,
        in_specs=(P("wide", "narrow"), P("narrow", None), P()),
        out_specs=P("wide", "narrow"),
        check_vma=False,
    )
```

time: 298 us -> 136 us (0.46)
  waiting for transfers between devices: 235 us -> 32.1 us
  starting transfers between devices: 0.04 us -> 33.7 us
  other arithmetic: 22.9 us -> 39 us
  matrix products: 23.2 us -> 8.65 us
  between operations: 13.5 us -> 0.31 us
  Pallas kernels: 0 us -> 13.1 us
  local copies, waits for them, and re-layouts: 1.68 us -> 7.44 us
    psum x2 -> x0, waiting for transfers between devices: 235 us -> none  [the longest x1 193 us: body(): touched = lax.psum(terms, 'wide')]
    ppermute x0 -> x19, starting transfers between devices: none -> 22.1 us  [the longest x3 4.05 us: body(): lax.ppermute(piece, 'wide', shift_x[d])]
    all_to_all x0 -> x2, waiting for transfers between devices: none -> 20.6 us  [the longest x1 10.7 us: body(): both = lax.all_to_all(both, 'wide', 0, 0, axis_index_groups=z_groups)]
    dot_general x5 -> x3, matrix products: 20.9 us -> 6.22 us  [the longest x1 4.02 us: body(): jnp.dot(gebhart, change, preferred_element_type=jnp.float32, precision=la...]
    pallas_call x0 -> x2, Pallas kernels: none -> 13.1 us  [the longest x1 8.63 us: pick(): pl.pallas_call(pick_kernel, out_shape=(shape, shape), in_specs=[pl.BlockS...]
    all_to_all x0 -> x2, starting transfers between devices: none -> 11.6 us  [the longest x1 8.19 us: body(): both = lax.all_to_all(both, 'wide', 0, 0, axis_index_groups=z_groups)]
    ppermute x0 -> x19, waiting for transfers between devices: none -> 11.6 us  [the longest x3 11 us: body(): lax.ppermute(slots[d], 'wide', shift_x[d])]
    another operation x5 -> x7, other arithmetic: 22.9 us -> 28.7 us  [the longest x3 14.7 us: invert(): factor = jnp.linalg.cholesky(normal)]
  transfers between devices with their start and end apart: 2 -> 21, of which waited for: 2 -> 6; matrix products, arithmetic and copies ran while one was open for 2% -> 32% of each run, Pallas kernels for 0% -> 6%
where the time goes in v1:
time: 136 us; the launch traced here: 134 us
  other arithmetic  39 us (29%)
  starting transfers between devices  33.7 us (25%)
  waiting for transfers between devices  32.1 us (24%)
  Pallas kernels  13.1 us (10%)
  matrix products  8.65 us (6%)
  local copies, waits for them, and re-layouts  7.44 us (5%)
    another operation x3, other arithmetic, invert(): factor = jnp.linalg.cholesky(normal)  14.7 us
    another operation x2, other arithmetic, invert(): return jax.scipy.linalg.cho_solve((factor, True), capacitance)  13.3 us
    ppermute x3, waiting for transfers between devices, body(): lax.ppermute(slots[d], 'wide', shift_x[d])  11 us
    all_to_all x1, waiting for transfers between devices, body(): both = lax.all_to_all(both, 'wide', 0, 0, axis_index_groups=z_groups)  10.7 us
    all_to_all x1, waiting for transfers between devices, body(): lax.all_to_all(jnp.broadcast_to(mine[None], (zs,) + mine.shape), 'wide',...  9.84 us
    pallas_call x1, Pallas kernels, pick(): pl.pallas_call(pick_kernel, out_shape=(shape, shape), in_specs=[pl.BlockS...  8.63 us
    all_to_all x1, starting transfers between devices, body(): both = lax.all_to_all(both, 'wide', 0, 0, axis_index_groups=z_groups)  8.19 us
    unnamed x12, local copies, waits for them, and re-layouts  4.43 us
  transfers between devices with their start and end apart: 21, of which 6 were waited for; matrix products, arithmetic and copies ran while one was open for 32% of the time, Pallas kernels for 6%

profile of v1, /device:TPU:3, one launch (start us, length us, event | category | flops | bytes accessed | tf_op | source)
XLA Modules:
  0.0 134.2 jit_solution(8000040347901324611)
XLA Ops:
  0.0 1.6 %copy-done = f32[4096,128]{1,0:T(8,128)S(1)} copy-done((f32[4096,128]{1,0:T(8,128)S(1)}, f32[4096,128]{1,0:T(8,128)}, u32[]{:S(2)}) %copy-start) | copy-done | bytes 2097176
  1.6 4.0 %fusion.23 = f32[256,128]{1,0:T(8,128)S(1)} fusion(f32[256,4096]{1,0:T(8,128)} %g_ref.3, f32[4096,128]{1,0:T(8,128)S(1)} %copy-done), kind=kOutput, calls=%fused_computation.64 | convolution fusion | flops 805306368 | bytes 6422528 | tf_op jit(solution)/shard_map/dot_general | solution.py:150
  5.6 2.8 %collective-permute-start.2 = (f32[256,128]{1,0:T(8,128)S(1)}, f32[256,128]{1,0:T(8,128)S(1)}, u32[]{:S(2)}, u32[]{:S(2)}) collective-permute-start(f32[256,128]{1,0:T(8,128)S(1)} %fusion.23), channel_id=1, source_target_pairs={{0,3},{1,0},{2,1},{3,2},{4,7},{5,4},{6,5},{7,6},{8,11},{9,8},{10,9... | collective-permute-start | bytes 393224 | tf_op jit(solution)/shard_map/ppermute | solution.py:153
  8.8 0.7 collective-permute-start
  9.5 0.6 pad_add_fusion.1.place_ref
  10.1 8.6 %pick_rows.1 = (f32[4,64,1024]{2,1,0:T(8,128)}, f32[4,64,1024]{2,1,0:T(8,128)}) custom-call(s32[128]{0:T(128)} %moved_ref.1, s32[2]{0:T(128)} %pad_add_fusion.1.place_ref, f32[256,4096]{1,0:T(8,128)} %g_ref.3), custom_call_target="tpu_custom_call" | custom-call | tf_op jit(solution)/shard_map/pick_rows/pallas_call | solution.py:49
  18.7 1.6 %collective-permute-start.3 = (f32[4,64,1024]{2,1,0:T(8,128)}, f32[4,64,1024]{2,1,0:T(8,128)S(1)}, u32[]{:S(2)}, u32[]{:S(2)}) collective-permute-start(f32[4,64,1024]{2,1,0:T(8,128)} %get-tuple-element.8), channel_id=1, source_target_pairs={{0,4},{4,0},{8,12},{12,8},{16,20},{20,16},{24,28},{28,24},{32,36},... | collective-permute-start | bytes 3145736 | tf_op jit(solution)/shard_map/ppermute | solution.py:148
  20.4 0.6 copy-done.3
  21.1 1.0 add_add_fusion
  22.5 0.7 broadcast_compare_fusion.1
  23.1 0.5 collective-permute-done.7
  23.7 0.6 dynamic-slice_add_fusion
  24.5 2.1 %collective-permute-start.9 = (f32[64,128]{1,0:T(8,128)}, f32[64,128]{1,0:T(8,128)}, u32[]{:S(2)}, u32[]{:S(2)}) collective-permute-start(f32[64,128]{1,0:T(8,128)} %dynamic-slice_add_fusion), channel_id=1, source_target_pairs={{0,16},{4,20},{8,24},{12,28},{16,0},{20,4},{24,8},{28,12},{32,48},... | collective-permute-start | bytes 98312 | tf_op jit(solution)/shard_map/ppermute | solution.py:162
  26.7 1.5 %collective-permute-start.8 = (f32[64,128]{1,0:T(8,128)}, f32[64,128]{1,0:T(8,128)}, u32[]{:S(2)}, u32[]{:S(2)}) collective-permute-start(f32[64,128]{1,0:T(8,128)} %dynamic-slice_add_fusion), channel_id=1, source_target_pairs={{0,8},{4,12},{8,16},{12,20},{16,24},{20,28},{24,0},{28,4},{32,40},... | collective-permute-start | bytes 98312 | tf_op jit(solution)/shard_map/ppermute | solution.py:162
  28.2 2.1 %bitcast_select_fusion.1 = (f32[64,1024]{1,0:T(8,128)}, f32[64,1024]{1,0:T(8,128)}, f32[64,1024]{1,0:T(8,128)}) fusion(f32[4,64,1024]{2,1,0:T(8,128)S(1)} %collective-permute-done.3, s32[]{:T(128)S(6)} %select_n.164, f32[4,64,1024]{2,1,0:T(8,128)} %get-tuple-element.7, pred[64]{0:T(512)(128)(4,1)S(1)} %get-tuple-element.16, s32[]{:T(128)S(6)} %select_n.161, ...), kind=kLoop, calls=%fused_computation.6 | loop fusion | flops 196608 | bytes 2359372 | tf_op jit(solution)/shard_map/jit(_where)/select_n | solution.py:170
  30.3 1.7 %collective-permute-start.5 = (f32[64,1024]{1,0:T(8,128)}, f32[64,1024]{1,0:T(8,128)}, u32[]{:S(2)}, u32[]{:S(2)}) collective-permute-start(f32[64,1024]{1,0:T(8,128)} %get-tuple-element.12), channel_id=1, source_target_pairs={{0,16},{4,20},{8,24},{12,28},{16,0},{20,4},{24,8},{28,12},{32,48},... | collective-permute-start | bytes 786440 | tf_op jit(solution)/shard_map/ppermute | solution.py:174
  32.0 1.5 %collective-permute-start.4 = (f32[64,1024]{1,0:T(8,128)}, f32[64,1024]{1,0:T(8,128)}, u32[]{:S(2)}, u32[]{:S(2)}) collective-permute-start(f32[64,1024]{1,0:T(8,128)} %get-tuple-element.13), channel_id=1, source_target_pairs={{0,24},{4,28},{8,0},{12,4},{16,8},{20,12},{24,16},{28,20},{32,56},... | collective-permute-start | bytes 786440 | tf_op jit(solution)/shard_map/ppermute | solution.py:174
  33.5 0.7 broadcast_compare_fusion
  34.2 0.8 add_add_fusion.1
  35.0 2.4 %collective-permute-done.6 = f32[64,1024]{1,0:T(8,128)S(1)} collective-permute-done((f32[64,1024]{1,0:T(8,128)}, f32[64,1024]{1,0:T(8,128)S(1)}, u32[]{:S(2)}, u32[]{:S(2)}) %collective-permute-start.6) | collective-permute-done | bytes 262176 | tf_op jit(solution)/shard_map/ppermute | solution.py:174
  37.4 1.5 %collective-permute-done.5 = f32[64,1024]{1,0:T(8,128)} collective-permute-done((f32[64,1024]{1,0:T(8,128)}, f32[64,1024]{1,0:T(8,128)}, u32[]{:S(2)}, u32[]{:S(2)}) %collective-permute-start.5) | collective-permute-done | bytes 262176 | tf_op jit(solution)/shard_map/ppermute | solution.py:174
  38.9 7.0 %collective-permute-done.4 = f32[64,1024]{1,0:T(8,128)} collective-permute-done((f32[64,1024]{1,0:T(8,128)}, f32[64,1024]{1,0:T(8,128)}, u32[]{:S(2)}, u32[]{:S(2)}) %collective-permute-start.4) | collective-permute-done | bytes 262176 | tf_op jit(solution)/shard_map/ppermute | solution.py:174
  46.0 1.3 fusion.2
  47.3 0.7 maximum_bitcast_fusion
  48.0 8.2 %all-to-all-start = ((f32[8,8,1152]{2,1,0:T(8,128)}), f32[8,8,1152]{2,1,0:T(8,128)S(1)}, u32[]{:S(2)}, u32[]{:S(2)}) async-start(f32[8,8,1152]{2,1,0:T(8,128)} %maximum_bitcast_fusion), calls=%async_computation | async-start | bytes 589824 | tf_op jit(solution)/shard_map/all_to_all | solution.py:177
  56.2 0.8 and_select_fusion.4
  57.0 10.7 %all-to-all-done = f32[8,8,1152]{2,1,0:T(8,128)S(1)} async-done(((f32[8,8,1152]{2,1,0:T(8,128)}), f32[8,8,1152]{2,1,0:T(8,128)S(1)}, u32[]{:S(2)}, u32[]{:S(2)}) %all-to-all-start) | async-done | bytes 294944 | tf_op jit(solution)/shard_map/all_to_all | solution.py:177
  67.9 0.7 broadcast_in_dim.62
  68.6 3.4 %all-to-all-start.1 = ((f32[8,8,1152]{2,1,0:T(8,128)}), f32[8,8,1152]{2,1,0:T(8,128)S(1)}, u32[]{:S(2)}, u32[]{:S(2)}) async-start(f32[8,8,1152]{2,1,0:T(8,128)} %broadcast_in_dim.62), calls=%async_computation.1 | async-start | bytes 589824 | tf_op jit(solution)/shard_map/all_to_all | solution.py:181
  72.1 9.8 %all-to-all-done.1 = f32[8,8,1152]{2,1,0:T(8,128)S(1)} async-done(((f32[8,8,1152]{2,1,0:T(8,128)}), f32[8,8,1152]{2,1,0:T(8,128)S(1)}, u32[]{:S(2)}, u32[]{:S(2)}) %all-to-all-start.1) | async-done | bytes 294944 | tf_op jit(solution)/shard_map/all_to_all | solution.py:181
  81.9 0.6 slice.26
  82.6 3.6 %collective-permute-start.11 = (f32[64,128]{1,0:T(8,128)}, f32[64,128]{1,0:T(8,128)}, u32[]{:S(2)}, u32[]{:S(2)}) collective-permute-start(f32[64,128]{1,0:T(8,128)} %slice.26), channel_id=1, source_target_pairs={{0,4},{4,0},{8,12},{12,8},{16,20},{20,16},{24,28},{28,24},{32,36},... | collective-permute-start | bytes 98312 | tf_op jit(solution)/shard_map/ppermute | solution.py:185
  86.6 1.8 %collective-permute-start.13 = (f32[64,1024]{1,0:T(8,128)S(1)}, f32[64,1024]{1,0:T(8,128)S(1)}, u32[]{:S(2)}, u32[]{:S(2)}) collective-permute-start(f32[64,1024]{1,0:T(8,128)S(1)} %slice.27.refs_0_), channel_id=1, source_target_pairs={{0,16},{4,20},{8,24},{12,28},{16,0},{20,4},{24,8},{28,12},{32,48},... | collective-permute-start | bytes 786440 | tf_op jit(solution)/shard_map/ppermute | solution.py:189
  88.4 2.0 %collective-permute-start.12 = (f32[64,1024]{1,0:T(8,128)S(1)}, f32[64,1024]{1,0:T(8,128)S(1)}, u32[]{:S(2)}, u32[]{:S(2)}) collective-permute-start(f32[64,1024]{1,0:T(8,128)S(1)} %slice.27.refs_0_), channel_id=1, source_target_pairs={{0,8},{4,12},{8,16},{12,20},{16,24},{20,28},{24,0},{28,4},{32,40},... | collective-permute-start | bytes 786440 | tf_op jit(solution)/shard_map/ppermute | solution.py:189
  90.4 1.9 %fusion.15 = f32[128,128]{1,0:T(8,128)} fusion(f32[64,128]{1,0:T(8,128)} %collective-permute-done.11, f32[64,128]{1,0:T(8,128)} %slice.26, pred[]{:T(512)S(6)} %eq.66), kind=kOutput, calls=%fused_computation.29 | convolution fusion | flops 25264128 | bytes 131073 | tf_op jit(solution)/shard_map/dot_general | solution.py:112
  92.3 1.6 %copy.4 = f32[128,128]{0,1:T(8,128)} copy(f32[128,128]{1,0:T(8,128)} %fusion.15) | data formatting | bytes 131072 | tf_op jit(solution)/shard_map/dot_general | solution.py:112
  93.9 1.5 %fusion.11 = f32[128,128]{1,0:T(8,128)} fusion(f32[128,128]{1,0:T(8,128)} %fusion.15, f32[128,128]{0,1:T(8,128)} %copy.4), kind=kLoop, calls=%fused_computation.21 | loop fusion | flops 32768 | bytes 196608 | tf_op jit(solution)/shard_map/jit(cholesky)/div | solution.py:113
  95.4 13.2 %cholesky.17 = f32[128,128]{1,0:T(8,128)} custom-call(f32[128,128]{1,0:T(8,128)} %fusion.11), custom_call_target="Cholesky" | custom-call | tf_op jit(solution)/shard_map/jit(cholesky)/cholesky | solution.py:113
  108.5 0.9 select_reduce_fusion.1
  109.4 0.6 compare_reduce_fusion
  110.0 2.1 %fusion.5 = f32[1,128,128]{2,1,0:T(8,128)} fusion(f32[128,128]{1,0:T(8,128)} %cholesky.17, pred[]{:T(512)} %compare_reduce_fusion), kind=kLoop, calls=%fused_computation.13 | loop fusion | flops 65536 | bytes 131073 | tf_op jit(solution)/shard_map/jit(_cho_solve)/triangular_solve | solution.py:114
  112.1 11.3 %custom-call.10 = f32[1,128,128]{1,2,0:T(8,128)} custom-call(f32[1,128,128]{2,1,0:T(8,128)} %fusion.5), custom_call_target="InvertDiagBlocksLowerTriangular" | custom-call | tf_op jit(solution)/shard_map/jit(_cho_solve)/triangular_solve | solution.py:114
  123.4 1.1 fusion.9
  124.5 1.2 collective-permute-start.18
  125.8 0.4 collective-permute-start.16
  126.2 1.0 fusion.7
  127.6 2.2 %copy-done.1 = f32[256,4096]{1,0:T(8,128)S(1)} copy-done((f32[256,4096]{1,0:T(8,128)S(1)}, f32[256,4096]{1,0:T(8,128)}, u32[]{:S(2)}) %copy-start.1) | copy-done | bytes 4194328
  129.8 4.4 %update_rows.1 = f32[256,4096]{1,0:T(8,128)} custom-call(s32[4]{0:T(128)S(1)} %pad_add_fusion.column_ref, s32[1]{0:T(128)} %bitcast.4.core_ref, f32[256,128]{1,0:T(8,128)S(1)} %fusion.24.solved_ref, f32[256,4096]{1,0:T(8,128)S(1)} %copy-done.1, f32[64,1024]{1,0:T(8,128)S(1)} %slice.27.refs_0_, f32[64,1024]{1,0:T(8,128)S(1)} %collective-permute-done.12.refs_1_, ...), custom_call_target="tpu_custom_call" | custom-call | tf_op jit(solution)/shard_map/update_rows/pallas_call | solution.py:94
  (41 shorter events, 2.1 us)
Async XLA Ops:
  0.0 1.6 %copy-start = (f32[4096,128]{1,0:T(8,128)S(1)}, f32[4096,128]{1,0:T(8,128)}, u32[]{:S(2)}) copy-start(f32[4096,128]{1,0:T(8,128)} %param.4) | copy-start | bytes 6291460
  1.6 18.7 %copy-start.4 = (s32[128]{0:T(128)S(1)}, s32[128]{0:T(128)}, u32[]{:S(2)}) copy-start(s32[128]{0:T(128)} %moved_ref.1) | copy-start | bytes 1540
  5.6 14.8 %collective-permute-start.2 = (f32[256,128]{1,0:T(8,128)S(1)}, f32[256,128]{1,0:T(8,128)S(1)}, u32[]{:S(2)}, u32[]{:S(2)}) collective-permute-start(f32[256,128]{1,0:T(8,128)S(1)} %fusion.23), channel_id=1, source_target_pairs={{0,3},{1,0},{2,1},{3,2},{4,7},{5,4},{6,5},{7,6},{8,11},{9,8},{10,9... | collective-permute-start | bytes 393224 | tf_op jit(solution)/shard_map/ppermute | solution.py:153
  8.4 12.0 %collective-permute-start.1 = (f32[256,128]{1,0:T(8,128)S(1)}, f32[256,128]{1,0:T(8,128)S(1)}, u32[]{:S(2)}, u32[]{:S(2)}) collective-permute-start(f32[256,128]{1,0:T(8,128)S(1)} %fusion.23), channel_id=1, source_target_pairs={{0,2},{1,3},{2,0},{3,1},{4,6},{5,7},{6,4},{7,5},{8,10},{9,11},{10,... | collective-permute-start | bytes 393224 | tf_op jit(solution)/shard_map/ppermute | solution.py:153
  8.8 12.3 %collective-permute-start = (f32[256,128]{1,0:T(8,128)S(1)}, f32[256,128]{1,0:T(8,128)}, u32[]{:S(2)}, u32[]{:S(2)}) collective-permute-start(f32[256,128]{1,0:T(8,128)S(1)} %fusion.23), channel_id=1, source_target_pairs={{0,1},{1,2},{2,3},{3,0},{4,5},{5,6},{6,7},{7,4},{8,9},{9,10},{10,1... | collective-permute-start | bytes 393224 | tf_op jit(solution)/shard_map/ppermute | solution.py:153
  18.7 9.5 %collective-permute-start.3 = (f32[4,64,1024]{2,1,0:T(8,128)}, f32[4,64,1024]{2,1,0:T(8,128)S(1)}, u32[]{:S(2)}, u32[]{:S(2)}) collective-permute-start(f32[4,64,1024]{2,1,0:T(8,128)} %get-tuple-element.8), channel_id=1, source_target_pairs={{0,4},{4,0},{8,12},{12,8},{16,20},{20,16},{24,28},{28,24},{32,36},... | collective-permute-start | bytes 3145736 | tf_op jit(solution)/shard_map/ppermute | solution.py:148
  20.3 13.1 %copy-start.5 = (s32[128]{0:T(128)}, s32[128]{0:T(128)S(1)}, u32[]{:S(2)}) copy-start(s32[128]{0:T(128)S(1)} %and_select_fusion.5) | copy-start | bytes 1540
  20.4 0.6 copy-start.3
  22.4 1.3 collective-permute-start.7
  24.3 7.8 %collective-permute-start.10 = (f32[64,128]{1,0:T(8,128)}, f32[64,128]{1,0:T(8,128)}, u32[]{:S(2)}, u32[]{:S(2)}) collective-permute-start(f32[64,128]{1,0:T(8,128)} %dynamic-slice_add_fusion), channel_id=1, source_target_pairs={{0,24},{4,28},{8,0},{12,4},{16,8},{20,12},{24,16},{28,20},{32,56},... | collective-permute-start | bytes 98312 | tf_op jit(solution)/shard_map/ppermute | solution.py:162
  24.5 9.6 %collective-permute-start.9 = (f32[64,128]{1,0:T(8,128)}, f32[64,128]{1,0:T(8,128)}, u32[]{:S(2)}, u32[]{:S(2)}) collective-permute-start(f32[64,128]{1,0:T(8,128)} %dynamic-slice_add_fusion), channel_id=1, source_target_pairs={{0,16},{4,20},{8,24},{12,28},{16,0},{20,4},{24,8},{28,12},{32,48},... | collective-permute-start | bytes 98312 | tf_op jit(solution)/shard_map/ppermute | solution.py:162
  26.7 7.5 %collective-permute-start.8 = (f32[64,128]{1,0:T(8,128)}, f32[64,128]{1,0:T(8,128)}, u32[]{:S(2)}, u32[]{:S(2)}) collective-permute-start(f32[64,128]{1,0:T(8,128)} %dynamic-slice_add_fusion), channel_id=1, source_target_pairs={{0,8},{4,12},{8,16},{12,20},{16,24},{20,28},{24,0},{28,4},{32,40},... | collective-permute-start | bytes 98312 | tf_op jit(solution)/shard_map/ppermute | solution.py:162
  30.3 7.1 %collective-permute-start.6 = (f32[64,1024]{1,0:T(8,128)}, f32[64,1024]{1,0:T(8,128)S(1)}, u32[]{:S(2)}, u32[]{:S(2)}) collective-permute-start(f32[64,1024]{1,0:T(8,128)} %get-tuple-element.11), channel_id=1, source_target_pairs={{0,8},{4,12},{8,16},{12,20},{16,24},{20,28},{24,0},{28,4},{32,40},... | collective-permute-start | bytes 786440 | tf_op jit(solution)/shard_map/ppermute | solution.py:174
  30.3 8.7 %collective-permute-start.5 = (f32[64,1024]{1,0:T(8,128)}, f32[64,1024]{1,0:T(8,128)}, u32[]{:S(2)}, u32[]{:S(2)}) collective-permute-start(f32[64,1024]{1,0:T(8,128)} %get-tuple-element.12), channel_id=1, source_target_pairs={{0,16},{4,20},{8,24},{12,28},{16,0},{20,4},{24,8},{28,12},{32,48},... | collective-permute-start | bytes 786440 | tf_op jit(solution)/shard_map/ppermute | solution.py:174
  32.0 13.9 %collective-permute-start.4 = (f32[64,1024]{1,0:T(8,128)}, f32[64,1024]{1,0:T(8,128)}, u32[]{:S(2)}, u32[]{:S(2)}) collective-permute-start(f32[64,1024]{1,0:T(8,128)} %get-tuple-element.13), channel_id=1, source_target_pairs={{0,24},{4,28},{8,0},{12,4},{16,8},{20,12},{24,16},{28,20},{32,56},... | collective-permute-start | bytes 786440 | tf_op jit(solution)/shard_map/ppermute | solution.py:174
  37.4 8.6 %copy-start.2 = (f32[64,1024]{1,0:T(8,128)}, f32[64,1024]{1,0:T(8,128)S(1)}, u32[]{:S(2)}) copy-start(f32[64,1024]{1,0:T(8,128)S(1)} %collective-permute-done.6) | copy-start | bytes 786436
  48.0 19.8 %all-to-all-start = ((f32[8,8,1152]{2,1,0:T(8,128)}), f32[8,8,1152]{2,1,0:T(8,128)S(1)}, u32[]{:S(2)}, u32[]{:S(2)}) async-start(f32[8,8,1152]{2,1,0:T(8,128)} %maximum_bitcast_fusion), calls=%async_computation | async-start | bytes 589824 | tf_op jit(solution)/shard_map/all_to_all | solution.py:177
  68.6 13.3 %all-to-all-start.1 = ((f32[8,8,1152]{2,1,0:T(8,128)}), f32[8,8,1152]{2,1,0:T(8,128)S(1)}, u32[]{:S(2)}, u32[]{:S(2)}) async-start(f32[8,8,1152]{2,1,0:T(8,128)} %broadcast_in_dim.62), calls=%async_computation.1 | async-start | bytes 589824 | tf_op jit(solution)/shard_map/all_to_all | solution.py:181
  82.6 7.8 %collective-permute-start.11 = (f32[64,128]{1,0:T(8,128)}, f32[64,128]{1,0:T(8,128)}, u32[]{:S(2)}, u32[]{:S(2)}) collective-permute-start(f32[64,128]{1,0:T(8,128)} %slice.26), channel_id=1, source_target_pairs={{0,4},{4,0},{8,12},{12,8},{16,20},{20,16},{24,28},{28,24},{32,36},... | collective-permute-start | bytes 98312 | tf_op jit(solution)/shard_map/ppermute | solution.py:185
  86.2 41.3 %collective-permute-start.15 = (f32[64,1024]{1,0:T(8,128)S(1)}, f32[64,1024]{1,0:T(8,128)S(1)}, u32[]{:S(2)}, u32[]{:S(2)}) collective-permute-start(f32[64,1024]{1,0:T(8,128)S(1)} %slice.27.refs_0_), channel_id=1, source_target_pairs={{0,4},{4,0},{8,12},{12,8},{16,20},{20,16},{24,28},{28,24},{32,36},... | collective-permute-start | bytes 786440 | tf_op jit(solution)/shard_map/ppermute | solution.py:190
  86.3 38.2 %collective-permute-start.14 = (f32[64,1024]{1,0:T(8,128)S(1)}, f32[64,1024]{1,0:T(8,128)S(1)}, u32[]{:S(2)}, u32[]{:S(2)}) collective-permute-start(f32[64,1024]{1,0:T(8,128)S(1)} %slice.27.refs_0_), channel_id=1, source_target_pairs={{0,24},{4,28},{8,0},{12,4},{16,8},{20,12},{24,16},{28,20},{32,56},... | collective-permute-start | bytes 786440 | tf_op jit(solution)/shard_map/ppermute | solution.py:189
  86.6 39.1 %collective-permute-start.13 = (f32[64,1024]{1,0:T(8,128)S(1)}, f32[64,1024]{1,0:T(8,128)S(1)}, u32[]{:S(2)}, u32[]{:S(2)}) collective-permute-start(f32[64,1024]{1,0:T(8,128)S(1)} %slice.27.refs_0_), channel_id=1, source_target_pairs={{0,16},{4,20},{8,24},{12,28},{16,0},{20,4},{24,8},{28,12},{32,48},... | collective-permute-start | bytes 786440 | tf_op jit(solution)/shard_map/ppermute | solution.py:189
  88.4 37.4 %collective-permute-start.12 = (f32[64,1024]{1,0:T(8,128)S(1)}, f32[64,1024]{1,0:T(8,128)S(1)}, u32[]{:S(2)}, u32[]{:S(2)}) collective-permute-start(f32[64,1024]{1,0:T(8,128)S(1)} %slice.27.refs_0_), channel_id=1, source_target_pairs={{0,8},{4,12},{8,16},{12,20},{16,24},{20,28},{24,0},{28,4},{32,40},... | collective-permute-start | bytes 786440 | tf_op jit(solution)/shard_map/ppermute | solution.py:189
  124.5 3.0 %collective-permute-start.18 = (f32[64,1024]{1,0:T(8,128)S(1)}, f32[64,1024]{1,0:T(8,128)S(1)}, u32[]{:S(2)}, u32[]{:S(2)}) collective-permute-start(f32[64,1024]{1,0:T(8,128)S(1)} %collective-permute-done.14.refs_3_), channel_id=1, source_target_pairs={{0,4},{4,0},{8,12},{12,8},{16,20},{20,16},{24,28},{28,24},{32,36},... | collective-permute-start | bytes 786440 | tf_op jit(solution)/shard_map/ppermute | solution.py:190
  125.7 1.9 %collective-permute-start.17 = (f32[64,1024]{1,0:T(8,128)S(1)}, f32[64,1024]{1,0:T(8,128)S(1)}, u32[]{:S(2)}, u32[]{:S(2)}) collective-permute-start(f32[64,1024]{1,0:T(8,128)S(1)} %collective-permute-done.13.refs_2_), channel_id=1, source_target_pairs={{0,4},{4,0},{8,12},{12,8},{16,20},{20,16},{24,28},{28,24},{32,36},... | collective-permute-start | bytes 786440 | tf_op jit(solution)/shard_map/ppermute | solution.py:190
  125.8 1.8 %collective-permute-start.16 = (f32[64,1024]{1,0:T(8,128)S(1)}, f32[64,1024]{1,0:T(8,128)S(1)}, u32[]{:S(2)}, u32[]{:S(2)}) collective-permute-start(f32[64,1024]{1,0:T(8,128)S(1)} %collective-permute-done.12.refs_1_), channel_id=1, source_target_pairs={{0,4},{4,0},{8,12},{12,8},{16,20},{20,16},{24,28},{28,24},{32,36},... | collective-permute-start | bytes 786440 | tf_op jit(solution)/shard_map/ppermute | solution.py:190
  127.6 2.2 %copy-start.1 = (f32[256,4096]{1,0:T(8,128)S(1)}, f32[256,4096]{1,0:T(8,128)}, u32[]{:S(2)}) copy-start(f32[256,4096]{1,0:T(8,128)} %g_ref.3) | copy-start | bytes 12582916

commit v2 on v0

v2 whole, which is shorter than its diff:
```python
import functools

import jax
import jax.numpy as jnp
from jax import lax
from jax.experimental import pallas as pl
from jax.experimental.pallas import tpu as pltpu
from jax.sharding import PartitionSpec as P

HIGHEST = lax.Precision.HIGHEST
CORES = 2
XS = 4


def pick_kernel(moved_ref, g_ref, keep_ref, send_ref, sem):
    rows_local = g_ref.shape[0]
    quarters, half, width = keep_ref.shape
    me = lax.axis_index("wide")
    first = me * rows_local
    core = me % CORES

    def copy(local, target, row, q):
        return pltpu.make_async_copy(
            g_ref.at[pl.ds(local, 1), pl.ds(q * width, width)], target.at[q, pl.ds(row, 1), :], sem
        )

    total = 0
    for side in range(CORES):
        def start(row, found, side=side):
            local = moved_ref[side * half + row] - first
            owned = jnp.logical_and(local >= 0, local < rows_local)

            @pl.when(owned)
            def _():
                @pl.when(core == side)
                def _():
                    for q in range(quarters):
                        copy(local, keep_ref, row, q).start()

                @pl.when(core != side)
                def _():
                    for q in range(quarters):
                        copy(local, send_ref, row, q).start()

            return found + jnp.where(owned, 1, 0)

        total = lax.fori_loop(0, half, start, total, unroll=8)

    def wait(i, carry):
        for q in range(quarters):
            copy(0, keep_ref, 0, q).wait()
        return carry

    lax.fori_loop(0, total, wait, 0)


def pick(gebhart, moved_nodes, half, width):
    shape = jax.ShapeDtypeStruct((XS, half, width), jnp.float32)
    return pl.pallas_call(
        pick_kernel,
        out_shape=(shape, shape),
        in_specs=[pl.BlockSpec(memory_space=pltpu.SMEM), pl.BlockSpec(memory_space=pl.ANY)],
        out_specs=(pl.BlockSpec(memory_space=pl.ANY), pl.BlockSpec(memory_space=pl.ANY)),
        scratch_shapes=[pltpu.SemaphoreType.DMA],
        compiler_params=pltpu.CompilerParams(vmem_limit_bytes=60 * 1024 * 1024),
        name="pick_rows",
    )(moved_nodes, gebhart)


def split(value):
    high = value.astype(jnp.bfloat16)
    low = (value - high.astype(jnp.float32)).astype(jnp.bfloat16)
    return high, low


def pair_inverse(p, q, s):
    scale = 1.0 / (p * s - q * q)
    return s * scale, -q * scale, p * scale


def quad_inverse(e):
    a, b, c = pair_inverse(e[0][0], e[0][1], e[1][1])
    t = [[a * e[0][2] + b * e[1][2], a * e[0][3] + b * e[1][3]], [b * e[0][2] + c * e[1][2], b * e[0][3] + c * e[1][3]]]
    s22 = e[2][2] - (e[0][2] * t[0][0] + e[1][2] * t[1][0])
    s23 = e[2][3] - (e[0][2] * t[0][1] + e[1][2] * t[1][1])
    s33 = e[3][3] - (e[0][3] * t[0][1] + e[1][3] * t[1][1])
    f, g, h = pair_inverse(s22, s23, s33)
    w = [[t[0][0] * f + t[0][1] * g, t[0][0] * g + t[0][1] * h], [t[1][0] * f + t[1][1] * g, t[1][0] * g + t[1][1] * h]]
    i00 = a + w[0][0] * t[0][0] + w[0][1] * t[0][1]
    i01 = b + w[0][0] * t[1][0] + w[0][1] * t[1][1]
    i11 = c + w[1][0] * t[1][0] + w[1][1] * t[1][1]
    return [
        [i00, i01, -w[0][0], -w[0][1]],
        [i01, i11, -w[1][0], -w[1][1]],
        [-w[0][0], -w[1][0], f, g],
        [-w[0][1], -w[1][1], g, h],
    ]


def spd_inverse(normal, block=16):
    pivots = 4
    count = normal.shape[0]
    lane = lax.broadcasted_iota(jnp.int32, (1, count), 1)
    sub = lax.broadcasted_iota(jnp.int32, (block, 1), 0)
    for first in range(0, count, block):
        panel = normal[first:first + block, :]
        for i in range(0, block, pivots):
            k = first + i
            cols = [jnp.broadcast_to(panel[:, k + m:k + m + 1], (block, count)) for m in range(pivots)]
            entry = [[jnp.broadcast_to(cols[n][i + m:i + m + 1, :], (8, count)) for n in range(pivots)] for m in range(pivots)]
            q = quad_inverse(entry)
            inside = jnp.logical_and(lane >= k, lane < k + pivots)
            rows = [
                jnp.where(inside, jnp.where(lane == k + m, 1.0, 0.0), jnp.broadcast_to(panel[i + m:i + m + 1, :], (8, count)))
                for m in range(pivots)
            ]
            new = [q[m][0] * rows[0] + (q[m][1] * rows[1] + (q[m][2] * rows[2] + q[m][3] * rows[3])) for m in range(pivots)]
            new = [jnp.concatenate([row] * (block // 8), axis=0) for row in new]
            panel = jnp.where(inside, 0.0, panel)
            for m in range(pivots):
                panel = panel - cols[m] * new[m]
            for m in range(pivots):
                panel = jnp.where(sub == i + m, new[m], panel)
        within = jnp.logical_and(lane >= first, lane < first + block)
        outer = jnp.dot(normal[:, first:first + block], panel, precision=HIGHEST, preferred_element_type=jnp.float32)
        rest = jnp.where(within, 0.0, normal) - outer
        above = [rest[:first]] if first > 0 else []
        below = [rest[first + block:]] if first + block < count else []
        normal = jnp.concatenate(above + [panel] + below, axis=0)
    return normal


def invert_kernel(mine_ref, theirs_ref, out_ref):
    core = lax.axis_index("wide") % CORES
    mine, theirs = mine_ref[...], theirs_ref[...]
    low = jnp.where(core == 0, mine, theirs)
    high = jnp.where(core == 0, theirs, mine)
    touched = jnp.concatenate([low, high], axis=0)
    count = touched.shape[0]
    row = lax.broadcasted_iota(jnp.int32, (count, count), 0)
    column = lax.broadcasted_iota(jnp.int32, (count, count), 1)
    capacitance = jnp.where(row == column, 1.0, 0.0) - touched
    normal = lax.dot_general(
        capacitance, capacitance, (((1,), (1,)), ((), ())), precision=HIGHEST, preferred_element_type=jnp.float32
    )
    out_ref[...] = jnp.dot(spd_inverse(normal), capacitance, precision=HIGHEST, preferred_element_type=jnp.float32)


def invert(mine, theirs):
    count = mine.shape[1]
    return pl.pallas_call(
        invert_kernel,
        out_shape=jax.ShapeDtypeStruct((count, count), jnp.float32),
        cost_estimate=pl.CostEstimate(flops=30_000_000, bytes_accessed=200_000, transcendentals=0),
        name="invert_capacitance",
    )(mine, theirs)


def update_kernel(column_ref, inverse_ref, *refs):
    narrow = len(refs) - 2 * XS - 3
    parts, refs = refs[:narrow], refs[narrow:]
    g_ref, mine, theirs, out_ref, left_ref = refs[0], refs[1:1 + XS], refs[1 + XS:1 + 2 * XS], refs[1 + 2 * XS], refs[2 + 2 * XS]
    half = mine[0].shape[0]
    step = pl.program_id(0)
    core = lax.axis_index("wide") % CORES

    @pl.when(step == 0)
    def _():
        response = parts[0][...]
        for part in parts[1:]:
            response = response + part[...]
        solved = lax.dot_general(
            response, inverse_ref[...], (((1,), (1,)), ((), ())), precision=HIGHEST, preferred_element_type=jnp.float32
        )
        low, high = solved[:, :half], solved[:, half:]
        s_mine = jnp.where(core == 0, low, high)
        s_theirs = jnp.where(core == 0, high, low)
        s_high, s_low = split(jnp.concatenate([s_mine, s_theirs], axis=1))
        left_ref[...] = jnp.concatenate([s_high, s_low, s_high], axis=1)

    for j in range(XS):
        @pl.when(step == j)
        def _():
            r_high, r_low = split(jnp.concatenate([mine[j][...], theirs[j][...]], axis=0))
            right = jnp.concatenate([r_high, r_high, r_low], axis=0)
            out_ref[...] = g_ref[...] + jnp.dot(left_ref[...], right, preferred_element_type=jnp.float32)


def update(gebhart, inverse, parts, mine, theirs, columns):
    rows, nodes = gebhart.shape
    half, width = mine[0].shape
    count = inverse.shape[0]
    piece = pl.BlockSpec((half, width), lambda i, col: (0, 0))
    block = pl.BlockSpec((rows, width), lambda i, col: (0, col[i]))
    part = pl.BlockSpec((rows, count), lambda i, col: (0, 0))
    return pl.pallas_call(
        update_kernel,
        out_shape=jax.ShapeDtypeStruct((rows, nodes), jnp.float32),
        grid_spec=pltpu.PrefetchScalarGridSpec(
            num_scalar_prefetch=1,
            grid=(XS,),
            in_specs=[pl.BlockSpec((count, count), lambda i, col: (0, 0))] + [part] * len(parts) + [block] + [piece] * (2 * XS),
            out_specs=block,
            scratch_shapes=[pltpu.VMEM((rows, 3 * count), jnp.bfloat16)],
        ),
        compiler_params=pltpu.CompilerParams(vmem_limit_bytes=60 * 1024 * 1024),
        name="update_rows",
    )(columns, inverse, *parts, gebhart, *mine, *theirs)


def body(wide, narrow, gebhart, change, moved_nodes):
    rows_local, width_local = gebhart.shape
    count = moved_nodes.shape[0]
    half = count // CORES
    zs = wide // (CORES * XS)
    width = width_local // XS
    group = half // zs
    me = lax.axis_index("wide")
    core = me % CORES
    x = (me // CORES) % XS
    z = me // (CORES * XS)

    def index(z, x, c):
        return (z * XS + x) * CORES + c

    places = [(z, x, c) for z in range(zs) for x in range(XS) for c in range(CORES)]
    swap = [(index(z, x, c), index(z, x, (c + 1) % CORES)) for z, x, c in places]
    shift_x = [[(index(z, x, c), index(z, (x + d) % XS, c)) for z, x, c in places] for d in range(XS)]
    shift_y = [[(i, (i + d) % narrow) for i in range(narrow)] for d in range(narrow)]
    x_groups = [[index(z, x, c) for x in range(XS)] for z in range(zs) for c in range(CORES)]
    z_groups = [[index(z, x, c) for z in range(zs)] for x in range(XS) for c in range(CORES)]

    owner = moved_nodes // rows_local
    owner_half = lax.dynamic_slice(owner, (core * half,), (half,))
    owner_core = owner_half % CORES
    owner_x = (owner_half // CORES) % XS
    owner_z = lax.dynamic_slice(owner_half // (CORES * XS), (z * group,), (group,))

    keep, send = pick(gebhart, moved_nodes, half, width)
    got = lax.ppermute(send, "wide", swap)

    partial_value = jnp.dot(gebhart, change, preferred_element_type=jnp.float32, precision=lax.Precision.HIGH)
    positions = me * rows_local + lax.broadcasted_iota(jnp.int32, (count, rows_local), 1)
    select = (moved_nodes[:, None] == positions).astype(jnp.float32)
    terms = jnp.dot(select, partial_value, preferred_element_type=jnp.float32, precision=HIGHEST)
    terms_mine = lax.dynamic_slice(terms, (core * half, 0), (half, count))
    terms_theirs = lax.dynamic_slice(terms, ((1 - core) * half, 0), (half, count))
    terms_chip = terms_mine + lax.ppermute(terms_theirs, "wide", swap)
    parts = [partial_value] + [lax.ppermute(partial_value, "narrow", shift_y[d]) for d in range(1, narrow)]

    rows_chip = jnp.where((owner_core == core)[None, :, None], keep, got)
    both = jnp.concatenate([rows_chip, jnp.broadcast_to(terms_chip[None], (XS, half, count))], axis=2)
    both = lax.all_to_all(both, "wide", 0, 0, axis_index_groups=x_groups)
    chosen = owner_x[None, :, None] == lax.broadcasted_iota(jnp.int32, (XS, 1, 1), 0)
    both = jnp.sum(jnp.where(chosen, both, 0.0), axis=0)

    both = lax.all_to_all(both.reshape(zs, group, width + count), "wide", 0, 0, axis_index_groups=z_groups)
    chosen = owner_z[None, :, None] == lax.broadcasted_iota(jnp.int32, (zs, 1, 1), 0)
    both = jnp.sum(jnp.where(chosen, both, 0.0), axis=0)
    both = lax.all_to_all(jnp.broadcast_to(both[None], (zs,) + both.shape), "wide", 0, 0, axis_index_groups=z_groups)
    both = both.reshape(half, width + count)

    touched_part = both[:, width:]
    touched = touched_part
    for d in range(1, narrow):
        touched = touched + lax.ppermute(touched_part, "narrow", shift_y[d])
    inverse = invert(touched, lax.ppermute(touched, "wide", swap))

    piece = both[:, :width]
    pieces = [piece] + [lax.ppermute(piece, "wide", shift_x[d]) for d in range(1, XS)]
    theirs = [lax.ppermute(p, "wide", swap) for p in pieces]
    columns = jnp.stack([(x - d) % XS for d in range(XS)]).astype(jnp.int32)
    return update(gebhart, inverse, parts, pieces, theirs, columns)


def solution(mesh):
    return jax.shard_map(
        functools.partial(body, mesh.shape["wide"], mesh.shape["narrow"]),
        mesh=mesh,
        in_specs=(P("wide", "narrow"), P("narrow", None), P()),
        out_specs=P("wide", "narrow"),
        check_vma=False,
    )
```

time: 298 us -> 112 us (0.38)
  waiting for transfers between devices: 235 us -> 32.2 us
  starting transfers between devices: 0.04 us -> 36.8 us
  Pallas kernels: 0 us -> 19 us
  matrix products: 23.2 us -> 4.36 us
  other arithmetic: 22.9 us -> 4.29 us
  between operations: 13.5 us -> 0.24 us
  blocking collectives: 0 us -> 12.4 us
    psum x2 -> x0, waiting for transfers between devices: 235 us -> none  [the longest x1 193 us: body(): touched = lax.psum(terms, 'wide')]
    all_to_all x0 -> x2, waiting for transfers between devices: none -> 25.8 us  [the longest x1 15.3 us: body(): both = lax.all_to_all(both, 'wide', 0, 0, axis_index_groups=x_groups)]
    ppermute x0 -> x16, starting transfers between devices: none -> 24.1 us  [the longest x4 7.78 us: body(): theirs = [lax.ppermute(p, 'wide', swap) for p in pieces]]
    another operation x5 -> x1, other arithmetic: 22.9 us -> 0.67 us  [body(): columns = jnp.stack([(x - d) % XS for d in range(XS)]).astype(jnp.int32)]
    pallas_call x0 -> x3, Pallas kernels: none -> 19 us  [the longest x1 8.56 us: invert(): pl.pallas_call(invert_kernel, out_shape=jax.ShapeDtypeStruct((count, coun...]
    dot_general x6 -> x2, matrix products: 22.7 us -> 4.36 us  [the longest x1 4.1 us: body(): jnp.dot(gebhart, change, preferred_element_type=jnp.float32, precision=la...]
    all_to_all x0 -> x2, starting transfers between devices: none -> 12.7 us  [the longest x1 8.26 us: body(): both = lax.all_to_all(both, 'wide', 0, 0, axis_index_groups=x_groups)]
    all_to_all x0 -> x1, blocking collectives: none -> 12.4 us  [body(): lax.all_to_all(jnp.broadcast_to(both[None], (zs,) + both.shape), 'wide',...]
  transfers between devices with their start and end apart: 2 -> 18, of which waited for: 2 -> 7; matrix products, arithmetic and copies ran while one was open for 2% -> 5% of each run, Pallas kernels for 0% -> 8%
where the time goes in v2:
time: 112 us; the launch traced here: 111 us
  starting transfers between devices  36.8 us (33%)
  waiting for transfers between devices  32.2 us (29%)
  Pallas kernels  19 us (17%)
  blocking collectives  12.4 us (11%)
  matrix products  4.36 us (4%)
  other arithmetic  4.29 us (4%)
  local copies, waits for them, and re-layouts  1.41 us (1%)
    all_to_all x1, waiting for transfers between devices, body(): both = lax.all_to_all(both, 'wide', 0, 0, axis_index_groups=x_groups)  15.3 us
    all_to_all x1, blocking collectives, body(): lax.all_to_all(jnp.broadcast_to(both[None], (zs,) + both.shape), 'wide',...  12.4 us
    all_to_all x1, waiting for transfers between devices, body(): lax.all_to_all(both.reshape(zs, group, width + count), 'wide', 0, 0, axis...  10.5 us
    pallas_call x1, Pallas kernels, invert(): pl.pallas_call(invert_kernel, out_shape=jax.ShapeDtypeStruct((count, coun...  8.56 us
    all_to_all x1, starting transfers between devices, body(): both = lax.all_to_all(both, 'wide', 0, 0, axis_index_groups=x_groups)  8.26 us
    ppermute x4, starting transfers between devices, body(): theirs = [lax.ppermute(p, 'wide', swap) for p in pieces]  7.78 us
    pallas_call x1, Pallas kernels, update(): pl.pallas_call(update_kernel, out_shape=jax.ShapeDtypeStruct((rows, nodes...  7.56 us
    ppermute x3, starting transfers between devices, body(): lax.ppermute(partial_value, 'narrow', shift_y[d])  5.23 us
  transfers between devices with their start and end apart: 18, of which 7 were waited for; matrix products, arithmetic and copies ran while one was open for 5% of the time, Pallas kernels for 8%

profile of v2, /device:TPU:3, one launch (start us, length us, event | category | flops | bytes accessed | tf_op | source)
XLA Modules:
  0.0 110.8 jit_solution(3784194891762097856)
XLA Ops:
  0.0 2.9 %pick_rows.1 = (f32[4,64,1024]{2,1,0:T(8,128)}, f32[4,64,1024]{2,1,0:T(8,128)}) custom-call(s32[128]{0:T(128)} %moved_ref.1, f32[256,4096]{1,0:T(8,128)} %refs_4_.1), custom_call_target="tpu_custom_call" | custom-call | tf_op jit(solution)/shard_map/pick_rows/pallas_call | solution.py:59
  2.9 0.6 collective-permute-start
  3.6 4.1 %fusion.6.refs_0_ = f32[256,128]{1,0:T(8,128)S(1)} fusion(f32[256,4096]{1,0:T(8,128)} %refs_4_.1, f32[4096,128]{1,0:T(8,128)S(1)} %copy-done), kind=kOutput, calls=%fused_computation.33 | convolution fusion | flops 805306368 | bytes 6422528 | tf_op jit(solution)/shard_map/dot_general | solution.py:242
  7.7 0.3 fusion
  8.0 0.1 collective-permute-start.1
  8.2 0.1 and_select_fusion.1
  8.3 1.0 collective-permute-done.1
  9.3 0.0 collective-permute-done
  9.3 1.4 %broadcast_select_fusion = f32[4,64,1024]{2,1,0:T(8,128)S(1)} fusion(f32[4,64,1024]{2,1,0:T(8,128)S(1)} %copy-done.3, f32[4,64,1024]{2,1,0:T(8,128)} %collective-permute-done, pred[64]{0:T(512)(128)(4,1)S(1)} %fusion.4), kind=kLoop, calls=%fused_computation.2 | loop fusion | flops 262144 | bytes 3145792 | tf_op jit(solution)/shard_map/jit(_where)/select_n | solution.py:251
  10.8 1.1 pad_maximum_fusion
  11.9 8.3 %all-to-all-start = ((f32[4,64,1152]{2,1,0:T(8,128)}), f32[4,64,1152]{2,1,0:T(8,128)S(1)}, u32[]{:S(2)}, u32[]{:S(2)}) async-start(f32[4,64,1152]{2,1,0:T(8,128)} %pad_maximum_fusion), calls=%async_computation | async-start | bytes 2359296 | tf_op jit(solution)/shard_map/all_to_all | solution.py:253
  20.1 15.3 %all-to-all-done = f32[4,64,1152]{2,1,0:T(8,128)S(1)} async-done(((f32[4,64,1152]{2,1,0:T(8,128)}), f32[4,64,1152]{2,1,0:T(8,128)S(1)}, u32[]{:S(2)}, u32[]{:S(2)}) %all-to-all-start) | async-done | bytes 1179680 | tf_op jit(solution)/shard_map/all_to_all | solution.py:253
  35.4 0.9 select_reduce_fusion
  36.3 4.4 %all-to-all-start.1 = ((f32[8,8,1152]{2,1,0:T(8,128)}), f32[8,8,1152]{2,1,0:T(8,128)S(1)}, u32[]{:S(2)}, u32[]{:S(2)}) async-start(f32[8,8,1152]{2,1,0:T(8,128)} %bitcast.12), calls=%async_computation.1 | async-start | bytes 589824 | tf_op jit(solution)/shard_map/all_to_all | solution.py:257
  40.7 0.1 dynamic_slice.13
  40.8 10.5 %all-to-all-done.1 = f32[8,8,1152]{2,1,0:T(8,128)S(1)} async-done(((f32[8,8,1152]{2,1,0:T(8,128)}), f32[8,8,1152]{2,1,0:T(8,128)S(1)}, u32[]{:S(2)}, u32[]{:S(2)}) %all-to-all-start.1) | async-done | bytes 294944 | tf_op jit(solution)/shard_map/all_to_all | solution.py:257
  51.3 0.1 select_reduce_fusion.1
  51.5 12.4 %all_to_all.15 = f32[8,8,1152]{2,1,0:T(8,128)S(1)} all-to-all(f32[8,8,1152]{2,1,0:T(8,128)S(1)} %broadcast_in_dim.54), channel_id=1, replica_groups={{0,32,64,96,128,160,192,224},{4,36,68,100,132,164,196,228},{8,40,72,104..., dimensions={0} | all-to-all | bytes 589824 | tf_op jit(solution)/shard_map/all_to_all | solution.py:260
  63.9 1.3 %collective-permute-start.11 = (f32[64,1024]{1,0:T(8,128)S(1)}, f32[64,1024]{1,0:T(8,128)S(1)}, u32[]{:S(2)}, u32[]{:S(2)}) collective-permute-start(f32[64,1024]{1,0:T(8,128)S(1)} %slice.9.refs_5_), channel_id=1, source_target_pairs={{0,24},{4,28},{8,0},{12,4},{16,8},{20,12},{24,16},{28,20},{32,56},... | collective-permute-start | bytes 786440 | tf_op jit(solution)/shard_map/ppermute | solution.py:270
  65.2 1.6 %collective-permute-start.10 = (f32[64,1024]{1,0:T(8,128)S(1)}, f32[64,1024]{1,0:T(8,128)S(1)}, u32[]{:S(2)}, u32[]{:S(2)}) collective-permute-start(f32[64,1024]{1,0:T(8,128)S(1)} %slice.9.refs_5_), channel_id=1, source_target_pairs={{0,16},{4,20},{8,24},{12,28},{16,0},{20,4},{24,8},{28,12},{32,48},... | collective-permute-start | bytes 786440 | tf_op jit(solution)/shard_map/ppermute | solution.py:270
  66.8 2.0 %collective-permute-start.9 = (f32[64,1024]{1,0:T(8,128)S(1)}, f32[64,1024]{1,0:T(8,128)S(1)}, u32[]{:S(2)}, u32[]{:S(2)}) collective-permute-start(f32[64,1024]{1,0:T(8,128)S(1)} %slice.9.refs_5_), channel_id=1, source_target_pairs={{0,8},{4,12},{8,16},{12,20},{16,24},{20,28},{24,0},{28,4},{32,40},... | collective-permute-start | bytes 786440 | tf_op jit(solution)/shard_map/ppermute | solution.py:270
  68.7 2.7 %collective-permute-start.8 = (f32[256,128]{1,0:T(8,128)S(1)}, f32[256,128]{1,0:T(8,128)S(1)}, u32[]{:S(2)}, u32[]{:S(2)}) collective-permute-start(f32[256,128]{1,0:T(8,128)S(1)} %fusion.6.refs_0_), channel_id=1, source_target_pairs={{0,3},{1,0},{2,1},{3,2},{4,7},{5,4},{6,5},{7,6},{8,11},{9,8},{10,9... | collective-permute-start | bytes 393224 | tf_op jit(solution)/shard_map/ppermute | solution.py:249
  71.5 0.4 collective-permute-start.3
  71.8 1.9 %collective-permute-done.8.refs_3_ = f32[256,128]{1,0:T(8,128)S(1)} collective-permute-done((f32[256,128]{1,0:T(8,128)S(1)}, f32[256,128]{1,0:T(8,128)S(1)}, u32[]{:S(2)}, u32[]{:S(2)}) %collective-permute-start.8) | collective-permute-done | bytes 131104 | tf_op jit(solution)/shard_map/ppermute | solution.py:249
  73.7 3.1 %collective-permute-start.4 = (f32[64,128]{1,0:T(8,128)S(1)}, f32[64,128]{1,0:T(8,128)S(1)}, u32[]{:S(2)}, u32[]{:S(2)}) collective-permute-start(f32[64,128]{1,0:T(8,128)S(1)} %slice.8), channel_id=1, source_target_pairs={{0,3},{1,0},{2,1},{3,2},{4,7},{5,4},{6,5},{7,6},{8,11},{9,8},{10,9... | collective-permute-start | bytes 98312 | tf_op jit(solution)/shard_map/ppermute | solution.py:266
  76.8 0.0 collective-permute-done.3
  76.8 0.0 collective-permute-start.2
  76.8 1.1 %collective-permute-done.4 = f32[64,128]{1,0:T(8,128)S(1)} collective-permute-done((f32[64,128]{1,0:T(8,128)S(1)}, f32[64,128]{1,0:T(8,128)S(1)}, u32[]{:S(2)}, u32[]{:S(2)}) %collective-permute-start.4) | collective-permute-done | bytes 32800 | tf_op jit(solution)/shard_map/ppermute | solution.py:266
  78.0 1.9 %collective-permute-start.7 = (f32[256,128]{1,0:T(8,128)S(1)}, f32[256,128]{1,0:T(8,128)S(1)}, u32[]{:S(2)}, u32[]{:S(2)}) collective-permute-start(f32[256,128]{1,0:T(8,128)S(1)} %fusion.6.refs_0_), channel_id=1, source_target_pairs={{0,2},{1,3},{2,0},{3,1},{4,6},{5,7},{6,4},{7,5},{8,10},{9,11},{10,... | collective-permute-start | bytes 393224 | tf_op jit(solution)/shard_map/ppermute | solution.py:249
  79.9 1.5 %collective-permute-done.2 = f32[64,128]{1,0:T(8,128)S(1)} collective-permute-done((f32[64,128]{1,0:T(8,128)S(1)}, f32[64,128]{1,0:T(8,128)S(1)}, u32[]{:S(2)}, u32[]{:S(2)}) %collective-permute-start.2) | collective-permute-done | bytes 32800 | tf_op jit(solution)/shard_map/ppermute | solution.py:266
  81.3 7.0 %collective-permute-start.12 = (f32[64,1024]{1,0:T(8,128)S(1)}, f32[64,1024]{1,0:T(8,128)S(1)}, u32[]{:S(2)}, u32[]{:S(2)}) collective-permute-start(f32[64,1024]{1,0:T(8,128)S(1)} %slice.9.refs_5_), channel_id=1, source_target_pairs={{0,4},{4,0},{8,12},{12,8},{16,20},{20,16},{24,28},{28,24},{32,36},... | collective-permute-start | bytes 786440 | tf_op jit(solution)/shard_map/ppermute | solution.py:271
  88.3 0.0 collective-permute-done.11.refs_8_
  88.3 0.1 collective-permute-start.15
  88.4 0.0 collective-permute-done.10.refs_7_
  88.4 0.4 collective-permute-start.14
  88.8 0.0 collective-permute-done.9.refs_6_
  88.8 0.3 collective-permute-start.13
  89.1 0.0 copy-start.10
  89.2 2.1 %collective-permute-start.5 = (f32[64,128]{1,0:T(8,128)S(1)}, f32[64,128]{1,0:T(8,128)S(1)}, u32[]{:S(2)}, u32[]{:S(2)}) collective-permute-start(f32[64,128]{1,0:T(8,128)S(1)} %add_add_fusion.mine_ref), channel_id=1, source_target_pairs={{0,4},{4,0},{8,12},{12,8},{16,20},{20,16},{24,28},{28,24},{32,36},... | collective-permute-start | bytes 98312 | tf_op jit(solution)/shard_map/ppermute | solution.py:267
  91.3 0.9 collective-permute-done.5.theirs_ref
  92.1 0.6 copy-done.11
  92.7 0.6 collective-permute-start.6
  93.3 0.7 pad_add_fusion.column_ref
  94.0 8.6 %invert_capacitance.1.inverse_ref = f32[128,128]{1,0:T(8,128)} custom-call(f32[64,128]{1,0:T(8,128)} %copy-done.10, f32[64,128]{1,0:T(8,128)} %copy-done.11), custom_call_target="tpu_custom_call" | custom-call | flops 30000000 | bytes 200000 | tf_op jit(solution)/shard_map/invert_capacitance/pallas_call | solution.py:151
  102.5 0.0 collective-permute-done.12.refs_9_
  102.6 0.0 collective-permute-done.13.refs_10_
  102.6 0.6 copy-done.7
  103.2 7.6 %update_rows.1 = f32[256,4096]{1,0:T(8,128)} custom-call(s32[4]{0:T(128)} %pad_add_fusion.column_ref, f32[128,128]{1,0:T(8,128)} %invert_capacitance.1.inverse_ref, f32[256,128]{1,0:T(8,128)} %copy-done.1, f32[256,128]{1,0:T(8,128)} %collective-permute-done.6.refs_1_, f32[256,128]{1,0:T(8,128)} %copy-done.9, f32[256,128]{1,0:T(8,128)} %copy-done.8, ...), custom_call_target="tpu_custom_call" | custom-call | tf_op jit(solution)/shard_map/update_rows/pallas_call | solution.py:196
  (39 shorter events, 0.2 us)
Async XLA Ops:
  0.0 3.6 %copy-start = (f32[4096,128]{1,0:T(8,128)S(1)}, f32[4096,128]{1,0:T(8,128)}, u32[]{:S(2)}) copy-start(f32[4096,128]{1,0:T(8,128)} %param.4) | copy-start | bytes 6291460
  2.9 6.4 %collective-permute-start = (f32[4,64,1024]{2,1,0:T(8,128)}, f32[4,64,1024]{2,1,0:T(8,128)}, u32[]{:S(2)}, u32[]{:S(2)}) collective-permute-start(f32[4,64,1024]{2,1,0:T(8,128)} %get-tuple-element.8), channel_id=1, source_target_pairs={{0,4},{4,0},{8,12},{12,8},{16,20},{20,16},{24,28},{28,24},{32,36},... | collective-permute-start | bytes 3145736 | tf_op jit(solution)/shard_map/ppermute | solution.py:240
  3.6 4.1 %copy-start.12 = (s32[128]{0:T(128)S(1)}, s32[128]{0:T(128)}, u32[]{:S(2)}) copy-start(s32[128]{0:T(128)} %moved_ref.1) | copy-start | bytes 1540
  3.6 5.7 %copy-start.3 = (f32[4,64,1024]{2,1,0:T(8,128)S(1)}, f32[4,64,1024]{2,1,0:T(8,128)}, u32[]{:S(2)}) copy-start(f32[4,64,1024]{2,1,0:T(8,128)} %get-tuple-element.7) | copy-start | bytes 3145732
  7.7 84.4 %copy-start.1 = (f32[256,128]{1,0:T(8,128)}, f32[256,128]{1,0:T(8,128)S(1)}, u32[]{:S(2)}) copy-start(f32[256,128]{1,0:T(8,128)S(1)} %fusion.6.refs_0_) | copy-start | bytes 393220
  8.0 1.3 %collective-permute-start.1 = (f32[64,128]{1,0:T(8,128)S(1)}, f32[64,128]{1,0:T(8,128)S(1)}, u32[]{:S(2)}, u32[]{:S(2)}) collective-permute-start(f32[64,128]{1,0:T(8,128)S(1)} %constant_dynamic-slice_fusion), channel_id=1, source_target_pairs={{0,4},{4,0},{8,12},{12,8},{16,20},{20,16},{24,28},{28,24},{32,36},... | collective-permute-start | bytes 98312 | tf_op jit(solution)/shard_map/ppermute | solution.py:248
  11.9 23.6 %all-to-all-start = ((f32[4,64,1152]{2,1,0:T(8,128)}), f32[4,64,1152]{2,1,0:T(8,128)S(1)}, u32[]{:S(2)}, u32[]{:S(2)}) async-start(f32[4,64,1152]{2,1,0:T(8,128)} %pad_maximum_fusion), calls=%async_computation | async-start | bytes 2359296 | tf_op jit(solution)/shard_map/all_to_all | solution.py:253
  36.3 15.0 %all-to-all-start.1 = ((f32[8,8,1152]{2,1,0:T(8,128)}), f32[8,8,1152]{2,1,0:T(8,128)S(1)}, u32[]{:S(2)}, u32[]{:S(2)}) async-start(f32[8,8,1152]{2,1,0:T(8,128)} %bitcast.12), calls=%async_computation.1 | async-start | bytes 589824 | tf_op jit(solution)/shard_map/all_to_all | solution.py:257
  63.9 38.7 %copy-start.2 = (f32[64,1024]{1,0:T(8,128)}, f32[64,1024]{1,0:T(8,128)S(1)}, u32[]{:S(2)}) copy-start(f32[64,1024]{1,0:T(8,128)S(1)} %slice.9.refs_5_) | copy-start | bytes 786436
  63.9 24.4 %collective-permute-start.11 = (f32[64,1024]{1,0:T(8,128)S(1)}, f32[64,1024]{1,0:T(8,128)S(1)}, u32[]{:S(2)}, u32[]{:S(2)}) collective-permute-start(f32[64,1024]{1,0:T(8,128)S(1)} %slice.9.refs_5_), channel_id=1, source_target_pairs={{0,24},{4,28},{8,0},{12,4},{16,8},{20,12},{24,16},{28,20},{32,56},... | collective-permute-start | bytes 786440 | tf_op jit(solution)/shard_map/ppermute | solution.py:270
  65.2 23.2 %collective-permute-start.10 = (f32[64,1024]{1,0:T(8,128)S(1)}, f32[64,1024]{1,0:T(8,128)S(1)}, u32[]{:S(2)}, u32[]{:S(2)}) collective-permute-start(f32[64,1024]{1,0:T(8,128)S(1)} %slice.9.refs_5_), channel_id=1, source_target_pairs={{0,16},{4,20},{8,24},{12,28},{16,0},{20,4},{24,8},{28,12},{32,48},... | collective-permute-start | bytes 786440 | tf_op jit(solution)/shard_map/ppermute | solution.py:270
  66.8 22.1 %collective-permute-start.9 = (f32[64,1024]{1,0:T(8,128)S(1)}, f32[64,1024]{1,0:T(8,128)S(1)}, u32[]{:S(2)}, u32[]{:S(2)}) collective-permute-start(f32[64,1024]{1,0:T(8,128)S(1)} %slice.9.refs_5_), channel_id=1, source_target_pairs={{0,8},{4,12},{8,16},{12,20},{16,24},{20,28},{24,0},{28,4},{32,40},... | collective-permute-start | bytes 786440 | tf_op jit(solution)/shard_map/ppermute | solution.py:270
  68.7 5.0 %collective-permute-start.8 = (f32[256,128]{1,0:T(8,128)S(1)}, f32[256,128]{1,0:T(8,128)S(1)}, u32[]{:S(2)}, u32[]{:S(2)}) collective-permute-start(f32[256,128]{1,0:T(8,128)S(1)} %fusion.6.refs_0_), channel_id=1, source_target_pairs={{0,3},{1,0},{2,1},{3,2},{4,7},{5,4},{6,5},{7,6},{8,11},{9,8},{10,9... | collective-permute-start | bytes 393224 | tf_op jit(solution)/shard_map/ppermute | solution.py:249
  71.5 5.4 %collective-permute-start.3 = (f32[64,128]{1,0:T(8,128)S(1)}, f32[64,128]{1,0:T(8,128)S(1)}, u32[]{:S(2)}, u32[]{:S(2)}) collective-permute-start(f32[64,128]{1,0:T(8,128)S(1)} %slice.8), channel_id=1, source_target_pairs={{0,2},{1,3},{2,0},{3,1},{4,6},{5,7},{6,4},{7,5},{8,10},{9,11},{10,... | collective-permute-start | bytes 98312 | tf_op jit(solution)/shard_map/ppermute | solution.py:266
  73.7 17.5 %copy-start.8 = (f32[256,128]{1,0:T(8,128)}, f32[256,128]{1,0:T(8,128)S(1)}, u32[]{:S(2)}) copy-start(f32[256,128]{1,0:T(8,128)S(1)} %collective-permute-done.8.refs_3_) | copy-start | bytes 393220
  73.7 4.2 %collective-permute-start.4 = (f32[64,128]{1,0:T(8,128)S(1)}, f32[64,128]{1,0:T(8,128)S(1)}, u32[]{:S(2)}, u32[]{:S(2)}) collective-permute-start(f32[64,128]{1,0:T(8,128)S(1)} %slice.8), channel_id=1, source_target_pairs={{0,3},{1,0},{2,1},{3,2},{4,7},{5,4},{6,5},{7,6},{8,11},{9,8},{10,9... | collective-permute-start | bytes 98312 | tf_op jit(solution)/shard_map/ppermute | solution.py:266
  76.8 4.5 %collective-permute-start.2 = (f32[64,128]{1,0:T(8,128)S(1)}, f32[64,128]{1,0:T(8,128)S(1)}, u32[]{:S(2)}, u32[]{:S(2)}) collective-permute-start(f32[64,128]{1,0:T(8,128)S(1)} %slice.8), channel_id=1, source_target_pairs={{0,1},{1,2},{2,3},{3,0},{4,5},{5,6},{6,7},{7,4},{8,9},{9,10},{10,1... | collective-permute-start | bytes 98312 | tf_op jit(solution)/shard_map/ppermute | solution.py:266
  78.0 11.2 %collective-permute-start.7 = (f32[256,128]{1,0:T(8,128)S(1)}, f32[256,128]{1,0:T(8,128)S(1)}, u32[]{:S(2)}, u32[]{:S(2)}) collective-permute-start(f32[256,128]{1,0:T(8,128)S(1)} %fusion.6.refs_0_), channel_id=1, source_target_pairs={{0,2},{1,3},{2,0},{3,1},{4,6},{5,7},{6,4},{7,5},{8,10},{9,11},{10,... | collective-permute-start | bytes 393224 | tf_op jit(solution)/shard_map/ppermute | solution.py:249
  81.3 21.2 %collective-permute-start.12 = (f32[64,1024]{1,0:T(8,128)S(1)}, f32[64,1024]{1,0:T(8,128)S(1)}, u32[]{:S(2)}, u32[]{:S(2)}) collective-permute-start(f32[64,1024]{1,0:T(8,128)S(1)} %slice.9.refs_5_), channel_id=1, source_target_pairs={{0,4},{4,0},{8,12},{12,8},{16,20},{20,16},{24,28},{28,24},{32,36},... | collective-permute-start | bytes 786440 | tf_op jit(solution)/shard_map/ppermute | solution.py:271
  88.3 14.3 %copy-start.4 = (f32[64,1024]{1,0:T(8,128)}, f32[64,1024]{1,0:T(8,128)S(1)}, u32[]{:S(2)}) copy-start(f32[64,1024]{1,0:T(8,128)S(1)} %collective-permute-done.11.refs_8_) | copy-start | bytes 786436
  88.3 14.2 %collective-permute-start.15 = (f32[64,1024]{1,0:T(8,128)S(1)}, f32[64,1024]{1,0:T(8,128)}, u32[]{:S(2)}, u32[]{:S(2)}) collective-permute-start(f32[64,1024]{1,0:T(8,128)S(1)} %collective-permute-done.11.refs_8_), channel_id=1, source_target_pairs={{0,4},{4,0},{8,12},{12,8},{16,20},{20,16},{24,28},{28,24},{32,36},... | collective-permute-start | bytes 786440 | tf_op jit(solution)/shard_map/ppermute | solution.py:271
  88.4 14.2 %copy-start.5 = (f32[64,1024]{1,0:T(8,128)}, f32[64,1024]{1,0:T(8,128)S(1)}, u32[]{:S(2)}) copy-start(f32[64,1024]{1,0:T(8,128)S(1)} %collective-permute-done.10.refs_7_) | copy-start | bytes 786436
  88.4 14.1 %collective-permute-start.14 = (f32[64,1024]{1,0:T(8,128)S(1)}, f32[64,1024]{1,0:T(8,128)}, u32[]{:S(2)}, u32[]{:S(2)}) collective-permute-start(f32[64,1024]{1,0:T(8,128)S(1)} %collective-permute-done.10.refs_7_), channel_id=1, source_target_pairs={{0,4},{4,0},{8,12},{12,8},{16,20},{20,16},{24,28},{28,24},{32,36},... | collective-permute-start | bytes 786440 | tf_op jit(solution)/shard_map/ppermute | solution.py:271
  88.8 13.8 %copy-start.6 = (f32[64,1024]{1,0:T(8,128)}, f32[64,1024]{1,0:T(8,128)S(1)}, u32[]{:S(2)}) copy-start(f32[64,1024]{1,0:T(8,128)S(1)} %collective-permute-done.9.refs_6_) | copy-start | bytes 786436
  88.8 13.7 %collective-permute-start.13 = (f32[64,1024]{1,0:T(8,128)S(1)}, f32[64,1024]{1,0:T(8,128)}, u32[]{:S(2)}, u32[]{:S(2)}) collective-permute-start(f32[64,1024]{1,0:T(8,128)S(1)} %collective-permute-done.9.refs_6_), channel_id=1, source_target_pairs={{0,4},{4,0},{8,12},{12,8},{16,20},{20,16},{24,28},{28,24},{32,36},... | collective-permute-start | bytes 786440 | tf_op jit(solution)/shard_map/ppermute | solution.py:271
  89.1 3.0 %copy-start.10 = (f32[64,128]{1,0:T(8,128)}, f32[64,128]{1,0:T(8,128)S(1)}, u32[]{:S(2)}) copy-start(f32[64,128]{1,0:T(8,128)S(1)} %add_add_fusion.mine_ref) | copy-start | bytes 98308
  89.2 3.0 %copy-start.9 = (f32[256,128]{1,0:T(8,128)}, f32[256,128]{1,0:T(8,128)S(1)}, u32[]{:S(2)}) copy-start(f32[256,128]{1,0:T(8,128)S(1)} %collective-permute-done.7.refs_2_) | copy-start | bytes 393220
  89.2 2.9 %collective-permute-start.5 = (f32[64,128]{1,0:T(8,128)S(1)}, f32[64,128]{1,0:T(8,128)S(1)}, u32[]{:S(2)}, u32[]{:S(2)}) collective-permute-start(f32[64,128]{1,0:T(8,128)S(1)} %add_add_fusion.mine_ref), channel_id=1, source_target_pairs={{0,4},{4,0},{8,12},{12,8},{16,20},{20,16},{24,28},{28,24},{32,36},... | collective-permute-start | bytes 98312 | tf_op jit(solution)/shard_map/ppermute | solution.py:267
  92.1 0.6 copy-start.11
  92.7 9.8 %collective-permute-start.6 = (f32[256,128]{1,0:T(8,128)S(1)}, f32[256,128]{1,0:T(8,128)}, u32[]{:S(2)}, u32[]{:S(2)}) collective-permute-start(f32[256,128]{1,0:T(8,128)S(1)} %fusion.6.refs_0_), channel_id=1, source_target_pairs={{0,1},{1,2},{2,3},{3,0},{4,5},{5,6},{6,7},{7,4},{8,9},{9,10},{10,1... | collective-permute-start | bytes 393224 | tf_op jit(solution)/shard_map/ppermute | solution.py:249
  102.5 0.7 copy-start.7

commit v3 on v2

--- a/solution.py
+++ b/solution.py
@@ -10,6 +10,173 @@
 HIGHEST = lax.Precision.HIGHEST
 CORES = 2
 XS = 4
+SLOTS = 8
+PLANE = 32
+
+
+def respond_kernel(moved_ref, lanes_ref, g_ref, change_ref, out_ref, pick_ref, table_ref, kept_ref, lines_ref, g_sem, c_sem):
+    rows, count = out_ref.shape
+    width = pick_ref.shape[2] - count
+    chunks = g_sem.shape[0]
+    block = kept_ref.shape[1] // chunks
+    me = lax.axis_index("wide")
+    first = me * rows
+
+    copies = []
+    for i in range(chunks):
+        span = pl.ds(i * block, block)
+        copies.append((
+            pltpu.make_async_copy(g_ref.at[:, span], kept_ref.at[:, span], g_sem.at[i]),
+            pltpu.make_async_copy(change_ref.at[span, :], lines_ref.at[span, :], c_sem.at[i]),
+        ))
+        for copy in copies[-1]:
+            copy.start()
+
+    lane = lax.broadcasted_iota(jnp.int32, (1, count), 1)
+    node = lanes_ref[...]
+    owned = jnp.logical_and(node >= first, node < first + rows)
+    places = jnp.where(owned, lane, count).astype(jnp.float32)
+    last = -1.0
+    local = []
+    for slot in range(SLOTS):
+        last = jnp.min(jnp.where(places > last, places, float(count)))
+        found = last < float(count)
+        local.append(jnp.where(found, moved_ref[jnp.where(found, last, 0.0).astype(jnp.int32)] - first, 0))
+
+    shift = rows.bit_length() - 1
+    across = jnp.broadcast_to(lax.shift_right_logical(node, shift), (count, count)).astype(jnp.float32)
+    down = across.T
+    per_plane = float(CORES * XS)
+    plane_across = jnp.floor(across / per_plane)
+    plane_down = jnp.floor(down / per_plane)
+    i = lax.broadcasted_iota(jnp.int32, (count, count), 0)
+    j = lax.broadcasted_iota(jnp.int32, (count, count), 1)
+    one = jnp.where(across == down, 1.0, 0.0)
+    plane = jnp.where(plane_across == plane_down, 1.0, 0.0)
+    slot = jnp.sum(jnp.where(j < i, one, 0.0), axis=1, keepdims=True)
+    rank = jnp.sum(jnp.where(j < i, plane, 0.0), axis=1, keepdims=True)
+    rank_across = jnp.sum(jnp.where(i < j, plane, 0.0), axis=0, keepdims=True)
+    fits = jnp.where(jnp.logical_and(jnp.max(slot) < SLOTS, jnp.max(rank) < PLANE), 1, 0)
+    inside = down - plane_down * per_plane
+    x_down = jnp.floor(inside / float(CORES))
+    core_down = inside - x_down * float(CORES)
+    mine = jnp.where(core_down == (me % CORES).astype(jnp.float32), 0.0, float(XS * SLOTS))
+    here = plane_down == (me // (CORES * XS)).astype(jnp.float32)
+    match = jnp.logical_and(here, rank == j.astype(jnp.float32))
+    source = jnp.sum(jnp.where(match, x_down * float(SLOTS) + jnp.minimum(slot, SLOTS - 1.0) + mine, 0.0), axis=0, keepdims=True)
+    target = plane_across[:1] * float(PLANE) + jnp.minimum(rank_across, PLANE - 1.0)
+    table_ref[0:1, :] = target.astype(jnp.int32)
+    table_ref[1:2, :] = source.astype(jnp.int32)
+    table_ref[2:8, :] = jnp.full((6, count), fits, jnp.int32)
+
+    total = jnp.zeros((rows, count), jnp.float32)
+    for i in range(chunks):
+        for copy in copies[i]:
+            copy.wait()
+        g_high, g_low = split(kept_ref[:, i * block:(i + 1) * block])
+        c_high, c_low = split(lines_ref[i * block:(i + 1) * block, :])
+        wide_sum = jnp.dot(g_high, jnp.concatenate([c_high, c_low], axis=1), preferred_element_type=jnp.float32)
+        low_sum = jnp.dot(g_low, c_high, preferred_element_type=jnp.float32)
+        total = total + (wide_sum[:, :count] + (wide_sum[:, count:] + low_sum))
+    out_ref[...] = total
+
+    for slot in range(SLOTS):
+        at = pl.ds(local[slot], 1)
+        row = kept_ref[at, :]
+        extra = out_ref[at, :]
+        for q in range(XS):
+            pick_ref[q, slot:slot + 1, :width] = row[:, q * width:(q + 1) * width]
+            pick_ref[q, slot:slot + 1, width:] = extra
+
+
+def respond(gebhart, change, moved_nodes):
+    rows, nodes = gebhart.shape
+    count = change.shape[1]
+    chunks = 8
+    vmem = pl.BlockSpec(memory_space=pltpu.VMEM)
+    return pl.pallas_call(
+        respond_kernel,
+        out_shape=(
+            jax.ShapeDtypeStruct((rows, count), jnp.float32),
+            jax.ShapeDtypeStruct((XS, SLOTS, nodes // XS + count), jnp.float32),
+            jax.ShapeDtypeStruct((8, count), jnp.int32),
+        ),
+        in_specs=[
+            pl.BlockSpec(memory_space=pltpu.SMEM),
+            vmem,
+            pl.BlockSpec(memory_space=pl.ANY),
+            pl.BlockSpec(memory_space=pl.ANY),
+        ],
+        out_specs=(vmem, vmem, vmem),
+        scratch_shapes=[
+            pltpu.VMEM((rows, nodes), jnp.float32),
+            pltpu.VMEM((nodes, count), jnp.float32),
+            pltpu.SemaphoreType.DMA((chunks,)),
+            pltpu.SemaphoreType.DMA((chunks,)),
+        ],
+        compiler_params=pltpu.CompilerParams(vmem_limit_bytes=60 * 1024 * 1024),
+        name="respond_and_pick",
+    )(moved_nodes, moved_nodes.reshape(1, count), gebhart, change)
+
+
+def plane_kernel(table_ref, own_ref, other_ref, out_ref, rows_ref):
+    copies, plane, _ = out_ref.shape
+    count = table_ref.shape[1]
+    core = lax.axis_index("wide") % CORES
+    width = own_ref.shape[1] - count
+    part = width // CORES
+    slots = own_ref.shape[0]
+    for side, ref in ((0, own_ref), (1, other_ref)):
+        value = ref[...]
+        kept = jnp.where(core == 0, value[:, :part], value[:, part:width])
+        rows_ref[side * slots:(side + 1) * slots, :part] = kept
+        rows_ref[side * slots:(side + 1) * slots, part:] = value[:, width:]
+    for i in range(plane):
+        out_ref[0, i:i + 1, :] = rows_ref[pl.ds(table_ref[1, i], 1), :]
+    value = out_ref[0]
+    for copy in range(1, copies):
+        out_ref[copy] = value
+
+
+def plane_slots(table, own, other, planes):
+    count = table.shape[1]
+    slots, columns = own.shape
+    columns = (columns - count) // CORES + count
+    vmem = pl.BlockSpec(memory_space=pltpu.VMEM)
+    return pl.pallas_call(
+        plane_kernel,
+        out_shape=jax.ShapeDtypeStruct((planes, PLANE, columns), jnp.float32),
+        in_specs=[pl.BlockSpec(memory_space=pltpu.SMEM), vmem, vmem],
+        out_specs=vmem,
+        scratch_shapes=[pltpu.VMEM((2 * slots, columns), jnp.float32)],
+        compiler_params=pltpu.CompilerParams(vmem_limit_bytes=16 * 1024 * 1024),
+        name="plane_slots",
+    )(table, own, other)
+
+
+def order_kernel(table_ref, slots_ref, rows_ref, touched_ref):
+    count, part = rows_ref.shape
+    for k in range(count):
+        row = slots_ref[pl.ds(table_ref[0, k], 1), :]
+        rows_ref[k:k + 1, :] = row[:, :part]
+        touched_ref[0, k:k + 1, :] = row[:, part:]
+    touched = touched_ref[0]
+    for copy in range(1, touched_ref.shape[0]):
+        touched_ref[copy] = touched
+
+
+def order(table, slots, receivers):
+    count = table.shape[1]
+    part = slots.shape[1] - count
+    vmem = pl.BlockSpec(memory_space=pltpu.VMEM)
+    return pl.pallas_call(
+        order_kernel,
+        out_shape=(jax.ShapeDtypeStruct((count, part), jnp.float32), jax.ShapeDtypeStruct((receivers, count, count), jnp.float32)),
+        in_specs=[pl.BlockSpec(memory_space=pltpu.SMEM), vmem],
+        out_specs=(vmem, vmem),
+        compiler_params=pltpu.CompilerParams(vmem_limit_bytes=16 * 1024 * 1024),
+        name="order_rows",
+    )(table, slots)
 
 
 def pick_kernel(moved_ref, g_ref, keep_ref, send_ref, sem):
@@ -130,12 +297,12 @@
     return normal
 
 
-def invert_kernel(mine_ref, theirs_ref, out_ref):
-    core = lax.axis_index("wide") % CORES
-    mine, theirs = mine_ref[...], theirs_ref[...]
-    low = jnp.where(core == 0, mine, theirs)
-    high = jnp.where(core == 0, theirs, mine)
-    touched = jnp.concatenate([low, high], axis=0)
+def invert_kernel(parts_ref, g_ref, out_ref, kept_ref, sem):
+    copy = pltpu.make_async_copy(g_ref, kept_ref, sem)
+    copy.start()
+    touched = parts_ref[0]
+    for i in range(1, parts_ref.shape[0]):
+        touched = touched + parts_ref[i]
     count = touched.shape[0]
     row = lax.broadcasted_iota(jnp.int32, (count, count), 0)
     column = lax.broadcasted_iota(jnp.int32, (count, count), 1)
@@ -144,68 +311,69 @@
         capacitance, capacitance, (((1,), (1,)), ((), ())), precision=HIGHEST, preferred_element_type=jnp.float32
     )
     out_ref[...] = jnp.dot(spd_inverse(normal), capacitance, precision=HIGHEST, preferred_element_type=jnp.float32)
-
-
-def invert(mine, theirs):
-    count = mine.shape[1]
+    copy.wait()
+
+
+def invert(parts, gebhart):
+    vmem = pl.BlockSpec(memory_space=pltpu.VMEM)
     return pl.pallas_call(
         invert_kernel,
-        out_shape=jax.ShapeDtypeStruct((count, count), jnp.float32),
+        out_shape=(jax.ShapeDtypeStruct(parts.shape[1:], jnp.float32), pltpu.VMEM(gebhart.shape, jnp.float32)),
+        in_specs=[vmem, pl.BlockSpec(memory_space=pl.ANY)],
+        out_specs=(vmem, vmem),
+        scratch_shapes=[pltpu.SemaphoreType.DMA],
         cost_estimate=pl.CostEstimate(flops=30_000_000, bytes_accessed=200_000, transcendentals=0),
+        compiler_params=pltpu.CompilerParams(vmem_limit_bytes=16 * 1024 * 1024),
         name="invert_capacitance",
-    )(mine, theirs)
-
-
-def update_kernel(column_ref, inverse_ref, *refs):
-    narrow = len(refs) - 2 * XS - 3
-    parts, refs = refs[:narrow], refs[narrow:]
-    g_ref, mine, theirs, out_ref, left_ref = refs[0], refs[1:1 + XS], refs[1 + XS:1 + 2 * XS], refs[1 + 2 * XS], refs[2 + 2 * XS]
-    half = mine[0].shape[0]
-    step = pl.program_id(0)
-    core = lax.axis_index("wide") % CORES
-
-    @pl.when(step == 0)
-    def _():
-        response = parts[0][...]
-        for part in parts[1:]:
-            response = response + part[...]
-        solved = lax.dot_general(
-            response, inverse_ref[...], (((1,), (1,)), ((), ())), precision=HIGHEST, preferred_element_type=jnp.float32
-        )
-        low, high = solved[:, :half], solved[:, half:]
-        s_mine = jnp.where(core == 0, low, high)
-        s_theirs = jnp.where(core == 0, high, low)
-        s_high, s_low = split(jnp.concatenate([s_mine, s_theirs], axis=1))
-        left_ref[...] = jnp.concatenate([s_high, s_low, s_high], axis=1)
-
-    for j in range(XS):
-        @pl.when(step == j)
-        def _():
-            r_high, r_low = split(jnp.concatenate([mine[j][...], theirs[j][...]], axis=0))
+    )(parts, gebhart)
+
+
+def update_kernel(inverse_ref, g_ref, *refs):
+    out_ref, buffer_ref, sem = refs[-3:]
+    parts, pieces = refs[:-3 - 2 * XS], refs[-3 - 2 * XS:-3]
+    me = lax.axis_index("wide")
+    core = me % CORES
+    x = (me // CORES) % XS
+    part = pieces[0].shape[1]
+    width = CORES * part
+    response = parts[0][...]
+    for ref in parts[1:]:
+        response = response + ref[...]
+    solved = lax.dot_general(
+        response, inverse_ref[...], (((1,), (1,)), ((), ())), precision=HIGHEST, preferred_element_type=jnp.float32
+    )
+    s_high, s_low = split(solved)
+    left = jnp.concatenate([s_high, s_low, s_high], axis=1)
+    copies = []
+    for d in range(XS):
+        begin = lax.rem(x + (XS - d), XS) * width
+        mine, theirs = pieces[d][...], pieces[XS + d][...]
+        for side in range(CORES):
+            r_high, r_low = split(jnp.where(core == side, mine, theirs))
             right = jnp.concatenate([r_high, r_high, r_low], axis=0)
-            out_ref[...] = g_ref[...] + jnp.dot(left_ref[...], right, preferred_element_type=jnp.float32)
-
-
-def update(gebhart, inverse, parts, mine, theirs, columns):
-    rows, nodes = gebhart.shape
-    half, width = mine[0].shape
-    count = inverse.shape[0]
-    piece = pl.BlockSpec((half, width), lambda i, col: (0, 0))
-    block = pl.BlockSpec((rows, width), lambda i, col: (0, col[i]))
-    part = pl.BlockSpec((rows, count), lambda i, col: (0, 0))
+            here = pl.ds(pl.multiple_of(begin + side * part, part), part)
+            slot = d * CORES + side
+            buffer_ref[slot] = g_ref[:, here] + jnp.dot(left, right, preferred_element_type=jnp.float32)
+            copies.append(pltpu.make_async_copy(buffer_ref.at[slot], out_ref.at[:, here], sem.at[slot]))
+            copies[slot].start()
+    for copy in copies:
+        copy.wait()
+
+
+def update(kept, inverse, response, mine, theirs):
+    rows, nodes = kept.shape
+    part = mine[0].shape[1]
+    vmem = pl.BlockSpec(memory_space=pltpu.VMEM)
+    blocks = CORES * XS
     return pl.pallas_call(
         update_kernel,
         out_shape=jax.ShapeDtypeStruct((rows, nodes), jnp.float32),
-        grid_spec=pltpu.PrefetchScalarGridSpec(
-            num_scalar_prefetch=1,
-            grid=(XS,),
-            in_specs=[pl.BlockSpec((count, count), lambda i, col: (0, 0))] + [part] * len(parts) + [block] + [piece] * (2 * XS),
-            out_specs=block,
-            scratch_shapes=[pltpu.VMEM((rows, 3 * count), jnp.bfloat16)],
-        ),
-        compiler_params=pltpu.CompilerParams(vmem_limit_bytes=60 * 1024 * 1024),
+        in_specs=[vmem] * (2 + len(response) + 2 * XS),
+        out_specs=pl.BlockSpec(memory_space=pl.ANY),
+        scratch_shapes=[pltpu.VMEM((blocks, rows, part), jnp.float32), pltpu.SemaphoreType.DMA((blocks,))],
+        compiler_params=pltpu.CompilerParams(vmem_limit_bytes=20 * 1024 * 1024),
         name="update_rows",
-    )(columns, inverse, *parts, gebhart, *mine, *theirs)
+    )(inverse, kept, *response, *mine, *theirs)
 
 
 def body(wide, narrow, gebhart, change, moved_nodes):
@@ -230,47 +398,61 @@
     x_groups = [[index(z, x, c) for x in range(XS)] for z in range(zs) for c in range(CORES)]
     z_groups = [[index(z, x, c) for z in range(zs)] for x in range(XS) for c in range(CORES)]
 
-    owner = moved_nodes // rows_local
-    owner_half = lax.dynamic_slice(owner, (core * half,), (half,))
-    owner_core = owner_half % CORES
-    owner_x = (owner_half // CORES) % XS
-    owner_z = lax.dynamic_slice(owner_half // (CORES * XS), (z * group,), (group,))
-
-    keep, send = pick(gebhart, moved_nodes, half, width)
-    got = lax.ppermute(send, "wide", swap)
-
-    partial_value = jnp.dot(gebhart, change, preferred_element_type=jnp.float32, precision=lax.Precision.HIGH)
-    positions = me * rows_local + lax.broadcasted_iota(jnp.int32, (count, rows_local), 1)
-    select = (moved_nodes[:, None] == positions).astype(jnp.float32)
-    terms = jnp.dot(select, partial_value, preferred_element_type=jnp.float32, precision=HIGHEST)
-    terms_mine = lax.dynamic_slice(terms, (core * half, 0), (half, count))
-    terms_theirs = lax.dynamic_slice(terms, ((1 - core) * half, 0), (half, count))
-    terms_chip = terms_mine + lax.ppermute(terms_theirs, "wide", swap)
-    parts = [partial_value] + [lax.ppermute(partial_value, "narrow", shift_y[d]) for d in range(1, narrow)]
-
-    rows_chip = jnp.where((owner_core == core)[None, :, None], keep, got)
-    both = jnp.concatenate([rows_chip, jnp.broadcast_to(terms_chip[None], (XS, half, count))], axis=2)
-    both = lax.all_to_all(both, "wide", 0, 0, axis_index_groups=x_groups)
-    chosen = owner_x[None, :, None] == lax.broadcasted_iota(jnp.int32, (XS, 1, 1), 0)
-    both = jnp.sum(jnp.where(chosen, both, 0.0), axis=0)
-
-    both = lax.all_to_all(both.reshape(zs, group, width + count), "wide", 0, 0, axis_index_groups=z_groups)
-    chosen = owner_z[None, :, None] == lax.broadcasted_iota(jnp.int32, (zs, 1, 1), 0)
-    both = jnp.sum(jnp.where(chosen, both, 0.0), axis=0)
-    both = lax.all_to_all(jnp.broadcast_to(both[None], (zs,) + both.shape), "wide", 0, 0, axis_index_groups=z_groups)
-    both = both.reshape(half, width + count)
-
-    touched_part = both[:, width:]
-    touched = touched_part
-    for d in range(1, narrow):
-        touched = touched + lax.ppermute(touched_part, "narrow", shift_y[d])
-    inverse = invert(touched, lax.ppermute(touched, "wide", swap))
-
-    piece = both[:, :width]
-    pieces = [piece] + [lax.ppermute(piece, "wide", shift_x[d]) for d in range(1, XS)]
-    theirs = [lax.ppermute(p, "wide", swap) for p in pieces]
-    columns = jnp.stack([(x - d) % XS for d in range(XS)]).astype(jnp.int32)
-    return update(gebhart, inverse, parts, pieces, theirs, columns)
+    part = width // CORES
+    partial_value, picked, table = respond(gebhart, change, moved_nodes)
+
+    def received(value):
+        return [lax.ppermute(value, "narrow", shift_y[d]) for d in range(1, narrow)]
+
+    def spread(gebhart, moved_nodes, partial_value, picked, table):
+        own = lax.all_to_all(picked, "wide", 0, 0, axis_index_groups=x_groups).reshape(XS * SLOTS, width + count)
+        other = lax.ppermute(own, "wide", swap)
+        slots = plane_slots(table, own, other, zs)
+        slots, partial_value = lax.optimization_barrier((slots, partial_value))
+        parts = received(partial_value)
+        slots = lax.all_to_all(slots, "wide", 0, 0, axis_index_groups=z_groups)
+        return order(table, slots.reshape(zs * PLANE, part + count), narrow) + tuple(parts)
+
+    def crowded(gebhart, moved_nodes, partial_value, picked, table):
+        owner = moved_nodes // rows_local
+        owner_half = lax.dynamic_slice(owner, (core * half,), (half,))
+        owner_core = owner_half % CORES
+        owner_x = (owner_half // CORES) % XS
+        owner_z = lax.dynamic_slice(owner_half // (CORES * XS), (z * group,), (group,))
+
+        keep, send = pick(gebhart, moved_nodes, half, width)
+        got = lax.ppermute(send, "wide", swap)
+        positions = me * rows_local + lax.broadcasted_iota(jnp.int32, (count, rows_local), 1)
+        select = (moved_nodes[:, None] == positions).astype(jnp.float32)
+        terms = jnp.dot(select, partial_value, preferred_element_type=jnp.float32, precision=HIGHEST)
+        terms_mine = lax.dynamic_slice(terms, (core * half, 0), (half, count))
+        terms_theirs = lax.dynamic_slice(terms, ((1 - core) * half, 0), (half, count))
+        terms_chip = terms_mine + lax.ppermute(terms_theirs, "wide", swap)
+
+        rows_chip = jnp.where((owner_core == core)[None, :, None], keep, got)
+        both = jnp.concatenate([rows_chip, jnp.broadcast_to(terms_chip[None], (XS, half, count))], axis=2)
+        both = lax.all_to_all(both, "wide", 0, 0, axis_index_groups=x_groups)
+        chosen = owner_x[None, :, None] == lax.broadcasted_iota(jnp.int32, (XS, 1, 1), 0)
+        both = jnp.sum(jnp.where(chosen, both, 0.0), axis=0)
+
+        both = lax.all_to_all(both.reshape(zs, group, width + count), "wide", 0, 0, axis_index_groups=z_groups)
+        chosen = owner_z[None, :, None] == lax.broadcasted_iota(jnp.int32, (zs, 1, 1), 0)
+        both = jnp.sum(jnp.where(chosen, both, 0.0), axis=0)
+        both = lax.all_to_all(jnp.broadcast_to(both[None], (zs,) + both.shape), "wide", 0, 0, axis_index_groups=z_groups)
+        both = both.reshape(half, width + count)
+
+        mine = jnp.concatenate([lax.dynamic_slice(both, (0, core * part), (half, part)), both[:, width:]], axis=1)
+        theirs = jnp.concatenate([lax.dynamic_slice(both, (0, (1 - core) * part), (half, part)), both[:, width:]], axis=1)
+        theirs = lax.ppermute(theirs, "wide", swap)
+        both = jnp.where(core == 0, jnp.concatenate([mine, theirs]), jnp.concatenate([theirs, mine]))
+        return (both[:, :part], jnp.broadcast_to(both[None, :, part:], (narrow, count, count))) + tuple(received(partial_value))
+
+    mine, touched, *parts = lax.cond(table[2, 0] == 1, spread, crowded, gebhart, moved_nodes, partial_value, picked, table)
+    inverse, kept = invert(lax.all_to_all(touched, "narrow", 0, 0), gebhart)
+    pieces = [mine] + [lax.ppermute(mine, "wide", shift_x[d]) for d in range(1, XS)]
+    pieces, inverse = lax.optimization_barrier((pieces, inverse))
+    theirs = [lax.ppermute(piece, "wide", swap) for piece in pieces]
+    return update(kept, inverse, [partial_value] + parts, pieces, theirs)
 
 
 def solution(mesh):

time: 112 us -> 80.3 us (0.72)
  starting transfers between devices: 36.8 us -> 21 us
  waiting for transfers between devices: 32.2 us -> 19.7 us
  blocking collectives: 12.4 us -> 17.3 us
  matrix products: 4.36 us -> 0 us
  other arithmetic: 4.29 us -> 0 us
  Pallas kernels: 19 us -> 20.2 us
    ppermute x16 -> x11, starting transfers between devices: 24.1 us -> 12.9 us  [the longest x3 3.78 us: received(): return [lax.ppermute(value, 'narrow', shift_y[d]) for d in range(1, narrow)]]
    all_to_all x2 -> x1, waiting for transfers between devices: 25.8 us -> 17 us  [spread(): slots = lax.all_to_all(slots, 'wide', 0, 0, axis_index_groups=z_groups)]
    pallas_call x2 -> x4, Pallas kernels: 11.5 us -> 16.4 us  [the longest x1 8.63 us: invert(): pl.pallas_call(invert_kernel, out_shape=(jax.ShapeDtypeStruct(parts.shape...]
    all_to_all x1 -> x2, blocking collectives: 12.4 us -> 17.3 us  [the longest x1 9.5 us: body(): inverse, kept = invert(lax.all_to_all(touched, 'narrow', 0, 0), gebhart)]
    all_to_all x2 -> x1, starting transfers between devices: 12.7 us -> 8.18 us  [spread(): slots = lax.all_to_all(slots, 'wide', 0, 0, axis_index_groups=z_groups)]
    dot_general x2 -> x0, matrix products: 4.36 us -> none  [the longest x1 4.1 us: body(): jnp.dot(gebhart, change, preferred_element_type=jnp.float32, precision=la...]
    pallas_call x1, Pallas kernels: 7.56 us -> 3.84 us  [update(): pl.pallas_call(update_kernel, out_shape=jax.ShapeDtypeStruct((rows, nodes...]
    ppermute x16 -> x11, waiting for transfers between devices: 6.39 us -> 2.7 us  [the longest x4 1.67 us: body(): theirs = [lax.ppermute(piece, 'wide', swap) for piece in pieces]]
  transfers between devices with their start and end apart: 18 -> 12, of which waited for: 7 -> 6; matrix products, arithmetic and copies ran while one was open for 5% -> 0% of each run, Pallas kernels for 8% -> 12%
where the time goes in v3:
time: 80.3 us; the launch traced here: 79.7 us
  starting transfers between devices  21 us (26%)
  Pallas kernels  20.2 us (25%)
  waiting for transfers between devices  19.7 us (25%)
  blocking collectives  17.3 us (22%)
  between operations  0.88 us (1%)
    all_to_all x1, waiting for transfers between devices, spread(): slots = lax.all_to_all(slots, 'wide', 0, 0, axis_index_groups=z_groups)  17 us
    all_to_all x1, blocking collectives, body(): inverse, kept = invert(lax.all_to_all(touched, 'narrow', 0, 0), gebhart)  9.5 us
    pallas_call x1, Pallas kernels, invert(): pl.pallas_call(invert_kernel, out_shape=(jax.ShapeDtypeStruct(parts.shape...  8.63 us
    all_to_all x1, starting transfers between devices, spread(): slots = lax.all_to_all(slots, 'wide', 0, 0, axis_index_groups=z_groups)  8.18 us
    all_to_all x1, blocking collectives, spread(): lax.all_to_all(picked, 'wide', 0, 0, axis_index_groups=x_groups)  7.79 us
    pallas_call x1, Pallas kernels, respond(): pl.pallas_call(respond_kernel, out_shape=(jax.ShapeDtypeStruct((rows, cou...  5.35 us
    pallas_call x1, Pallas kernels, update(): pl.pallas_call(update_kernel, out_shape=jax.ShapeDtypeStruct((rows, nodes...  3.84 us
    ppermute x3, starting transfers between devices, received(): return [lax.ppermute(value, 'narrow', shift_y[d]) for d in range(1, narrow)]  3.78 us
  transfers between devices with their start and end apart: 12, of which 6 were waited for; matrix products, arithmetic and copies ran while one was open for 0% of the time, Pallas kernels for 12%

profile of v3, /device:TPU:3, one launch (start us, length us, event | category | flops | bytes accessed | tf_op | source)
XLA Modules:
  0.0 79.7 jit_solution(14753060452768626964)
XLA Ops:
  0.0 0.0 copy-start
  0.0 5.4 %respond_and_pick.1 = (f32[256,128]{1,0:T(8,128)S(1)}, f32[4,8,1152]{2,1,0:T(8,128)S(1)}, s32[8,128]{1,0:T(8,128)S(1)}) custom-call(s32[128]{0:T(128)} %moved_ref.1, s32[1,128]{1,0:T(1,128)} %bitcast.12, f32[256,4096]{1,0:T(8,128)} %g_ref.3, f32[4096,128]{1,0:T(8,128)} %change_ref.1), custom_call_target="tpu_custom_call" | custom-call | tf_op jit(solution)/shard_map/respond_and_pick/pallas_call | solution.py:97
  5.4 0.5 slice.13
  6.5 0.0 copy-done
  6.5 42.3 %conditional.1 = (f32[128,512]{1,0:T(8,128)S(1)}, f32[4,128,128]{2,1,0:T(8,128)S(1)}, f32[256,128]{1,0:T(8,128)}, f32[256,128]{1,0:T(8,128)}, f32[256,128]{1,0:T(8,128)}) conditional(s32[]{:T(128)} %bitcast.5, (pred[]{:T(512)}, s32[128]{0:T(128)S(1)}, s32[]{:T(128)}, f32[256,4096]{1,0:T(8,128)}, s32[]{:T(128)}, /*index=5*/f32[256,128]{1,0:T(8,128)S(1)}, ...), branch_computations={%region_0.3_spmd, %region_3.4_spmd} | conditional | flops 52039744 | bytes 22592168 | solution.py:450
  6.6 7.8 %all_to_all.25 = f32[4,8,1152]{2,1,0:T(8,128)S(1)} all-to-all(f32[4,8,1152]{2,1,0:T(8,128)S(1)} %get-tuple-element.32), channel_id=1, replica_groups={{0,8,16,24},{4,12,20,28},{32,40,48,56},{36,44,52,60},{64,72,80,88},{68,..., dimensions={0} | all-to-all | bytes 294912 | tf_op jit(solution)/shard_map/cond/branch_1_fun/all_to_all | solution.py:408
  14.4 2.1 %collective-permute-start = (f32[32,1152]{1,0:T(8,128)S(1)}, f32[32,1152]{1,0:T(8,128)S(1)}, u32[]{:S(2)}, u32[]{:S(2)}) collective-permute-start(f32[32,1152]{1,0:T(8,128)S(1)} %bitcast.8), channel_id=1, source_target_pairs={{0,4},{4,0},{8,12},{12,8},{16,20},{20,16},{24,28},{28,24},{32,36},... | collective-permute-start | bytes 442376 | tf_op jit(solution)/shard_map/cond/branch_1_fun/ppermute | solution.py:409
  16.5 1.0 %collective-permute-done.other_ref = f32[32,1152]{1,0:T(8,128)S(1)} collective-permute-done((f32[32,1152]{1,0:T(8,128)S(1)}, f32[32,1152]{1,0:T(8,128)S(1)}, u32[]{:S(2)}, u32[]{:S(2)}) %collective-permute-start) | collective-permute-done | bytes 147488 | tf_op jit(solution)/shard_map/cond/branch_1_fun/ppermute | solution.py:409
  17.5 1.5 %plane_slots.1 = f32[8,32,640]{2,1,0:T(8,128)} custom-call(s32[8,128]{1,0:T(8,128)S(1)} %get-tuple-element.31.table_ref, f32[32,1152]{1,0:T(8,128)S(1)} %bitcast.9, f32[32,1152]{1,0:T(8,128)S(1)} %collective-permute-done.other_ref), custom_call_target="tpu_custom_call" | custom-call | tf_op jit(solution)/shard_map/cond/branch_1_fun/plane_slots/pallas_call | solution.py:146
  19.0 8.2 %all-to-all-start.1 = ((f32[8,32,640]{2,1,0:T(8,128)}), f32[8,32,640]{2,1,0:T(8,128)S(1)}, u32[]{:S(2)}, u32[]{:S(2)}) async-start(f32[8,32,640]{2,1,0:T(8,128)} %plane_slots.1), calls=%async_computation.1 | async-start | bytes 1310720 | tf_op jit(solution)/shard_map/cond/branch_1_fun/all_to_all | solution.py:413
  27.2 2.7 %collective-permute-start.3 = (f32[256,128]{1,0:T(8,128)S(1)}, f32[256,128]{1,0:T(8,128)}, u32[]{:S(2)}, u32[]{:S(2)}) collective-permute-start(f32[256,128]{1,0:T(8,128)S(1)} %get-tuple-element.37), channel_id=1, source_target_pairs={{0,3},{1,0},{2,1},{3,2},{4,7},{5,4},{6,5},{7,6},{8,11},{9,8},{10,9... | collective-permute-start | bytes 393224 | tf_op jit(solution)/shard_map/cond/branch_1_fun/ppermute | solution.py:405
  29.9 0.4 collective-permute-start.2
  30.3 0.7 collective-permute-start.1
  31.0 17.0 %all-to-all-done.1 = f32[8,32,640]{2,1,0:T(8,128)S(1)} async-done(((f32[8,32,640]{2,1,0:T(8,128)}), f32[8,32,640]{2,1,0:T(8,128)S(1)}, u32[]{:S(2)}, u32[]{:S(2)}) %all-to-all-start.1) | async-done | bytes 655392 | tf_op jit(solution)/shard_map/cond/branch_1_fun/all_to_all | solution.py:413
  48.0 0.9 %order_rows.1 = (f32[128,512]{1,0:T(8,128)S(1)}, f32[4,128,128]{2,1,0:T(8,128)S(1)}) custom-call(s32[8,128]{1,0:T(8,128)S(1)} %get-tuple-element.31.table_ref, f32[256,640]{1,0:T(8,128)S(1)} %bitcast.7), custom_call_target="tpu_custom_call" | custom-call | tf_op jit(solution)/shard_map/cond/branch_1_fun/order_rows/pallas_call | solution.py:172
  48.8 0.0 collective-permute-done.3
  48.8 0.0 collective-permute-done.2
  48.8 0.0 collective-permute-done.1
  48.8 1.4 %collective-permute-start.12 = (f32[128,512]{1,0:T(8,128)S(1)}, f32[128,512]{1,0:T(8,128)S(1)}, u32[]{:S(2)}, u32[]{:S(2)}) collective-permute-start(f32[128,512]{1,0:T(8,128)S(1)} %get-tuple-element.64.refs_4_), channel_id=1, source_target_pairs={{0,24},{4,28},{8,0},{12,4},{16,8},{20,12},{24,16},{28,20},{32,56},... | collective-permute-start | bytes 786440 | tf_op jit(solution)/shard_map/ppermute | solution.py:452
  50.3 0.2 collective-permute-start.11
  50.5 1.8 %collective-permute-start.10 = (f32[128,512]{1,0:T(8,128)S(1)}, f32[128,512]{1,0:T(8,128)S(1)}, u32[]{:S(2)}, u32[]{:S(2)}) collective-permute-start(f32[128,512]{1,0:T(8,128)S(1)} %get-tuple-element.64.refs_4_), channel_id=1, source_target_pairs={{0,8},{4,12},{8,16},{12,20},{16,24},{20,28},{24,0},{28,4},{32,40},... | collective-permute-start | bytes 786440 | tf_op jit(solution)/shard_map/ppermute | solution.py:452
  52.4 9.5 %all_to_all.26.parts_ref = f32[4,128,128]{2,1,0:T(8,128)S(1)} all-to-all(f32[4,128,128]{2,1,0:T(8,128)S(1)} %get-tuple-element.57), channel_id=1, replica_groups=mesh['wide'=64,'narrow'=4] {'narrow'}, dimensions={0} | all-to-all | bytes 524288 | tf_op jit(solution)/shard_map/all_to_all | solution.py:451
  61.9 8.6 %invert_capacitance.1 = (f32[128,128]{1,0:T(8,128)S(1)}, f32[256,4096]{1,0:T(8,128)S(1)}) custom-call(f32[4,128,128]{2,1,0:T(8,128)S(1)} %all_to_all.26.parts_ref, f32[256,4096]{1,0:T(8,128)} %g_ref.3), custom_call_target="tpu_custom_call" | custom-call | flops 30000000 | bytes 200000 | tf_op jit(solution)/shard_map/invert_capacitance/pallas_call | solution.py:319
  70.5 0.0 collective-permute-done.12.refs_7_
  70.5 0.0 collective-permute-done.11.refs_6_
  70.5 0.0 collective-permute-done.10.refs_5_
  70.5 2.8 %collective-permute-start.13 = (f32[128,512]{1,0:T(8,128)S(1)}, f32[128,512]{1,0:T(8,128)S(1)}, u32[]{:S(2)}, u32[]{:S(2)}) collective-permute-start(f32[128,512]{1,0:T(8,128)S(1)} %get-tuple-element.64.refs_4_), channel_id=1, source_target_pairs={{0,4},{4,0},{8,12},{12,8},{16,20},{20,16},{24,28},{28,24},{32,36},... | collective-permute-start | bytes 786440 | tf_op jit(solution)/shard_map/ppermute | solution.py:454
  73.4 0.1 collective-permute-start.14
  73.5 0.4 collective-permute-start.15
  73.9 0.1 collective-permute-start.16
  74.0 0.6 collective-permute-done.13.refs_8_
  74.5 0.4 collective-permute-done.14.refs_9_
  74.9 0.4 collective-permute-done.15.refs_10_
  75.3 0.4 collective-permute-done.16.refs_11_
  75.7 3.8 %update_rows.1 = f32[256,4096]{1,0:T(8,128)} custom-call(f32[128,128]{1,0:T(8,128)S(1)} %get-tuple-element.59.inverse_ref, f32[256,4096]{1,0:T(8,128)S(1)} %get-tuple-element.60.g_ref, f32[256,128]{1,0:T(8,128)S(1)} %get-tuple-element.54.refs_0_, f32[256,128]{1,0:T(8,128)} %get-tuple-element.61.refs_1_, f32[256,128]{1,0:T(8,128)} %get-tuple-element.62.refs_2_, ...), custom_call_target="tpu_custom_call" | custom-call | tf_op jit(solution)/shard_map/update_rows/pallas_call | solution.py:368
Async XLA Ops:
  0.0 6.5 %copy-start = (s32[128]{0:T(128)S(1)}, s32[128]{0:T(128)}, u32[]{:S(2)}) copy-start(s32[128]{0:T(128)} %moved_ref.1) | copy-start | bytes 1540
  14.4 3.1 %collective-permute-start = (f32[32,1152]{1,0:T(8,128)S(1)}, f32[32,1152]{1,0:T(8,128)S(1)}, u32[]{:S(2)}, u32[]{:S(2)}) collective-permute-start(f32[32,1152]{1,0:T(8,128)S(1)} %bitcast.8), channel_id=1, source_target_pairs={{0,4},{4,0},{8,12},{12,8},{16,20},{20,16},{24,28},{28,24},{32,36},... | collective-permute-start | bytes 442376 | tf_op jit(solution)/shard_map/cond/branch_1_fun/ppermute | solution.py:409
  19.0 28.9 %all-to-all-start.1 = ((f32[8,32,640]{2,1,0:T(8,128)}), f32[8,32,640]{2,1,0:T(8,128)S(1)}, u32[]{:S(2)}, u32[]{:S(2)}) async-start(f32[8,32,640]{2,1,0:T(8,128)} %plane_slots.1), calls=%async_computation.1 | async-start | bytes 1310720 | tf_op jit(solution)/shard_map/cond/branch_1_fun/all_to_all | solution.py:413
  27.2 21.6 %collective-permute-start.3 = (f32[256,128]{1,0:T(8,128)S(1)}, f32[256,128]{1,0:T(8,128)}, u32[]{:S(2)}, u32[]{:S(2)}) collective-permute-start(f32[256,128]{1,0:T(8,128)S(1)} %get-tuple-element.37), channel_id=1, source_target_pairs={{0,3},{1,0},{2,1},{3,2},{4,7},{5,4},{6,5},{7,6},{8,11},{9,8},{10,9... | collective-permute-start | bytes 393224 | tf_op jit(solution)/shard_map/cond/branch_1_fun/ppermute | solution.py:405
  29.9 18.9 %collective-permute-start.2 = (f32[256,128]{1,0:T(8,128)S(1)}, f32[256,128]{1,0:T(8,128)}, u32[]{:S(2)}, u32[]{:S(2)}) collective-permute-start(f32[256,128]{1,0:T(8,128)S(1)} %get-tuple-element.37), channel_id=1, source_target_pairs={{0,2},{1,3},{2,0},{3,1},{4,6},{5,7},{6,4},{7,5},{8,10},{9,11},{10,... | collective-permute-start | bytes 393224 | tf_op jit(solution)/shard_map/cond/branch_1_fun/ppermute | solution.py:405
  30.3 18.5 %collective-permute-start.1 = (f32[256,128]{1,0:T(8,128)S(1)}, f32[256,128]{1,0:T(8,128)}, u32[]{:S(2)}, u32[]{:S(2)}) collective-permute-start(f32[256,128]{1,0:T(8,128)S(1)} %get-tuple-element.37), channel_id=1, source_target_pairs={{0,1},{1,2},{2,3},{3,0},{4,5},{5,6},{6,7},{7,4},{8,9},{9,10},{10,1... | collective-permute-start | bytes 393224 | tf_op jit(solution)/shard_map/cond/branch_1_fun/ppermute | solution.py:405
  48.8 21.7 %collective-permute-start.12 = (f32[128,512]{1,0:T(8,128)S(1)}, f32[128,512]{1,0:T(8,128)S(1)}, u32[]{:S(2)}, u32[]{:S(2)}) collective-permute-start(f32[128,512]{1,0:T(8,128)S(1)} %get-tuple-element.64.refs_4_), channel_id=1, source_target_pairs={{0,24},{4,28},{8,0},{12,4},{16,8},{20,12},{24,16},{28,20},{32,56},... | collective-permute-start | bytes 786440 | tf_op jit(solution)/shard_map/ppermute | solution.py:452
  50.3 20.2 %collective-permute-start.11 = (f32[128,512]{1,0:T(8,128)S(1)}, f32[128,512]{1,0:T(8,128)S(1)}, u32[]{:S(2)}, u32[]{:S(2)}) collective-permute-start(f32[128,512]{1,0:T(8,128)S(1)} %get-tuple-element.64.refs_4_), channel_id=1, source_target_pairs={{0,16},{4,20},{8,24},{12,28},{16,0},{20,4},{24,8},{28,12},{32,48},... | collective-permute-start | bytes 786440 | tf_op jit(solution)/shard_map/ppermute | solution.py:452
  50.5 20.0 %collective-permute-start.10 = (f32[128,512]{1,0:T(8,128)S(1)}, f32[128,512]{1,0:T(8,128)S(1)}, u32[]{:S(2)}, u32[]{:S(2)}) collective-permute-start(f32[128,512]{1,0:T(8,128)S(1)} %get-tuple-element.64.refs_4_), channel_id=1, source_target_pairs={{0,8},{4,12},{8,16},{12,20},{16,24},{20,28},{24,0},{28,4},{32,40},... | collective-permute-start | bytes 786440 | tf_op jit(solution)/shard_map/ppermute | solution.py:452
  70.5 4.0 %collective-permute-start.13 = (f32[128,512]{1,0:T(8,128)S(1)}, f32[128,512]{1,0:T(8,128)S(1)}, u32[]{:S(2)}, u32[]{:S(2)}) collective-permute-start(f32[128,512]{1,0:T(8,128)S(1)} %get-tuple-element.64.refs_4_), channel_id=1, source_target_pairs={{0,4},{4,0},{8,12},{12,8},{16,20},{20,16},{24,28},{28,24},{32,36},... | collective-permute-start | bytes 786440 | tf_op jit(solution)/shard_map/ppermute | solution.py:454
  73.4 1.5 %collective-permute-start.14 = (f32[128,512]{1,0:T(8,128)S(1)}, f32[128,512]{1,0:T(8,128)S(1)}, u32[]{:S(2)}, u32[]{:S(2)}) collective-permute-start(f32[128,512]{1,0:T(8,128)S(1)} %collective-permute-done.10.refs_5_), channel_id=1, source_target_pairs={{0,4},{4,0},{8,12},{12,8},{16,20},{20,16},{24,28},{28,24},{32,36},... | collective-permute-start | bytes 786440 | tf_op jit(solution)/shard_map/ppermute | solution.py:454
  73.5 1.8 %collective-permute-start.15 = (f32[128,512]{1,0:T(8,128)S(1)}, f32[128,512]{1,0:T(8,128)S(1)}, u32[]{:S(2)}, u32[]{:S(2)}) collective-permute-start(f32[128,512]{1,0:T(8,128)S(1)} %collective-permute-done.11.refs_6_), channel_id=1, source_target_pairs={{0,4},{4,0},{8,12},{12,8},{16,20},{20,16},{24,28},{28,24},{32,36},... | collective-permute-start | bytes 786440 | tf_op jit(solution)/shard_map/ppermute | solution.py:454
  73.9 1.8 %collective-permute-start.16 = (f32[128,512]{1,0:T(8,128)S(1)}, f32[128,512]{1,0:T(8,128)S(1)}, u32[]{:S(2)}, u32[]{:S(2)}) collective-permute-start(f32[128,512]{1,0:T(8,128)S(1)} %collective-permute-done.12.refs_7_), channel_id=1, source_target_pairs={{0,4},{4,0},{8,12},{12,8},{16,20},{20,16},{24,28},{28,24},{32,36},... | collective-permute-start | bytes 786440 | tf_op jit(solution)/shard_map/ppermute | solution.py:454

commit v4 on v3

v4 whole, which is shorter than its diff:
```python
import functools

import jax
import jax.numpy as jnp
from jax import lax
from jax.experimental import pallas as pl
from jax.experimental.pallas import tpu as pltpu
from jax.sharding import PartitionSpec as P

HIGHEST = lax.Precision.HIGHEST
CORES = 2
XS = 4
SLOTS = 8
PLANE = 32


def pick_kernel(lanes_ref, g_ref, change_ref, *refs):
    pick_refs, table_ref, line_ref, lines_ref, halves_ref, row_sem, sem = refs[:XS], *refs[XS:]
    nodes, count = lines_ref.shape
    rows = g_ref.shape[0]
    width = nodes // XS
    chunks = sem.shape[0]
    block = nodes // chunks
    me = lax.axis_index("wide")
    first = me * rows
    x = (me // CORES) % XS

    copies = []
    for i in range(chunks):
        span = pl.ds(i * block, block)
        copies.append(pltpu.make_async_copy(change_ref.at[span, :], lines_ref.at[span, :], sem.at[i]))
        copies[i].start()

    node_across = jnp.broadcast_to(lanes_ref[...].astype(jnp.float32), (count, count))
    node_down = node_across.T
    across = jnp.floor(node_across / float(rows))
    down = jnp.floor(node_down / float(rows))
    i = lax.broadcasted_iota(jnp.int32, (count, count), 0)
    j = lax.broadcasted_iota(jnp.int32, (count, count), 1)
    one = jnp.where(across == down, 1.0, 0.0)
    slot = jnp.sum(jnp.where(j < i, one, 0.0), axis=1, keepdims=True)
    match = jnp.logical_and(down == me.astype(jnp.float32), slot == j.astype(jnp.float32))
    local = jnp.sum(jnp.where(match, node_down - first.astype(jnp.float32), 0.0), axis=0, keepdims=True).astype(jnp.int32)
    picks = []
    for s in range(SLOTS):
        picks.append(pltpu.make_async_copy(g_ref.at[pl.ds(local[0, s], 1), :], line_ref.at[pl.ds(s, 1), :], row_sem.at[s]))
        picks[s].start()

    per_plane = float(CORES * XS)
    plane_across = jnp.floor(across / per_plane)
    plane_down = jnp.floor(down / per_plane)
    plane = jnp.where(plane_across == plane_down, 1.0, 0.0)
    rank = jnp.sum(jnp.where(j < i, plane, 0.0), axis=1, keepdims=True)
    rank_across = jnp.sum(jnp.where(i < j, plane, 0.0), axis=0, keepdims=True)
    fits = jnp.where(jnp.logical_and(jnp.max(slot) < SLOTS, jnp.max(rank) < PLANE), 1, 0)
    inside = down - plane_down * per_plane
    x_down = jnp.floor(inside / float(CORES))
    core_down = inside - x_down * float(CORES)
    behind = x.astype(jnp.float32) - x_down
    behind = jnp.where(behind < 0, behind + float(XS), behind)
    side = jnp.where(core_down == (me % CORES).astype(jnp.float32), 0.0, float(XS * SLOTS))
    here = plane_down == (me // (CORES * XS)).astype(jnp.float32)
    match = jnp.logical_and(here, rank == j.astype(jnp.float32))
    source = jnp.sum(jnp.where(match, behind * float(SLOTS) + jnp.minimum(slot, SLOTS - 1.0) + side, 0.0), axis=0, keepdims=True)
    target = plane_across[:1] * float(PLANE) + jnp.minimum(rank_across, PLANE - 1.0)
    table_ref[0:1, :] = target.astype(jnp.int32)
    table_ref[1:2, :] = source.astype(jnp.int32)
    table_ref[2:8, :] = jnp.full((6, count), fits, jnp.int32)

    for i in range(chunks):
        span = pl.ds(i * block, block)
        copies[i].wait()
        c_high, c_low = split(lines_ref[span, :])
        halves_ref[span, :count] = c_high
        halves_ref[span, count:] = c_low
    for pick in picks:
        pick.wait()
    r_high, r_low = split(line_ref[...])
    both = jnp.dot(jnp.concatenate([r_high, r_low], axis=0), halves_ref[...], preferred_element_type=jnp.float32)
    terms = both[:SLOTS, :count] + (both[:SLOTS, count:] + both[SLOTS:, :count])
    for d in range(XS):
        quarter = pl.ds(pl.multiple_of(lax.rem(x + d, XS) * width, width), width)
        pick_refs[d][:, :width] = line_ref[:, quarter]
        pick_refs[d][:, width:] = terms


def pick_slots(gebhart, change, moved_nodes):
    nodes, count = change.shape
    chunks = 4
    vmem = pl.BlockSpec(memory_space=pltpu.VMEM)
    hbm = pl.BlockSpec(memory_space=pl.ANY)
    *picked, table = pl.pallas_call(
        pick_kernel,
        out_shape=(jax.ShapeDtypeStruct((SLOTS, nodes // XS + count), jnp.float32),) * XS
        + (jax.ShapeDtypeStruct((8, count), jnp.int32),),
        in_specs=[vmem, hbm, hbm],
        out_specs=(vmem,) * (XS + 1),
        scratch_shapes=[
            pltpu.VMEM((SLOTS, nodes), jnp.float32),
            pltpu.VMEM((nodes, count), jnp.float32),
            pltpu.VMEM((nodes, 2 * count), jnp.bfloat16),
            pltpu.SemaphoreType.DMA((SLOTS,)),
            pltpu.SemaphoreType.DMA((chunks,)),
        ],
        compiler_params=pltpu.CompilerParams(vmem_limit_bytes=60 * 1024 * 1024),
        name="pick_slots",
    )(moved_nodes.reshape(1, count), gebhart, change)
    return picked, table


def respond_kernel(token_ref, g_ref, change_ref, out_ref, kept_ref, lines_ref, g_sem, c_sem):
    rows, count = out_ref.shape
    chunks = g_sem.shape[0]
    block = kept_ref.shape[1] // chunks
    copies = []
    for i in range(chunks):
        span = pl.ds(i * block, block)
        copies.append((
            pltpu.make_async_copy(g_ref.at[:, span], kept_ref.at[:, span], g_sem.at[i]),
            pltpu.make_async_copy(change_ref.at[span, :], lines_ref.at[span, :], c_sem.at[i]),
        ))
        for copy in copies[-1]:
            copy.start()
    total = jnp.zeros((rows, count), jnp.float32)
    for i in range(chunks):
        for copy in copies[i]:
            copy.wait()
        g_high, g_low = split(kept_ref[:, i * block:(i + 1) * block])
        c_high, c_low = split(lines_ref[i * block:(i + 1) * block, :])
        wide_sum = jnp.dot(g_high, jnp.concatenate([c_high, c_low], axis=1), preferred_element_type=jnp.float32)
        low_sum = jnp.dot(g_low, c_high, preferred_element_type=jnp.float32)
        total = total + (wide_sum[:, :count] + (wide_sum[:, count:] + low_sum))
    out_ref[...] = total


def respond(token, gebhart, change):
    rows, nodes = gebhart.shape
    count = change.shape[1]
    chunks = 8
    vmem = pl.BlockSpec(memory_space=pltpu.VMEM)
    hbm = pl.BlockSpec(memory_space=pl.ANY)
    return pl.pallas_call(
        respond_kernel,
        out_shape=jax.ShapeDtypeStruct((rows, count), jnp.float32),
        in_specs=[vmem, hbm, hbm],
        out_specs=vmem,
        scratch_shapes=[
            pltpu.VMEM((rows, nodes), jnp.float32),
            pltpu.VMEM((nodes, count), jnp.float32),
            pltpu.SemaphoreType.DMA((chunks,)),
            pltpu.SemaphoreType.DMA((chunks,)),
        ],
        cost_estimate=pl.CostEstimate(flops=800_000_000, bytes_accessed=8_000_000, transcendentals=0),
        compiler_params=pltpu.CompilerParams(vmem_limit_bytes=24 * 1024 * 1024),
        name="respond",
    )(token, gebhart, change)


def plane_kernel(table_ref, *refs):
    slots_refs, out_ref, rows_ref = refs[:-2], refs[-2], refs[-1]
    copies, plane, columns = out_ref.shape
    count = table_ref.shape[1]
    core = lax.axis_index("wide") % CORES
    part = columns - count
    width = CORES * part
    for i, ref in enumerate(slots_refs):
        value = ref[...]
        here = slice(i * SLOTS, (i + 1) * SLOTS)
        rows_ref[here, :part] = jnp.where(core == 0, value[:, :part], value[:, part:width])
        rows_ref[here, part:] = value[:, width:]
    for i in range(plane):
        out_ref[0, i:i + 1, :] = rows_ref[pl.ds(table_ref[1, i], 1), :]
    value = out_ref[0]
    for copy in range(1, copies):
        out_ref[copy] = value


def plane_slots(table, slots, planes):
    count = table.shape[1]
    columns = (slots[0].shape[1] - count) // CORES + count
    vmem = pl.BlockSpec(memory_space=pltpu.VMEM)
    return pl.pallas_call(
        plane_kernel,
        out_shape=jax.ShapeDtypeStruct((planes, PLANE, columns), jnp.float32),
        in_specs=[pl.BlockSpec(memory_space=pltpu.SMEM)] + [vmem] * len(slots),
        out_specs=vmem,
        scratch_shapes=[pltpu.VMEM((len(slots) * SLOTS, columns), jnp.float32)],
        compiler_params=pltpu.CompilerParams(vmem_limit_bytes=16 * 1024 * 1024),
        name="plane_slots",
    )(table, *slots)


def order_kernel(table_ref, slots_ref, rows_ref, touched_ref):
    copies, count, part = rows_ref.shape
    for k in range(count):
        row = slots_ref[pl.ds(table_ref[0, k], 1), :]
        rows_ref[0, k:k + 1, :] = row[:, :part]
        touched_ref[k:k + 1, :] = row[:, part:]
    rows = rows_ref[0]
    for copy in range(1, copies):
        rows_ref[copy] = rows


def order(table, slots):
    count = table.shape[1]
    part = slots.shape[1] - count
    vmem = pl.BlockSpec(memory_space=pltpu.VMEM)
    return pl.pallas_call(
        order_kernel,
        out_shape=(jax.ShapeDtypeStruct((XS, count, part), jnp.float32), jax.ShapeDtypeStruct((count, count), jnp.float32)),
        in_specs=[pl.BlockSpec(memory_space=pltpu.SMEM), vmem],
        out_specs=(vmem, vmem),
        compiler_params=pltpu.CompilerParams(vmem_limit_bytes=16 * 1024 * 1024),
        name="order_rows",
    )(table, slots)


def pick_all_kernel(moved_ref, g_ref, keep_ref, send_ref, sem):
    rows_local = g_ref.shape[0]
    quarters, half, width = keep_ref.shape
    me = lax.axis_index("wide")
    first = me * rows_local
    core = me % CORES

    def copy(local, target, row, q):
        return pltpu.make_async_copy(
            g_ref.at[pl.ds(local, 1), pl.ds(q * width, width)], target.at[q, pl.ds(row, 1), :], sem
        )

    total = 0
    for side in range(CORES):
        def start(row, found, side=side):
            local = moved_ref[side * half + row] - first
            owned = jnp.logical_and(local >= 0, local < rows_local)

            @pl.when(owned)
            def _():
                @pl.when(core == side)
                def _():
                    for q in range(quarters):
                        copy(local, keep_ref, row, q).start()

                @pl.when(core != side)
                def _():
                    for q in range(quarters):
                        copy(local, send_ref, row, q).start()

            return found + jnp.where(owned, 1, 0)

        total = lax.fori_loop(0, half, start, total, unroll=8)

    def wait(i, carry):
        for q in range(quarters):
            copy(0, keep_ref, 0, q).wait()
        return carry

    lax.fori_loop(0, total, wait, 0)


def pick_all(gebhart, moved_nodes, half, width):
    shape = jax.ShapeDtypeStruct((XS, half, width), jnp.float32)
    return pl.pallas_call(
        pick_all_kernel,
        out_shape=(shape, shape),
        in_specs=[pl.BlockSpec(memory_space=pltpu.SMEM), pl.BlockSpec(memory_space=pl.ANY)],
        out_specs=(pl.BlockSpec(memory_space=pl.ANY), pl.BlockSpec(memory_space=pl.ANY)),
        scratch_shapes=[pltpu.SemaphoreType.DMA],
        compiler_params=pltpu.CompilerParams(vmem_limit_bytes=60 * 1024 * 1024),
        name="pick_rows",
    )(moved_nodes, gebhart)


def split(value):
    high = value.astype(jnp.bfloat16)
    low = (value - high.astype(jnp.float32)).astype(jnp.bfloat16)
    return high, low


def pair_inverse(p, q, s):
    scale = 1.0 / (p * s - q * q)
    return s * scale, -q * scale, p * scale


def quad_inverse(e):
    a, b, c = pair_inverse(e[0][0], e[0][1], e[1][1])
    t = [[a * e[0][2] + b * e[1][2], a * e[0][3] + b * e[1][3]], [b * e[0][2] + c * e[1][2], b * e[0][3] + c * e[1][3]]]
    s22 = e[2][2] - (e[0][2] * t[0][0] + e[1][2] * t[1][0])
    s23 = e[2][3] - (e[0][2] * t[0][1] + e[1][2] * t[1][1])
    s33 = e[3][3] - (e[0][3] * t[0][1] + e[1][3] * t[1][1])
    f, g, h = pair_inverse(s22, s23, s33)
    w = [[t[0][0] * f + t[0][1] * g, t[0][0] * g + t[0][1] * h], [t[1][0] * f + t[1][1] * g, t[1][0] * g + t[1][1] * h]]
    i00 = a + w[0][0] * t[0][0] + w[0][1] * t[0][1]
    i01 = b + w[0][0] * t[1][0] + w[0][1] * t[1][1]
    i11 = c + w[1][0] * t[1][0] + w[1][1] * t[1][1]
    return [
        [i00, i01, -w[0][0], -w[0][1]],
        [i01, i11, -w[1][0], -w[1][1]],
        [-w[0][0], -w[1][0], f, g],
        [-w[0][1], -w[1][1], g, h],
    ]


def spd_inverse(normal, block=16):
    pivots = 4
    count = normal.shape[0]
    lane = lax.broadcasted_iota(jnp.int32, (1, count), 1)
    sub = lax.broadcasted_iota(jnp.int32, (block, 1), 0)
    for first in range(0, count, block):
        panel = normal[first:first + block, :]
        for i in range(0, block, pivots):
            k = first + i
            cols = [jnp.broadcast_to(panel[:, k + m:k + m + 1], (block, count)) for m in range(pivots)]
            entry = [[jnp.broadcast_to(cols[n][i + m:i + m + 1, :], (8, count)) for n in range(pivots)] for m in range(pivots)]
            q = quad_inverse(entry)
            inside = jnp.logical_and(lane >= k, lane < k + pivots)
            rows = [
                jnp.where(inside, jnp.where(lane == k + m, 1.0, 0.0), jnp.broadcast_to(panel[i + m:i + m + 1, :], (8, count)))
                for m in range(pivots)
            ]
            new = [q[m][0] * rows[0] + (q[m][1] * rows[1] + (q[m][2] * rows[2] + q[m][3] * rows[3])) for m in range(pivots)]
            new = [jnp.concatenate([row] * (block // 8), axis=0) for row in new]
            panel = jnp.where(inside, 0.0, panel)
            for m in range(pivots):
                panel = panel - cols[m] * new[m]
            for m in range(pivots):
                panel = jnp.where(sub == i + m, new[m], panel)
        within = jnp.logical_and(lane >= first, lane < first + block)
        outer = jnp.dot(normal[:, first:first + block], panel, precision=HIGHEST, preferred_element_type=jnp.float32)
        rest = jnp.where(within, 0.0, normal) - outer
        above = [rest[:first]] if first > 0 else []
        below = [rest[first + block:]] if first + block < count else []
        normal = jnp.concatenate(above + [panel] + below, axis=0)
    return normal


def invert_kernel(*refs):
    out_ref = refs[-1]
    touched = refs[0][...]
    for ref in refs[1:-1]:
        touched = touched + ref[...]
    count = touched.shape[0]
    row = lax.broadcasted_iota(jnp.int32, (count, count), 0)
    column = lax.broadcasted_iota(jnp.int32, (count, count), 1)
    capacitance = jnp.where(row == column, 1.0, 0.0) - touched
    normal = lax.dot_general(
        capacitance, capacitance, (((1,), (1,)), ((), ())), precision=HIGHEST, preferred_element_type=jnp.float32
    )
    out_ref[...] = jnp.dot(spd_inverse(normal), capacitance, precision=HIGHEST, preferred_element_type=jnp.float32)


def invert(parts):
    vmem = pl.BlockSpec(memory_space=pltpu.VMEM)
    return pl.pallas_call(
        invert_kernel,
        out_shape=jax.ShapeDtypeStruct(parts[0].shape, jnp.float32),
        in_specs=[vmem] * len(parts),
        out_specs=vmem,
        cost_estimate=pl.CostEstimate(flops=2_000_000_000, bytes_accessed=8_000_000, transcendentals=0),
        compiler_params=pltpu.CompilerParams(vmem_limit_bytes=16 * 1024 * 1024),
        name="invert_capacitance",
    )(*parts)


def places(core, part):
    return [pl.ds(pl.multiple_of((q * CORES + core) * part, part), part) for q in range(XS)]


def write_blocks(left, blocks, ready, pieces_ref, out_ref, buffer_ref, sem, core):
    copies = []
    for q, here in enumerate(places(core, pieces_ref.shape[2])):
        r_high, r_low = split(pieces_ref[q])
        right = jnp.concatenate([r_high, r_high, r_low], axis=0)
        change = jnp.dot(left, right, preferred_element_type=jnp.float32)
        if ready is not None:
            ready[q].wait()
        buffer_ref[q] = blocks[q] + change
        copies.append(pltpu.make_async_copy(buffer_ref.at[q], out_ref.at[:, here], sem.at[q]))
        copies[q].start()
    for copy in copies:
        copy.wait()


def update_own_kernel(inverse_ref, g_ref, pieces_ref, *refs):
    out_ref, left_ref, other_ref, own_ref, buffer_ref, own_sem, other_sem, sem = refs[-8:]
    core = lax.axis_index("wide") % CORES
    part = pieces_ref.shape[2]
    ready = []
    for q, here in enumerate(places(core, part)):
        ready.append(pltpu.make_async_copy(g_ref.at[:, here], own_ref.at[q], own_sem.at[q]))
        ready[q].start()
    later = []
    for q, here in enumerate(places(1 - core, part)):
        later.append(pltpu.make_async_copy(g_ref.at[:, here], other_ref.at[q], other_sem.at[q]))
        later[q].start()
    response = refs[0][...]
    for ref in refs[1:-8]:
        response = response + ref[...]
    solved = lax.dot_general(
        response, inverse_ref[...], (((1,), (1,)), ((), ())), precision=HIGHEST, preferred_element_type=jnp.float32
    )
    s_high, s_low = split(solved)
    left = jnp.concatenate([s_high, s_low, s_high], axis=1)
    left_ref[...] = left
    write_blocks(left, own_ref, ready, pieces_ref, out_ref, buffer_ref, sem, core)
    for copy in later:
        copy.wait()


def update_other_kernel(left_ref, blocks_ref, pieces_ref, before_ref, out_ref, buffer_ref, sem):
    write_blocks(left_ref[...], blocks_ref, None, pieces_ref, out_ref, buffer_ref, sem, 1 - lax.axis_index("wide") % CORES)


def update(gebhart, inverse, response, pieces, swapped):
    rows, nodes = gebhart.shape
    count, part = pieces.shape[1:]
    vmem = pl.BlockSpec(memory_space=pltpu.VMEM)
    hbm = pl.BlockSpec(memory_space=pl.ANY)
    whole = jax.ShapeDtypeStruct((rows, nodes), jnp.float32)
    blocks = pltpu.VMEM((XS, rows, part), jnp.float32)
    sems = pltpu.SemaphoreType.DMA((XS,))
    own, left, other = pl.pallas_call(
        update_own_kernel,
        out_shape=(whole, jax.ShapeDtypeStruct((rows, 3 * count), jnp.bfloat16), blocks),
        in_specs=[vmem, hbm] + [vmem] * (1 + len(response)),
        out_specs=(hbm, vmem, vmem),
        scratch_shapes=[blocks, blocks, sems, sems, sems],
        cost_estimate=pl.CostEstimate(flops=1_000_000_000, bytes_accessed=6_000_000, transcendentals=0),
        compiler_params=pltpu.CompilerParams(vmem_limit_bytes=20 * 1024 * 1024),
        name="update_own",
    )(inverse, gebhart, pieces, *response)
    return pl.pallas_call(
        update_other_kernel,
        out_shape=whole,
        in_specs=[vmem, vmem, vmem, hbm],
        out_specs=hbm,
        scratch_shapes=[blocks, sems],
        input_output_aliases={3: 0},
        compiler_params=pltpu.CompilerParams(vmem_limit_bytes=20 * 1024 * 1024),
        name="update_other",
    )(left, other, swapped, own)


def body(wide, narrow, gebhart, change, moved_nodes):
    rows_local, width_local = gebhart.shape
    count = moved_nodes.shape[0]
    half = count // CORES
    zs = wide // (CORES * XS)
    width = width_local // XS
    group = half // zs
    me = lax.axis_index("wide")
    core = me % CORES
    x = (me // CORES) % XS
    z = me // (CORES * XS)

    def index(z, x, c):
        return (z * XS + x) * CORES + c

    places = [(z, x, c) for z in range(zs) for x in range(XS) for c in range(CORES)]
    swap = [(index(z, x, c), index(z, x, (c + 1) % CORES)) for z, x, c in places]
    shift_x = [[(index(z, x, c), index(z, (x + d) % XS, c)) for z, x, c in places] for d in range(XS)]
    shift_y = [[(i, (i + d) % narrow) for i in range(narrow)] for d in range(narrow)]
    x_groups = [[index(z, x, c) for x in range(XS)] for z in range(zs) for c in range(CORES)]
    z_groups = [[index(z, x, c) for z in range(zs)] for x in range(XS) for c in range(CORES)]

    part = width // CORES
    picked, table = pick_slots(gebhart, change, moved_nodes)

    def received(value):
        return [lax.ppermute(value, "narrow", shift_y[d]) for d in range(1, narrow)]

    def finish(rows, touched, response, gebhart):
        pieces = lax.all_to_all(rows, "wide", 0, 0, axis_index_groups=x_groups)
        inverse = invert([touched] + received(touched))
        pieces, inverse = lax.optimization_barrier((pieces, inverse))
        return update(gebhart, inverse, response, pieces, lax.ppermute(pieces, "wide", swap))

    def spread(gebhart, change, moved_nodes, picked, table):
        own = [picked[0]] + [lax.ppermute(picked[d], "wide", shift_x[d]) for d in range(1, XS)]
        other = [lax.ppermute(slots, "wide", swap) for slots in own]
        slots = plane_slots(table, own + other, zs)
        slots, token = lax.optimization_barrier((slots, table))
        partial_value = respond(token, gebhart, change)
        response = [partial_value] + received(partial_value)
        slots = lax.all_to_all(slots, "wide", 0, 0, axis_index_groups=z_groups)
        slots, response = lax.optimization_barrier((slots, response))
        rows, touched = order(table, slots.reshape(zs * PLANE, part + count))
        return finish(rows, touched, response, gebhart)

    def crowded(gebhart, change, moved_nodes, picked, table):
        partial_value = respond(table, gebhart, change)
        owner = moved_nodes // rows_local
        owner_half = lax.dynamic_slice(owner, (core * half,), (half,))
        owner_core = owner_half % CORES
        owner_x = (owner_half // CORES) % XS
        owner_z = lax.dynamic_slice(owner_half // (CORES * XS), (z * group,), (group,))

        keep, send = pick_all(gebhart, moved_nodes, half, width)
        got = lax.ppermute(send, "wide", swap)
        positions = me * rows_local + lax.broadcasted_iota(jnp.int32, (count, rows_local), 1)
        select = (moved_nodes[:, None] == positions).astype(jnp.float32)
        terms = jnp.dot(select, partial_value, preferred_element_type=jnp.float32, precision=HIGHEST)
        terms_mine = lax.dynamic_slice(terms, (core * half, 0), (half, count))
        terms_theirs = lax.dynamic_slice(terms, ((1 - core) * half, 0), (half, count))
        terms_chip = terms_mine + lax.ppermute(terms_theirs, "wide", swap)

        rows_chip = jnp.where((owner_core == core)[None, :, None], keep, got)
        both = jnp.concatenate([rows_chip, jnp.broadcast_to(terms_chip[None], (XS, half, count))], axis=2)
        both = lax.all_to_all(both, "wide", 0, 0, axis_index_groups=x_groups)
        chosen = owner_x[None, :, None] == lax.broadcasted_iota(jnp.int32, (XS, 1, 1), 0)
        both = jnp.sum(jnp.where(chosen, both, 0.0), axis=0)

        both = lax.all_to_all(both.reshape(zs, group, width + count), "wide", 0, 0, axis_index_groups=z_groups)
        chosen = owner_z[None, :, None] == lax.broadcasted_iota(jnp.int32, (zs, 1, 1), 0)
        both = jnp.sum(jnp.where(chosen, both, 0.0), axis=0)
        both = lax.all_to_all(jnp.broadcast_to(both[None], (zs,) + both.shape), "wide", 0, 0, axis_index_groups=z_groups)
        both = both.reshape(half, width + count)

        mine = jnp.concatenate([lax.dynamic_slice(both, (0, core * part), (half, part)), both[:, width:]], axis=1)
        theirs = jnp.concatenate([lax.dynamic_slice(both, (0, (1 - core) * part), (half, part)), both[:, width:]], axis=1)
        theirs = lax.ppermute(theirs, "wide", swap)
        both = jnp.where(core == 0, jnp.concatenate([mine, theirs]), jnp.concatenate([theirs, mine]))
        rows = jnp.broadcast_to(both[None, :, :part], (XS, count, part))
        return finish(rows, both[:, part:], [partial_value] + received(partial_value), gebhart)

    return lax.cond(table[2, 0] == 1, spread, crowded, gebhart, change, moved_nodes, picked, table)


def solution(mesh):
    return jax.shard_map(
        functools.partial(body, mesh.shape["wide"], mesh.shape["narrow"]),
        mesh=mesh,
        in_specs=(P("wide", "narrow"), P("narrow", None), P()),
        out_specs=P("wide", "narrow"),
        check_vma=False,
    )
```

time: 80.3 us -> 74.4 us (0.927)
  blocking collectives: 17.3 us -> 0 us
  starting transfers between devices: 21 us -> 31.1 us
  Pallas kernels: 20.2 us -> 22.2 us
  waiting for transfers between devices: 19.7 us -> 18.5 us
    all_to_all x2 -> x0, blocking collectives: 17.3 us -> none  [the longest x1 9.5 us: body(): inverse, kept = invert(lax.all_to_all(touched, 'narrow', 0, 0), gebhart)]
    ppermute x3 -> x6, waiting for transfers between devices: 0.01 us -> 13 us  [received(): return [lax.ppermute(value, 'narrow', shift_y[d]) for d in range(1, narrow)]]
    all_to_all x1, waiting for transfers between devices: 17 us -> 4.57 us  [spread(): slots = lax.all_to_all(slots, 'wide', 0, 0, axis_index_groups=z_groups)]
    all_to_all x0 -> x1, starting transfers between devices: none -> 4.74 us  [finish(): pieces = lax.all_to_all(rows, 'wide', 0, 0, axis_index_groups=x_groups)]
    ppermute x3 -> x6, starting transfers between devices: 3.78 us -> 7.61 us  [received(): return [lax.ppermute(value, 'narrow', shift_y[d]) for d in range(1, narrow)]]
    ppermute x8, starting transfers between devices: 9.08 us -> 11.5 us  [the longest x4 4.96 us: spread(): other = [lax.ppermute(slots, 'wide', swap) for slots in own]]
    pallas_call x4 -> x6, Pallas kernels: 18.7 us -> 20.7 us  [the longest x1 7.16 us: invert(): pl.pallas_call(invert_kernel, out_shape=jax.ShapeDtypeStruct(parts[0].sha...]
    ppermute x8, waiting for transfers between devices: 2.69 us -> 0.95 us  [the longest x4 0.86 us: spread(): other = [lax.ppermute(slots, 'wide', swap) for slots in own]]
  transfers between devices with their start and end apart: 12 -> 16, of which waited for: 6 -> 9; matrix products, arithmetic and copies ran while one was open for 0% -> 0% of each run, Pallas kernels for 12% -> 19%
where the time goes in v4:
time: 74.4 us; the launch traced here: 73.8 us
  starting transfers between devices  31.1 us (42%)
  Pallas kernels  22.2 us (30%)
  waiting for transfers between devices  18.5 us (25%)
  between operations  0.9 us (1%)
    ppermute x6, waiting for transfers between devices, received(): return [lax.ppermute(value, 'narrow', shift_y[d]) for d in range(1, narrow)]  13 us
    ppermute x6, starting transfers between devices, received(): return [lax.ppermute(value, 'narrow', shift_y[d]) for d in range(1, narrow)]  7.61 us
    all_to_all x1, starting transfers between devices, spread(): slots = lax.all_to_all(slots, 'wide', 0, 0, axis_index_groups=z_groups)  7.2 us
    pallas_call x1, Pallas kernels, invert(): pl.pallas_call(invert_kernel, out_shape=jax.ShapeDtypeStruct(parts[0].sha...  7.16 us
    ppermute x4, starting transfers between devices, spread(): other = [lax.ppermute(slots, 'wide', swap) for slots in own]  4.96 us
    all_to_all x1, starting transfers between devices, finish(): pieces = lax.all_to_all(rows, 'wide', 0, 0, axis_index_groups=x_groups)  4.74 us
    all_to_all x1, waiting for transfers between devices, spread(): slots = lax.all_to_all(slots, 'wide', 0, 0, axis_index_groups=z_groups)  4.57 us
    ppermute x3, starting transfers between devices, spread(): lax.ppermute(picked[d], 'wide', shift_x[d])  3.99 us
  transfers between devices with their start and end apart: 16, of which 9 were waited for; matrix products, arithmetic and copies ran while one was open for 0% of the time, Pallas kernels for 19%

profile of v4, /device:TPU:3, one launch (start us, length us, event | category | flops | bytes accessed | tf_op | source)
XLA Modules:
  0.0 73.8 jit_solution(6376396803910996770)
XLA Ops:
  0.0 0.0 copy-start
  0.0 0.0 copy-start.2
  0.0 3.1 %pick_slots.1 = (f32[8,1152]{1,0:T(8,128)S(1)}, f32[8,1152]{1,0:T(8,128)S(1)}, f32[8,1152]{1,0:T(8,128)S(1)}, f32[8,1152]{1,0:T(8,128)S(1)}, s32[8,128]{1,0:T(8,128)S(1)}) custom-call(s32[1,128]{1,0:T(1,128)} %bitcast.9, f32[256,4096]{1,0:T(8,128)} %g_ref.1, f32[4096,128]{1,0:T(8,128)} %change_ref.1), custom_call_target="tpu_custom_call" | custom-call | tf_op jit(solution)/shard_map/pick_slots/pallas_call | solution.py:92
  3.2 0.5 slice.13
  4.3 0.0 copy-done
  4.3 0.0 copy-done.2
  4.3 69.2 %conditional.1 = (f32[256,4096]{1,0:T(8,128)}) conditional(s32[]{:T(128)} %bitcast.4, (s32[]{:T(128)}, s32[]{:T(128)}, s32[128]{0:T(128)S(1)}, f32[256,4096]{1,0:T(8,128)}, s32[8,128]{1,0:T(8,128)S(1)}, /*index=5*/f32[4096,128]{1,0:T(8,128)S(1)}, ()) %tuple.39, (f32[8,1152]{1,0:T(8,128)S(1)}, f32[8,1152]{1,0:T(8,128)S(1)}, f32[8,1152]{1,0:T(8,128)S(1)}, ...), branch_computations={%region_0.3_spmd, %region_3.4_spmd} | conditional | flops 3852039680 | bytes 57896212 | solution.py:525
  4.6 1.3 %collective-permute-start = (f32[8,1152]{1,0:T(8,128)S(1)}, f32[8,1152]{1,0:T(8,128)S(1)}, u32[]{:S(2)}, u32[]{:S(2)}) collective-permute-start(f32[8,1152]{1,0:T(8,128)S(1)} %get-tuple-element.95), channel_id=1, source_target_pairs={{0,8},{4,12},{8,16},{12,20},{16,24},{20,28},{24,0},{28,4},{32,40},... | collective-permute-start | bytes 110600 | tf_op jit(solution)/shard_map/cond/branch_1_fun/ppermute | solution.py:478
  5.9 0.7 collective-permute-start.1
  6.6 2.0 %collective-permute-start.2 = (f32[8,1152]{1,0:T(8,128)S(1)}, f32[8,1152]{1,0:T(8,128)S(1)}, u32[]{:S(2)}, u32[]{:S(2)}) collective-permute-start(f32[8,1152]{1,0:T(8,128)S(1)} %get-tuple-element.97), channel_id=1, source_target_pairs={{0,24},{4,28},{8,0},{12,4},{16,8},{20,12},{24,16},{28,20},{32,56},... | collective-permute-start | bytes 110600 | tf_op jit(solution)/shard_map/cond/branch_1_fun/ppermute | solution.py:478
  8.6 1.5 %collective-permute-start.3 = (f32[8,1152]{1,0:T(8,128)S(1)}, f32[8,1152]{1,0:T(8,128)S(1)}, u32[]{:S(2)}, u32[]{:S(2)}) collective-permute-start(f32[8,1152]{1,0:T(8,128)S(1)} %get-tuple-element.94.refs_0_), channel_id=1, source_target_pairs={{0,4},{4,0},{8,12},{12,8},{16,20},{20,16},{24,28},{28,24},{32,36},... | collective-permute-start | bytes 110600 | tf_op jit(solution)/shard_map/cond/branch_1_fun/ppermute | solution.py:479
  10.1 0.0 collective-permute-done.refs_1_
  10.1 0.0 collective-permute-start.4
  10.1 0.1 collective-permute-done.1.refs_2_
  10.2 2.1 %collective-permute-start.5 = (f32[8,1152]{1,0:T(8,128)S(1)}, f32[8,1152]{1,0:T(8,128)S(1)}, u32[]{:S(2)}, u32[]{:S(2)}) collective-permute-start(f32[8,1152]{1,0:T(8,128)S(1)} %collective-permute-done.1.refs_2_), channel_id=1, source_target_pairs={{0,4},{4,0},{8,12},{12,8},{16,20},{20,16},{24,28},{28,24},{32,36},... | collective-permute-start | bytes 110600 | tf_op jit(solution)/shard_map/cond/branch_1_fun/ppermute | solution.py:479
  12.3 0.0 collective-permute-done.2.refs_3_
  12.3 1.3 %collective-permute-start.6 = (f32[8,1152]{1,0:T(8,128)S(1)}, f32[8,1152]{1,0:T(8,128)S(1)}, u32[]{:S(2)}, u32[]{:S(2)}) collective-permute-start(f32[8,1152]{1,0:T(8,128)S(1)} %collective-permute-done.2.refs_3_), channel_id=1, source_target_pairs={{0,4},{4,0},{8,12},{12,8},{16,20},{20,16},{24,28},{28,24},{32,36},... | collective-permute-start | bytes 110600 | tf_op jit(solution)/shard_map/cond/branch_1_fun/ppermute | solution.py:479
  13.6 0.0 collective-permute-done.3.refs_4_
  13.6 0.0 collective-permute-done.4.refs_5_
  13.6 0.0 collective-permute-done.5.refs_6_
  13.6 0.9 %collective-permute-done.6.refs_7_ = f32[8,1152]{1,0:T(8,128)S(1)} collective-permute-done((f32[8,1152]{1,0:T(8,128)S(1)}, f32[8,1152]{1,0:T(8,128)S(1)}, u32[]{:S(2)}, u32[]{:S(2)}) %collective-permute-start.6) | collective-permute-done | bytes 36896 | tf_op jit(solution)/shard_map/cond/branch_1_fun/ppermute | solution.py:479
  14.5 1.5 %plane_slots.1 = f32[8,32,640]{2,1,0:T(8,128)} custom-call(s32[8,128]{1,0:T(8,128)S(1)} %get-tuple-element.99.table_ref.token_ref, f32[8,1152]{1,0:T(8,128)S(1)} %get-tuple-element.94.refs_0_, f32[8,1152]{1,0:T(8,128)S(1)} %collective-permute-done.refs_1_, f32[8,1152]{1,0:T(8,128)S(1)} %collective-permute-done.1.refs_2_, ...), custom_call_target="tpu_custom_call" | custom-call | tf_op jit(solution)/shard_map/cond/branch_1_fun/plane_slots/pallas_call | solution.py:182
  16.0 7.2 %all-to-all-start = ((f32[8,32,640]{2,1,0:T(8,128)}), f32[8,32,640]{2,1,0:T(8,128)S(1)}, u32[]{:S(2)}, u32[]{:S(2)}) async-start(f32[8,32,640]{2,1,0:T(8,128)} %plane_slots.1), calls=%async_computation | async-start | bytes 1310720 | tf_op jit(solution)/shard_map/cond/branch_1_fun/all_to_all | solution.py:484
  23.2 3.7 %respond.3.refs_0_ = f32[256,128]{1,0:T(8,128)S(1)} custom-call(s32[8,128]{1,0:T(8,128)S(1)} %get-tuple-element.99.table_ref.token_ref, f32[256,4096]{1,0:T(8,128)} %get-tuple-element.100.g_ref, f32[4096,128]{1,0:T(8,128)S(1)} %get-tuple-element.101.change_ref), custom_call_target="tpu_custom_call" | custom-call | flops 800000000 | bytes 8000000 | tf_op jit(solution)/shard_map/cond/branch_1_fun/respond/pallas_call | solution.py:142
  26.9 2.8 %collective-permute-start.9 = (f32[256,128]{1,0:T(8,128)S(1)}, f32[256,128]{1,0:T(8,128)S(1)}, u32[]{:S(2)}, u32[]{:S(2)}) collective-permute-start(f32[256,128]{1,0:T(8,128)S(1)} %respond.3.refs_0_), channel_id=1, source_target_pairs={{0,3},{1,0},{2,1},{3,2},{4,7},{5,4},{6,5},{7,6},{8,11},{9,8},{10,9... | collective-permute-start | bytes 393224 | tf_op jit(solution)/shard_map/cond/branch_1_fun/ppermute | solution.py:469
  29.7 0.4 collective-permute-start.8
  30.1 0.7 collective-permute-start.7
  30.8 4.1 %collective-permute-done.9.refs_3_ = f32[256,128]{1,0:T(8,128)S(1)} collective-permute-done((f32[256,128]{1,0:T(8,128)S(1)}, f32[256,128]{1,0:T(8,128)S(1)}, u32[]{:S(2)}, u32[]{:S(2)}) %collective-permute-start.9) | collective-permute-done | bytes 131104 | tf_op jit(solution)/shard_map/cond/branch_1_fun/ppermute | solution.py:469
  34.9 0.7 collective-permute-done.8.refs_2_
  35.5 3.9 %collective-permute-done.7.refs_1_ = f32[256,128]{1,0:T(8,128)S(1)} collective-permute-done((f32[256,128]{1,0:T(8,128)S(1)}, f32[256,128]{1,0:T(8,128)S(1)}, u32[]{:S(2)}, u32[]{:S(2)}) %collective-permute-start.7) | collective-permute-done | bytes 131104 | tf_op jit(solution)/shard_map/cond/branch_1_fun/ppermute | solution.py:469
  39.4 4.6 %all-to-all-done = f32[8,32,640]{2,1,0:T(8,128)S(1)} async-done(((f32[8,32,640]{2,1,0:T(8,128)}), f32[8,32,640]{2,1,0:T(8,128)S(1)}, u32[]{:S(2)}, u32[]{:S(2)}) %all-to-all-start) | async-done | bytes 655392 | tf_op jit(solution)/shard_map/cond/branch_1_fun/all_to_all | solution.py:484
  44.0 1.8 %order_rows.1 = (f32[4,128,512]{2,1,0:T(8,128)}, f32[128,128]{1,0:T(8,128)S(1)}) custom-call(s32[8,128]{1,0:T(8,128)S(1)} %get-tuple-element.99.table_ref.token_ref, f32[256,640]{1,0:T(8,128)S(1)} %bitcast.6), custom_call_target="tpu_custom_call" | custom-call | tf_op jit(solution)/shard_map/cond/branch_1_fun/order_rows/pallas_call | solution.py:208
  45.8 4.7 %all-to-all-start.1 = ((f32[4,128,512]{2,1,0:T(8,128)}), f32[4,128,512]{2,1,0:T(8,128)S(1)}, u32[]{:S(2)}, u32[]{:S(2)}) async-start(f32[4,128,512]{2,1,0:T(8,128)} %get-tuple-element.103), calls=%async_computation.1 | async-start | bytes 2097152 | tf_op jit(solution)/shard_map/cond/branch_1_fun/all_to_all | solution.py:472
  50.6 2.7 %collective-permute-start.12 = (f32[128,128]{1,0:T(8,128)S(1)}, f32[128,128]{1,0:T(8,128)S(1)}, u32[]{:S(2)}, u32[]{:S(2)}) collective-permute-start(f32[128,128]{1,0:T(8,128)S(1)} %get-tuple-element.104.refs_0_), channel_id=1, source_target_pairs={{0,3},{1,0},{2,1},{3,2},{4,7},{5,4},{6,5},{7,6},{8,11},{9,8},{10,9... | collective-permute-start | bytes 196616 | tf_op jit(solution)/shard_map/cond/branch_1_fun/ppermute | solution.py:469
  53.3 0.3 collective-permute-start.11
  53.7 0.7 collective-permute-start.10
  54.4 0.3 collective-permute-done.12.refs_3_
  54.7 3.4 %collective-permute-done.11.refs_2_ = f32[128,128]{1,0:T(8,128)S(1)} collective-permute-done((f32[128,128]{1,0:T(8,128)S(1)}, f32[128,128]{1,0:T(8,128)S(1)}, u32[]{:S(2)}, u32[]{:S(2)}) %collective-permute-start.11) | collective-permute-done | bytes 65568 | tf_op jit(solution)/shard_map/cond/branch_1_fun/ppermute | solution.py:469
  58.0 0.6 collective-permute-done.10.refs_1_
  58.6 7.2 %invert_capacitance.3.inverse_ref = f32[128,128]{1,0:T(8,128)S(1)} custom-call(f32[128,128]{1,0:T(8,128)S(1)} %get-tuple-element.104.refs_0_, f32[128,128]{1,0:T(8,128)S(1)} %collective-permute-done.10.refs_1_, f32[128,128]{1,0:T(8,128)S(1)} %collective-permute-done.11.refs_2_, f32[128,128]{1,0:T(8,128)S(1)} %collective-permute-done.12.refs_3_), custom_call_target="tpu_custom_call" | custom-call | flops 2000000000 | bytes 8000000 | tf_op jit(solution)/shard_map/cond/branch_1_fun/invert_capacitance/pallas_call | solution.py:353
  65.8 0.0 all-to-all-done.1.pieces_ref
  65.8 2.6 %collective-permute-start.13 = (f32[4,128,512]{2,1,0:T(8,128)S(1)}, f32[4,128,512]{2,1,0:T(8,128)S(1)}, u32[]{:S(2)}, u32[]{:S(2)}) collective-permute-start(f32[4,128,512]{2,1,0:T(8,128)S(1)} %all-to-all-done.1.pieces_ref), channel_id=1, source_target_pairs={{0,4},{4,0},{8,12},{12,8},{16,20},{20,16},{24,28},{28,24},{32,36},... | collective-permute-start | bytes 3145736 | tf_op jit(solution)/shard_map/cond/branch_1_fun/ppermute | solution.py:475
  68.4 3.2 %update_own.3 = (f32[256,4096]{1,0:T(8,128)}, bf16[256,384]{1,0:T(8,128)(2,1)S(1)}, f32[4,256,512]{2,1,0:T(8,128)S(1)}) custom-call(f32[128,128]{1,0:T(8,128)S(1)} %invert_capacitance.3.inverse_ref, f32[256,4096]{1,0:T(8,128)} %get-tuple-element.100.g_ref, f32[4,128,512]{2,1,0:T(8,128)S(1)} %all-to-all-done.1.pieces_ref, f32[256,128]{1,0:T(8,128)S(1)} %respond.3.refs_0_, ...), custom_call_target="tpu_custom_call" | custom-call | flops 1000000000 | bytes 6000000 | tf_op jit(solution)/shard_map/cond/branch_1_fun/update_own/pallas_call | solution.py:421
  71.6 0.0 collective-permute-done.13.pieces_ref
  71.6 1.7 %update_other.3 = f32[256,4096]{1,0:T(8,128)} custom-call(bf16[256,384]{1,0:T(8,128)(2,1)S(1)} %get-tuple-element.111.left_ref, f32[4,256,512]{2,1,0:T(8,128)S(1)} %get-tuple-element.112.blocks_ref, f32[4,128,512]{2,1,0:T(8,128)S(1)} %collective-permute-done.13.pieces_ref, f32[256,4096]{1,0:T(8,128)} %get-tuple-element.113.before_ref), custom_call_target="tpu_custom_call", output_to_operand_aliasing={{}: (3, {})} | custom-call | tf_op jit(solution)/shard_map/cond/branch_1_fun/update_other/pallas_call | solution.py:431
Async XLA Ops:
  0.0 4.3 %copy-start = (f32[4096,128]{1,0:T(8,128)S(1)}, f32[4096,128]{1,0:T(8,128)}, u32[]{:S(2)}) copy-start(f32[4096,128]{1,0:T(8,128)} %change_ref.1) | copy-start | bytes 6291460
  0.0 4.3 %copy-start.2 = (s32[128]{0:T(128)S(1)}, s32[128]{0:T(128)}, u32[]{:S(2)}) copy-start(s32[128]{0:T(128)} %param.7) | copy-start | bytes 1540
  4.6 5.5 %collective-permute-start = (f32[8,1152]{1,0:T(8,128)S(1)}, f32[8,1152]{1,0:T(8,128)S(1)}, u32[]{:S(2)}, u32[]{:S(2)}) collective-permute-start(f32[8,1152]{1,0:T(8,128)S(1)} %get-tuple-element.95), channel_id=1, source_target_pairs={{0,8},{4,12},{8,16},{12,20},{16,24},{20,28},{24,0},{28,4},{32,40},... | collective-permute-start | bytes 110600 | tf_op jit(solution)/shard_map/cond/branch_1_fun/ppermute | solution.py:478
  5.9 4.3 %collective-permute-start.1 = (f32[8,1152]{1,0:T(8,128)S(1)}, f32[8,1152]{1,0:T(8,128)S(1)}, u32[]{:S(2)}, u32[]{:S(2)}) collective-permute-start(f32[8,1152]{1,0:T(8,128)S(1)} %get-tuple-element.96), channel_id=1, source_target_pairs={{0,16},{4,20},{8,24},{12,28},{16,0},{20,4},{24,8},{28,12},{32,48},... | collective-permute-start | bytes 110600 | tf_op jit(solution)/shard_map/cond/branch_1_fun/ppermute | solution.py:478
  6.6 5.7 %collective-permute-start.2 = (f32[8,1152]{1,0:T(8,128)S(1)}, f32[8,1152]{1,0:T(8,128)S(1)}, u32[]{:S(2)}, u32[]{:S(2)}) collective-permute-start(f32[8,1152]{1,0:T(8,128)S(1)} %get-tuple-element.97), channel_id=1, source_target_pairs={{0,24},{4,28},{8,0},{12,4},{16,8},{20,12},{24,16},{28,20},{32,56},... | collective-permute-start | bytes 110600 | tf_op jit(solution)/shard_map/cond/branch_1_fun/ppermute | solution.py:478
  8.6 5.1 %collective-permute-start.3 = (f32[8,1152]{1,0:T(8,128)S(1)}, f32[8,1152]{1,0:T(8,128)S(1)}, u32[]{:S(2)}, u32[]{:S(2)}) collective-permute-start(f32[8,1152]{1,0:T(8,128)S(1)} %get-tuple-element.94.refs_0_), channel_id=1, source_target_pairs={{0,4},{4,0},{8,12},{12,8},{16,20},{20,16},{24,28},{28,24},{32,36},... | collective-permute-start | bytes 110600 | tf_op jit(solution)/shard_map/cond/branch_1_fun/ppermute | solution.py:479
  10.1 3.5 %collective-permute-start.4 = (f32[8,1152]{1,0:T(8,128)S(1)}, f32[8,1152]{1,0:T(8,128)S(1)}, u32[]{:S(2)}, u32[]{:S(2)}) collective-permute-start(f32[8,1152]{1,0:T(8,128)S(1)} %collective-permute-done.refs_1_), channel_id=1, source_target_pairs={{0,4},{4,0},{8,12},{12,8},{16,20},{20,16},{24,28},{28,24},{32,36},... | collective-permute-start | bytes 110600 | tf_op jit(solution)/shard_map/cond/branch_1_fun/ppermute | solution.py:479
  10.2 3.5 %collective-permute-start.5 = (f32[8,1152]{1,0:T(8,128)S(1)}, f32[8,1152]{1,0:T(8,128)S(1)}, u32[]{:S(2)}, u32[]{:S(2)}) collective-permute-start(f32[8,1152]{1,0:T(8,128)S(1)} %collective-permute-done.1.refs_2_), channel_id=1, source_target_pairs={{0,4},{4,0},{8,12},{12,8},{16,20},{20,16},{24,28},{28,24},{32,36},... | collective-permute-start | bytes 110600 | tf_op jit(solution)/shard_map/cond/branch_1_fun/ppermute | solution.py:479
  12.3 2.2 %collective-permute-start.6 = (f32[8,1152]{1,0:T(8,128)S(1)}, f32[8,1152]{1,0:T(8,128)S(1)}, u32[]{:S(2)}, u32[]{:S(2)}) collective-permute-start(f32[8,1152]{1,0:T(8,128)S(1)} %collective-permute-done.2.refs_3_), channel_id=1, source_target_pairs={{0,4},{4,0},{8,12},{12,8},{16,20},{20,16},{24,28},{28,24},{32,36},... | collective-permute-start | bytes 110600 | tf_op jit(solution)/shard_map/cond/branch_1_fun/ppermute | solution.py:479
  16.0 28.0 %all-to-all-start = ((f32[8,32,640]{2,1,0:T(8,128)}), f32[8,32,640]{2,1,0:T(8,128)S(1)}, u32[]{:S(2)}, u32[]{:S(2)}) async-start(f32[8,32,640]{2,1,0:T(8,128)} %plane_slots.1), calls=%async_computation | async-start | bytes 1310720 | tf_op jit(solution)/shard_map/cond/branch_1_fun/all_to_all | solution.py:484
  26.9 7.9 %collective-permute-start.9 = (f32[256,128]{1,0:T(8,128)S(1)}, f32[256,128]{1,0:T(8,128)S(1)}, u32[]{:S(2)}, u32[]{:S(2)}) collective-permute-start(f32[256,128]{1,0:T(8,128)S(1)} %respond.3.refs_0_), channel_id=1, source_target_pairs={{0,3},{1,0},{2,1},{3,2},{4,7},{5,4},{6,5},{7,6},{8,11},{9,8},{10,9... | collective-permute-start | bytes 393224 | tf_op jit(solution)/shard_map/cond/branch_1_fun/ppermute | solution.py:469
  29.7 5.8 %collective-permute-start.8 = (f32[256,128]{1,0:T(8,128)S(1)}, f32[256,128]{1,0:T(8,128)S(1)}, u32[]{:S(2)}, u32[]{:S(2)}) collective-permute-start(f32[256,128]{1,0:T(8,128)S(1)} %respond.3.refs_0_), channel_id=1, source_target_pairs={{0,2},{1,3},{2,0},{3,1},{4,6},{5,7},{6,4},{7,5},{8,10},{9,11},{10,... | collective-permute-start | bytes 393224 | tf_op jit(solution)/shard_map/cond/branch_1_fun/ppermute | solution.py:469
  30.1 9.4 %collective-permute-start.7 = (f32[256,128]{1,0:T(8,128)S(1)}, f32[256,128]{1,0:T(8,128)S(1)}, u32[]{:S(2)}, u32[]{:S(2)}) collective-permute-start(f32[256,128]{1,0:T(8,128)S(1)} %respond.3.refs_0_), channel_id=1, source_target_pairs={{0,1},{1,2},{2,3},{3,0},{4,5},{5,6},{6,7},{7,4},{8,9},{9,10},{10,1... | collective-permute-start | bytes 393224 | tf_op jit(solution)/shard_map/cond/branch_1_fun/ppermute | solution.py:469
  45.8 20.0 %all-to-all-start.1 = ((f32[4,128,512]{2,1,0:T(8,128)}), f32[4,128,512]{2,1,0:T(8,128)S(1)}, u32[]{:S(2)}, u32[]{:S(2)}) async-start(f32[4,128,512]{2,1,0:T(8,128)} %get-tuple-element.103), calls=%async_computation.1 | async-start | bytes 2097152 | tf_op jit(solution)/shard_map/cond/branch_1_fun/all_to_all | solution.py:472
  50.6 4.1 %collective-permute-start.12 = (f32[128,128]{1,0:T(8,128)S(1)}, f32[128,128]{1,0:T(8,128)S(1)}, u32[]{:S(2)}, u32[]{:S(2)}) collective-permute-start(f32[128,128]{1,0:T(8,128)S(1)} %get-tuple-element.104.refs_0_), channel_id=1, source_target_pairs={{0,3},{1,0},{2,1},{3,2},{4,7},{5,4},{6,5},{7,6},{8,11},{9,8},{10,9... | collective-permute-start | bytes 196616 | tf_op jit(solution)/shard_map/cond/branch_1_fun/ppermute | solution.py:469
  53.3 4.7 %collective-permute-start.11 = (f32[128,128]{1,0:T(8,128)S(1)}, f32[128,128]{1,0:T(8,128)S(1)}, u32[]{:S(2)}, u32[]{:S(2)}) collective-permute-start(f32[128,128]{1,0:T(8,128)S(1)} %get-tuple-element.104.refs_0_), channel_id=1, source_target_pairs={{0,2},{1,3},{2,0},{3,1},{4,6},{5,7},{6,4},{7,5},{8,10},{9,11},{10,... | collective-permute-start | bytes 196616 | tf_op jit(solution)/shard_map/cond/branch_1_fun/ppermute | solution.py:469
  53.7 5.0 %collective-permute-start.10 = (f32[128,128]{1,0:T(8,128)S(1)}, f32[128,128]{1,0:T(8,128)S(1)}, u32[]{:S(2)}, u32[]{:S(2)}) collective-permute-start(f32[128,128]{1,0:T(8,128)S(1)} %get-tuple-element.104.refs_0_), channel_id=1, source_target_pairs={{0,1},{1,2},{2,3},{3,0},{4,5},{5,6},{6,7},{7,4},{8,9},{9,10},{10,1... | collective-permute-start | bytes 196616 | tf_op jit(solution)/shard_map/cond/branch_1_fun/ppermute | solution.py:469
  65.8 5.8 %collective-permute-start.13 = (f32[4,128,512]{2,1,0:T(8,128)S(1)}, f32[4,128,512]{2,1,0:T(8,128)S(1)}, u32[]{:S(2)}, u32[]{:S(2)}) collective-permute-start(f32[4,128,512]{2,1,0:T(8,128)S(1)} %all-to-all-done.1.pieces_ref), channel_id=1, source_target_pairs={{0,4},{4,0},{8,12},{12,8},{16,20},{20,16},{24,28},{28,24},{32,36},... | collective-permute-start | bytes 3145736 | tf_op jit(solution)/shard_map/cond/branch_1_fun/ppermute | solution.py:475

commit v5 on v4

--- a/solution.py
+++ b/solution.py
@@ -10,8 +10,8 @@
 HIGHEST = lax.Precision.HIGHEST
 CORES = 2
 XS = 4
-SLOTS = 8
-PLANE = 32
+SLOTS = 16
+PLANES = (24, 32)
 
 
 def pick_kernel(lanes_ref, g_ref, change_ref, *refs):
@@ -52,7 +52,13 @@
     plane = jnp.where(plane_across == plane_down, 1.0, 0.0)
     rank = jnp.sum(jnp.where(j < i, plane, 0.0), axis=1, keepdims=True)
     rank_across = jnp.sum(jnp.where(i < j, plane, 0.0), axis=0, keepdims=True)
-    fits = jnp.where(jnp.logical_and(jnp.max(slot) < SLOTS, jnp.max(rank) < PLANE), 1, 0)
+    most = jnp.max(rank)
+    path = len(PLANES)
+    room = float(PLANES[-1])
+    for choice in reversed(range(len(PLANES))):
+        path = jnp.where(most < PLANES[choice], choice, path)
+        room = jnp.where(most < PLANES[choice], float(PLANES[choice]), room)
+    path = jnp.where(jnp.max(slot) < SLOTS, path, len(PLANES))
     inside = down - plane_down * per_plane
     x_down = jnp.floor(inside / float(CORES))
     core_down = inside - x_down * float(CORES)
@@ -62,10 +68,10 @@
     here = plane_down == (me // (CORES * XS)).astype(jnp.float32)
     match = jnp.logical_and(here, rank == j.astype(jnp.float32))
     source = jnp.sum(jnp.where(match, behind * float(SLOTS) + jnp.minimum(slot, SLOTS - 1.0) + side, 0.0), axis=0, keepdims=True)
-    target = plane_across[:1] * float(PLANE) + jnp.minimum(rank_across, PLANE - 1.0)
+    target = plane_across[:1] * room + jnp.minimum(rank_across, room - 1.0)
     table_ref[0:1, :] = target.astype(jnp.int32)
     table_ref[1:2, :] = source.astype(jnp.int32)
-    table_ref[2:8, :] = jnp.full((6, count), fits, jnp.int32)
+    table_ref[2:8, :] = jnp.full((6, count), path, jnp.int32)
 
     for i in range(chunks):
         span = pl.ds(i * block, block)
@@ -175,13 +181,13 @@
         out_ref[copy] = value
 
 
-def plane_slots(table, slots, planes):
+def plane_slots(table, slots, planes, room):
     count = table.shape[1]
     columns = (slots[0].shape[1] - count) // CORES + count
     vmem = pl.BlockSpec(memory_space=pltpu.VMEM)
     return pl.pallas_call(
         plane_kernel,
-        out_shape=jax.ShapeDtypeStruct((planes, PLANE, columns), jnp.float32),
+        out_shape=jax.ShapeDtypeStruct((planes, room, columns), jnp.float32),
         in_specs=[pl.BlockSpec(memory_space=pltpu.SMEM)] + [vmem] * len(slots),
         out_specs=vmem,
         scratch_shapes=[pltpu.VMEM((len(slots) * SLOTS, columns), jnp.float32)],
@@ -191,14 +197,15 @@
 
 
 def order_kernel(table_ref, slots_ref, rows_ref, touched_ref):
-    copies, count, part = rows_ref.shape
-    for k in range(count):
+    count, part = rows_ref.shape
+
+    def move(k, carry):
         row = slots_ref[pl.ds(table_ref[0, k], 1), :]
-        rows_ref[0, k:k + 1, :] = row[:, :part]
-        touched_ref[k:k + 1, :] = row[:, part:]
-    rows = rows_ref[0]
-    for copy in range(1, copies):
-        rows_ref[copy] = rows
+        rows_ref[pl.ds(k, 1), :] = row[:, :part]
+        touched_ref[pl.ds(k, 1), :] = row[:, part:]
+        return carry
+
+    lax.fori_loop(0, count, move, 0, unroll=8)
 
 
 def order(table, slots):
@@ -207,7 +214,7 @@
     vmem = pl.BlockSpec(memory_space=pltpu.VMEM)
     return pl.pallas_call(
         order_kernel,
-        out_shape=(jax.ShapeDtypeStruct((XS, count, part), jnp.float32), jax.ShapeDtypeStruct((count, count), jnp.float32)),
+        out_shape=(jax.ShapeDtypeStruct((count, part), jnp.float32), jax.ShapeDtypeStruct((count, count), jnp.float32)),
         in_specs=[pl.BlockSpec(memory_space=pltpu.SMEM), vmem],
         out_specs=(vmem, vmem),
         compiler_params=pltpu.CompilerParams(vmem_limit_bytes=16 * 1024 * 1024),
@@ -362,38 +369,26 @@
 
 
 def places(core, part):
-    return [pl.ds(pl.multiple_of((q * CORES + core) * part, part), part) for q in range(XS)]
-
-
-def write_blocks(left, blocks, ready, pieces_ref, out_ref, buffer_ref, sem, core):
+    x = (lax.axis_index("wide") // CORES) % XS
+    return [pl.ds(pl.multiple_of((lax.rem(x + (XS - d), XS) * CORES + core) * part, part), part) for d in range(XS)]
+
+
+def write_blocks(left, g_ref, pieces, out_ref, buffer_ref, sem, core):
     copies = []
-    for q, here in enumerate(places(core, pieces_ref.shape[2])):
-        r_high, r_low = split(pieces_ref[q])
+    for d, here in enumerate(places(core, pieces[0].shape[1])):
+        r_high, r_low = split(pieces[d][...])
         right = jnp.concatenate([r_high, r_high, r_low], axis=0)
-        change = jnp.dot(left, right, preferred_element_type=jnp.float32)
-        if ready is not None:
-            ready[q].wait()
-        buffer_ref[q] = blocks[q] + change
-        copies.append(pltpu.make_async_copy(buffer_ref.at[q], out_ref.at[:, here], sem.at[q]))
-        copies[q].start()
+        buffer_ref[d] = g_ref[:, here] + jnp.dot(left, right, preferred_element_type=jnp.float32)
+        copies.append(pltpu.make_async_copy(buffer_ref.at[d], out_ref.at[:, here], sem.at[d]))
+        copies[d].start()
     for copy in copies:
         copy.wait()
 
 
-def update_own_kernel(inverse_ref, g_ref, pieces_ref, *refs):
-    out_ref, left_ref, other_ref, own_ref, buffer_ref, own_sem, other_sem, sem = refs[-8:]
-    core = lax.axis_index("wide") % CORES
-    part = pieces_ref.shape[2]
-    ready = []
-    for q, here in enumerate(places(core, part)):
-        ready.append(pltpu.make_async_copy(g_ref.at[:, here], own_ref.at[q], own_sem.at[q]))
-        ready[q].start()
-    later = []
-    for q, here in enumerate(places(1 - core, part)):
-        later.append(pltpu.make_async_copy(g_ref.at[:, here], other_ref.at[q], other_sem.at[q]))
-        later[q].start()
-    response = refs[0][...]
-    for ref in refs[1:-8]:
+def update_own_kernel(inverse_ref, g_ref, *refs):
+    pieces, response_refs, (out_ref, left_ref, buffer_ref, sem) = refs[:XS], refs[XS:-4], refs[-4:]
+    response = response_refs[0][...]
+    for ref in response_refs[1:]:
         response = response + ref[...]
     solved = lax.dot_general(
         response, inverse_ref[...], (((1,), (1,)), ((), ())), precision=HIGHEST, preferred_element_type=jnp.float32
@@ -401,43 +396,42 @@
     s_high, s_low = split(solved)
     left = jnp.concatenate([s_high, s_low, s_high], axis=1)
     left_ref[...] = left
-    write_blocks(left, own_ref, ready, pieces_ref, out_ref, buffer_ref, sem, core)
-    for copy in later:
-        copy.wait()
-
-
-def update_other_kernel(left_ref, blocks_ref, pieces_ref, before_ref, out_ref, buffer_ref, sem):
-    write_blocks(left_ref[...], blocks_ref, None, pieces_ref, out_ref, buffer_ref, sem, 1 - lax.axis_index("wide") % CORES)
+    write_blocks(left, g_ref, pieces, out_ref, buffer_ref, sem, lax.axis_index("wide") % CORES)
+
+
+def update_other_kernel(left_ref, g_ref, before_ref, *refs):
+    pieces, (out_ref, buffer_ref, sem) = refs[:XS], refs[XS:]
+    write_blocks(left_ref[...], g_ref, pieces, out_ref, buffer_ref, sem, 1 - lax.axis_index("wide") % CORES)
 
 
 def update(gebhart, inverse, response, pieces, swapped):
     rows, nodes = gebhart.shape
-    count, part = pieces.shape[1:]
+    count, part = pieces[0].shape
     vmem = pl.BlockSpec(memory_space=pltpu.VMEM)
     hbm = pl.BlockSpec(memory_space=pl.ANY)
     whole = jax.ShapeDtypeStruct((rows, nodes), jnp.float32)
-    blocks = pltpu.VMEM((XS, rows, part), jnp.float32)
-    sems = pltpu.SemaphoreType.DMA((XS,))
-    own, left, other = pl.pallas_call(
+    scratch = [pltpu.VMEM((XS, rows, part), jnp.float32), pltpu.SemaphoreType.DMA((XS,))]
+    params = pltpu.CompilerParams(vmem_limit_bytes=16 * 1024 * 1024)
+    own, left = pl.pallas_call(
         update_own_kernel,
-        out_shape=(whole, jax.ShapeDtypeStruct((rows, 3 * count), jnp.bfloat16), blocks),
-        in_specs=[vmem, hbm] + [vmem] * (1 + len(response)),
-        out_specs=(hbm, vmem, vmem),
-        scratch_shapes=[blocks, blocks, sems, sems, sems],
+        out_shape=(whole, jax.ShapeDtypeStruct((rows, 3 * count), jnp.bfloat16)),
+        in_specs=[vmem] * (2 + XS + len(response)),
+        out_specs=(hbm, vmem),
+        scratch_shapes=scratch,
         cost_estimate=pl.CostEstimate(flops=1_000_000_000, bytes_accessed=6_000_000, transcendentals=0),
-        compiler_params=pltpu.CompilerParams(vmem_limit_bytes=20 * 1024 * 1024),
+        compiler_params=params,
         name="update_own",
-    )(inverse, gebhart, pieces, *response)
+    )(inverse, gebhart, *pieces, *response)
     return pl.pallas_call(
         update_other_kernel,
         out_shape=whole,
-        in_specs=[vmem, vmem, vmem, hbm],
+        in_specs=[vmem, vmem, hbm] + [vmem] * XS,
         out_specs=hbm,
-        scratch_shapes=[blocks, sems],
-        input_output_aliases={3: 0},
-        compiler_params=pltpu.CompilerParams(vmem_limit_bytes=20 * 1024 * 1024),
+        scratch_shapes=scratch,
+        input_output_aliases={2: 0},
+        compiler_params=params,
         name="update_other",
-    )(left, other, swapped, own)
+    )(left, gebhart, own, *swapped)
 
 
 def body(wide, narrow, gebhart, change, moved_nodes):
@@ -468,25 +462,19 @@
     def received(value):
         return [lax.ppermute(value, "narrow", shift_y[d]) for d in range(1, narrow)]
 
-    def finish(rows, touched, response, gebhart):
-        pieces = lax.all_to_all(rows, "wide", 0, 0, axis_index_groups=x_groups)
-        inverse = invert([touched] + received(touched))
-        pieces, inverse = lax.optimization_barrier((pieces, inverse))
-        return update(gebhart, inverse, response, pieces, lax.ppermute(pieces, "wide", swap))
-
-    def spread(gebhart, change, moved_nodes, picked, table):
-        own = [picked[0]] + [lax.ppermute(picked[d], "wide", shift_x[d]) for d in range(1, XS)]
-        other = [lax.ppermute(slots, "wide", swap) for slots in own]
-        slots = plane_slots(table, own + other, zs)
+    own = [picked[0]] + [lax.ppermute(picked[d], "wide", shift_x[d]) for d in range(1, XS)]
+    other = [lax.ppermute(slots, "wide", swap) for slots in own]
+
+    def spread(room, gebhart, change, moved_nodes, slots, table):
+        slots = plane_slots(table, slots, zs, room)
         slots, token = lax.optimization_barrier((slots, table))
         partial_value = respond(token, gebhart, change)
         response = [partial_value] + received(partial_value)
         slots = lax.all_to_all(slots, "wide", 0, 0, axis_index_groups=z_groups)
         slots, response = lax.optimization_barrier((slots, response))
-        rows, touched = order(table, slots.reshape(zs * PLANE, part + count))
-        return finish(rows, touched, response, gebhart)
-
-    def crowded(gebhart, change, moved_nodes, picked, table):
+        return tuple(order(table, slots.reshape(zs * room, part + count))) + tuple(response)
+
+    def crowded(gebhart, change, moved_nodes, slots, table):
         partial_value = respond(table, gebhart, change)
         owner = moved_nodes // rows_local
         owner_half = lax.dynamic_slice(owner, (core * half,), (half,))
@@ -519,10 +507,15 @@
         theirs = jnp.concatenate([lax.dynamic_slice(both, (0, (1 - core) * part), (half, part)), both[:, width:]], axis=1)
         theirs = lax.ppermute(theirs, "wide", swap)
         both = jnp.where(core == 0, jnp.concatenate([mine, theirs]), jnp.concatenate([theirs, mine]))
-        rows = jnp.broadcast_to(both[None, :, :part], (XS, count, part))
-        return finish(rows, both[:, part:], [partial_value] + received(partial_value), gebhart)
-
-    return lax.cond(table[2, 0] == 1, spread, crowded, gebhart, change, moved_nodes, picked, table)
+        return (both[:, :part], both[:, part:], partial_value) + tuple(received(partial_value))
+
+    paths = [functools.partial(spread, room) for room in PLANES] + [crowded]
+    rows, touched, *response = lax.switch(table[2, 0], paths, gebhart, change, moved_nodes, own + other, table)
+
+    pieces = [rows] + [lax.ppermute(rows, "wide", shift_x[d]) for d in range(1, XS)]
+    inverse = invert([touched] + received(touched))
+    pieces, inverse = lax.optimization_barrier((pieces, inverse))
+    return update(gebhart, inverse, response, pieces, [lax.ppermute(piece, "wide", swap) for piece in pieces])
 
 
 def solution(mesh):

time: 74.4 us -> 71.2 us (0.957)
  waiting for transfers between devices: 18.5 us -> 13.9 us
  starting transfers between devices: 31.1 us -> 32.2 us
  Pallas kernels: 22.2 us -> 23.1 us
    ppermute x8 -> x14, starting transfers between devices: 11.5 us -> 17.4 us  [the longest x4 5.26 us: body(): other = [lax.ppermute(slots, 'wide', swap) for slots in own]]
    all_to_all x1 -> x0, starting transfers between devices: 4.74 us -> none  [finish(): pieces = lax.all_to_all(rows, 'wide', 0, 0, axis_index_groups=x_groups)]
    all_to_all x1, waiting for transfers between devices: 4.57 us -> 0.09 us  [spread(): slots = lax.all_to_all(slots, 'wide', 0, 0, axis_index_groups=z_groups)]
    pallas_call x1, Pallas kernels: 3.15 us -> 4.26 us  [pick_slots(): pl.pallas_call(pick_kernel, out_shape=(jax.ShapeDtypeStruct((SLOTS, nodes...]
    pallas_call x2, Pallas kernels: 3.37 us -> 2.56 us  [the longest x1 1.48 us: plane_slots(): pl.pallas_call(plane_kernel, out_shape=jax.ShapeDtypeStruct((planes, room...]
  transfers between devices with their start and end apart: 16 -> 21, of which waited for: 9 -> 7; matrix products, arithmetic and copies ran while one was open for 0% -> 1% of each run, Pallas kernels for 19% -> 21%
where the time goes in v5:
time: 71.2 us; the launch traced here: 71 us
  starting transfers between devices  32.2 us (45%)
  Pallas kernels  23.1 us (32%)
  waiting for transfers between devices  13.9 us (20%)
  between operations  0.98 us (1%)
    ppermute x6, waiting for transfers between devices, received(): return [lax.ppermute(value, 'narrow', shift_y[d]) for d in range(1, narrow)]  13.3 us
    ppermute x6, starting transfers between devices, received(): return [lax.ppermute(value, 'narrow', shift_y[d]) for d in range(1, narrow)]  7.71 us
    all_to_all x1, starting transfers between devices, spread(): slots = lax.all_to_all(slots, 'wide', 0, 0, axis_index_groups=z_groups)  7.18 us
    pallas_call x1, Pallas kernels, invert(): pl.pallas_call(invert_kernel, out_shape=jax.ShapeDtypeStruct(parts[0].sha...  7.16 us
    ppermute x4, starting transfers between devices, body(): other = [lax.ppermute(slots, 'wide', swap) for slots in own]  5.26 us
    ppermute x3, starting transfers between devices, body(): lax.ppermute(rows, 'wide', shift_x[d])  4.63 us
    pallas_call x1, Pallas kernels, respond(): pl.pallas_call(respond_kernel, out_shape=jax.ShapeDtypeStruct((rows, coun...  4.3 us
    pallas_call x1, Pallas kernels, pick_slots(): pl.pallas_call(pick_kernel, out_shape=(jax.ShapeDtypeStruct((SLOTS, nodes...  4.26 us
  transfers between devices with their start and end apart: 21, of which 7 were waited for; matrix products, arithmetic and copies ran while one was open for 1% of the time, Pallas kernels for 21%

profile of v5, /device:TPU:3, one launch (start us, length us, event | category | flops | bytes accessed | tf_op | source)
XLA Modules:
  0.0 71.0 jit_solution(6730325394343642558)
XLA Ops:
  0.0 4.3 %pick_slots.1 = (f32[16,1152]{1,0:T(8,128)S(1)}, f32[16,1152]{1,0:T(8,128)}, f32[16,1152]{1,0:T(8,128)}, f32[16,1152]{1,0:T(8,128)}, s32[8,128]{1,0:T(8,128)S(1)}) custom-call(s32[1,128]{1,0:T(1,128)} %bitcast.11, f32[256,4096]{1,0:T(8,128)} %g_ref.5, f32[4096,128]{1,0:T(8,128)} %change_ref.1), custom_call_target="tpu_custom_call" | custom-call | tf_op jit(solution)/shard_map/pick_slots/pallas_call | solution.py:98
  4.3 1.3 %collective-permute-start.12 = (f32[16,1152]{1,0:T(8,128)}, f32[16,1152]{1,0:T(8,128)S(1)}, u32[]{:S(2)}, u32[]{:S(2)}) collective-permute-start(f32[16,1152]{1,0:T(8,128)} %get-tuple-element.175), channel_id=1, source_target_pairs={{0,8},{4,12},{8,16},{12,20},{16,24},{20,28},{24,0},{28,4},{32,40},... | collective-permute-start | bytes 221192 | tf_op jit(solution)/shard_map/ppermute | solution.py:465
  5.5 0.8 %collective-permute-start.13 = (f32[16,1152]{1,0:T(8,128)}, f32[16,1152]{1,0:T(8,128)S(1)}, u32[]{:S(2)}, u32[]{:S(2)}) collective-permute-start(f32[16,1152]{1,0:T(8,128)} %get-tuple-element.176), channel_id=1, source_target_pairs={{0,16},{4,20},{8,24},{12,28},{16,0},{20,4},{24,8},{28,12},{32,48},... | collective-permute-start | bytes 221192 | tf_op jit(solution)/shard_map/ppermute | solution.py:465
  6.3 2.0 %collective-permute-start.14 = (f32[16,1152]{1,0:T(8,128)}, f32[16,1152]{1,0:T(8,128)S(1)}, u32[]{:S(2)}, u32[]{:S(2)}) collective-permute-start(f32[16,1152]{1,0:T(8,128)} %get-tuple-element.177), channel_id=1, source_target_pairs={{0,24},{4,28},{8,0},{12,4},{16,8},{20,12},{24,16},{28,20},{32,56},... | collective-permute-start | bytes 221192 | tf_op jit(solution)/shard_map/ppermute | solution.py:465
  8.3 1.4 %collective-permute-start.15 = (f32[16,1152]{1,0:T(8,128)S(1)}, f32[16,1152]{1,0:T(8,128)S(1)}, u32[]{:S(2)}, u32[]{:S(2)}) collective-permute-start(f32[16,1152]{1,0:T(8,128)S(1)} %get-tuple-element.174), channel_id=1, source_target_pairs={{0,4},{4,0},{8,12},{12,8},{16,20},{20,16},{24,28},{28,24},{32,36},... | collective-permute-start | bytes 221192 | tf_op jit(solution)/shard_map/ppermute | solution.py:466
  9.7 0.0 collective-permute-done.12
  9.7 0.3 collective-permute-start.16
  10.0 0.5 collective-permute-done.13
  10.5 2.2 %collective-permute-start.17 = (f32[16,1152]{1,0:T(8,128)S(1)}, f32[16,1152]{1,0:T(8,128)S(1)}, u32[]{:S(2)}, u32[]{:S(2)}) collective-permute-start(f32[16,1152]{1,0:T(8,128)S(1)} %collective-permute-done.13), channel_id=1, source_target_pairs={{0,4},{4,0},{8,12},{12,8},{16,20},{20,16},{24,28},{28,24},{32,36},... | collective-permute-start | bytes 221192 | tf_op jit(solution)/shard_map/ppermute | solution.py:466
  12.8 0.0 collective-permute-done.14
  12.8 1.3 %collective-permute-start.18 = (f32[16,1152]{1,0:T(8,128)S(1)}, f32[16,1152]{1,0:T(8,128)S(1)}, u32[]{:S(2)}, u32[]{:S(2)}) collective-permute-start(f32[16,1152]{1,0:T(8,128)S(1)} %collective-permute-done.14), channel_id=1, source_target_pairs={{0,4},{4,0},{8,12},{12,8},{16,20},{20,16},{24,28},{28,24},{32,36},... | collective-permute-start | bytes 221192 | tf_op jit(solution)/shard_map/ppermute | solution.py:466
  14.1 0.5 slice.13
  15.3 0.0 collective-permute-done.15
  15.3 0.0 collective-permute-done.16
  15.3 0.0 collective-permute-done.17
  15.3 0.0 collective-permute-done.18
  15.3 27.2 %conditional.1 = (f32[128,512]{1,0:T(8,128)S(1)}, f32[128,128]{1,0:T(8,128)S(1)}, f32[256,128]{1,0:T(8,128)}, f32[256,128]{1,0:T(8,128)}, f32[256,128]{1,0:T(8,128)}, /*index=5*/f32[256,128]{1,0:T(8,128)}) conditional(s32[]{:T(128)} %bitcast.5, (s32[8,128]{1,0:T(8,128)S(1)}, f32[16,1152]{1,0:T(8,128)S(1)}, f32[16,1152]{1,0:T(8,128)S(1)}, ...), branch_computations={%region_0.1_spmd, %region_1.2_spmd, %region_2.5_spmd} | conditional | flops 852039744 | bytes 34458876 | solution.py:513
  15.3 1.5 %plane_slots.2 = f32[8,24,640]{2,1,0:T(8,128)} custom-call(s32[8,128]{1,0:T(8,128)S(1)} %get-tuple-element.117.table_ref.token_ref, f32[16,1152]{1,0:T(8,128)S(1)} %get-tuple-element.108.refs_0_, f32[16,1152]{1,0:T(8,128)S(1)} %get-tuple-element.109.refs_1_, f32[16,1152]{1,0:T(8,128)S(1)} %get-tuple-element.110.refs_2_, ...), custom_call_target="tpu_custom_call" | custom-call | tf_op jit(solution)/shard_map/cond/branch_0_fun/plane_slots/pallas_call | solution.py:188
  16.8 7.2 %all-to-all-start = ((f32[8,24,640]{2,1,0:T(8,128)}), f32[8,24,640]{2,1,0:T(8,128)S(1)}, u32[]{:S(2)}, u32[]{:S(2)}) async-start(f32[8,24,640]{2,1,0:T(8,128)} %plane_slots.2), calls=%async_computation | async-start | bytes 983040 | tf_op jit(solution)/shard_map/cond/branch_0_fun/all_to_all | solution.py:473
  24.0 4.3 %respond.3 = f32[256,128]{1,0:T(8,128)} custom-call(s32[8,128]{1,0:T(8,128)S(1)} %get-tuple-element.117.table_ref.token_ref, f32[256,4096]{1,0:T(8,128)} %get-tuple-element.118.g_ref, f32[4096,128]{1,0:T(8,128)S(1)} %get-tuple-element.119.change_ref), custom_call_target="tpu_custom_call" | custom-call | flops 800000000 | bytes 8000000 | tf_op jit(solution)/shard_map/cond/branch_0_fun/respond/pallas_call | solution.py:148
  28.3 2.8 %collective-permute-start.2 = (f32[256,128]{1,0:T(8,128)}, f32[256,128]{1,0:T(8,128)}, u32[]{:S(2)}, u32[]{:S(2)}) collective-permute-start(f32[256,128]{1,0:T(8,128)} %respond.3), channel_id=1, source_target_pairs={{0,3},{1,0},{2,1},{3,2},{4,7},{5,4},{6,5},{7,6},{8,11},{9,8},{10,9... | collective-permute-start | bytes 393224 | tf_op jit(solution)/shard_map/cond/branch_0_fun/ppermute | solution.py:463
  31.1 0.3 collective-permute-start.1
  31.5 0.7 collective-permute-start
  32.2 4.4 %collective-permute-done.2 = f32[256,128]{1,0:T(8,128)} collective-permute-done((f32[256,128]{1,0:T(8,128)}, f32[256,128]{1,0:T(8,128)}, u32[]{:S(2)}, u32[]{:S(2)}) %collective-permute-start.2) | collective-permute-done | bytes 131104 | tf_op jit(solution)/shard_map/cond/branch_0_fun/ppermute | solution.py:463
  36.5 0.6 collective-permute-done.1
  37.1 4.0 %collective-permute-done = f32[256,128]{1,0:T(8,128)} collective-permute-done((f32[256,128]{1,0:T(8,128)}, f32[256,128]{1,0:T(8,128)}, u32[]{:S(2)}, u32[]{:S(2)}) %collective-permute-start) | collective-permute-done | bytes 131104 | tf_op jit(solution)/shard_map/cond/branch_0_fun/ppermute | solution.py:463
  41.2 0.1 all-to-all-done
  41.3 1.1 %order_rows.2 = (f32[128,512]{1,0:T(8,128)S(1)}, f32[128,128]{1,0:T(8,128)S(1)}) custom-call(s32[8,128]{1,0:T(8,128)S(1)} %get-tuple-element.117.table_ref.token_ref, f32[192,640]{1,0:T(8,128)S(1)} %bitcast.8), custom_call_target="tpu_custom_call" | custom-call | tf_op jit(solution)/shard_map/cond/branch_0_fun/order_rows/pallas_call | solution.py:215
  42.6 2.8 %collective-permute-start.24 = (f32[128,128]{1,0:T(8,128)S(1)}, f32[128,128]{1,0:T(8,128)S(1)}, u32[]{:S(2)}, u32[]{:S(2)}) collective-permute-start(f32[128,128]{1,0:T(8,128)S(1)} %get-tuple-element.179.refs_0_), channel_id=1, source_target_pairs={{0,3},{1,0},{2,1},{3,2},{4,7},{5,4},{6,5},{7,6},{8,11},{9,8},{10,9... | collective-permute-start | bytes 196616 | tf_op jit(solution)/shard_map/ppermute | solution.py:463
  45.4 1.2 %collective-permute-start.21 = (f32[128,512]{1,0:T(8,128)S(1)}, f32[128,512]{1,0:T(8,128)S(1)}, u32[]{:S(2)}, u32[]{:S(2)}) collective-permute-start(f32[128,512]{1,0:T(8,128)S(1)} %get-tuple-element.181.refs_0_), channel_id=1, source_target_pairs={{0,24},{4,28},{8,0},{12,4},{16,8},{20,12},{24,16},{28,20},{32,56},... | collective-permute-start | bytes 786440 | tf_op jit(solution)/shard_map/ppermute | solution.py:515
  46.5 1.4 %collective-permute-start.20 = (f32[128,512]{1,0:T(8,128)S(1)}, f32[128,512]{1,0:T(8,128)S(1)}, u32[]{:S(2)}, u32[]{:S(2)}) collective-permute-start(f32[128,512]{1,0:T(8,128)S(1)} %get-tuple-element.181.refs_0_), channel_id=1, source_target_pairs={{0,16},{4,20},{8,24},{12,28},{16,0},{20,4},{24,8},{28,12},{32,48},... | collective-permute-start | bytes 786440 | tf_op jit(solution)/shard_map/ppermute | solution.py:515
  47.9 2.1 %collective-permute-start.19 = (f32[128,512]{1,0:T(8,128)S(1)}, f32[128,512]{1,0:T(8,128)S(1)}, u32[]{:S(2)}, u32[]{:S(2)}) collective-permute-start(f32[128,512]{1,0:T(8,128)S(1)} %get-tuple-element.181.refs_0_), channel_id=1, source_target_pairs={{0,8},{4,12},{8,16},{12,20},{16,24},{20,28},{24,0},{28,4},{32,40},... | collective-permute-start | bytes 786440 | tf_op jit(solution)/shard_map/ppermute | solution.py:515
  50.0 0.4 collective-permute-start.23
  50.4 0.0 collective-permute-done.24.refs_3_
  50.4 0.7 collective-permute-start.22
  51.1 3.6 %collective-permute-done.23.refs_2_ = f32[128,128]{1,0:T(8,128)S(1)} collective-permute-done((f32[128,128]{1,0:T(8,128)S(1)}, f32[128,128]{1,0:T(8,128)S(1)}, u32[]{:S(2)}, u32[]{:S(2)}) %collective-permute-start.23) | collective-permute-done | bytes 65568 | tf_op jit(solution)/shard_map/ppermute | solution.py:463
  54.7 0.6 collective-permute-done.22.refs_1_
  55.3 7.2 %invert_capacitance.1.inverse_ref = f32[128,128]{1,0:T(8,128)S(1)} custom-call(f32[128,128]{1,0:T(8,128)S(1)} %get-tuple-element.179.refs_0_, f32[128,128]{1,0:T(8,128)S(1)} %collective-permute-done.22.refs_1_, f32[128,128]{1,0:T(8,128)S(1)} %collective-permute-done.23.refs_2_, f32[128,128]{1,0:T(8,128)S(1)} %collective-permute-done.24.refs_3_), custom_call_target="tpu_custom_call" | custom-call | flops 2000000000 | bytes 8000000 | tf_op jit(solution)/shard_map/invert_capacitance/pallas_call | solution.py:360
  62.5 0.0 collective-permute-done.21.refs_3_
  62.5 0.0 collective-permute-done.19.refs_1_
  62.5 2.8 %collective-permute-start.25 = (f32[128,512]{1,0:T(8,128)S(1)}, f32[128,512]{1,0:T(8,128)S(1)}, u32[]{:S(2)}, u32[]{:S(2)}) collective-permute-start(f32[128,512]{1,0:T(8,128)S(1)} %get-tuple-element.181.refs_0_), channel_id=1, source_target_pairs={{0,4},{4,0},{8,12},{12,8},{16,20},{20,16},{24,28},{28,24},{32,36},... | collective-permute-start | bytes 786440 | tf_op jit(solution)/shard_map/ppermute | solution.py:518
  65.4 0.1 collective-permute-start.26
  65.5 0.4 collective-permute-start.27
  65.9 0.1 collective-permute-start.28
  66.0 3.2 %update_own.1 = (f32[256,4096]{1,0:T(8,128)}, bf16[256,384]{1,0:T(8,128)(2,1)S(1)}) custom-call(f32[128,128]{1,0:T(8,128)S(1)} %invert_capacitance.1.inverse_ref, f32[256,4096]{1,0:T(8,128)S(1)} %copy-done, f32[128,512]{1,0:T(8,128)S(1)} %get-tuple-element.181.refs_0_, f32[128,512]{1,0:T(8,128)S(1)} %collective-permute-done.19.refs_1_, ...), custom_call_target="tpu_custom_call" | custom-call | flops 1000000000 | bytes 6000000 | tf_op jit(solution)/shard_map/update_own/pallas_call | solution.py:415
  69.2 0.0 collective-permute-done.26.refs_1_
  69.2 0.0 collective-permute-done.27.refs_2_
  69.2 1.6 %update_other.1 = f32[256,4096]{1,0:T(8,128)} custom-call(bf16[256,384]{1,0:T(8,128)(2,1)S(1)} %get-tuple-element.189.left_ref, f32[256,4096]{1,0:T(8,128)S(1)} %copy-done, f32[256,4096]{1,0:T(8,128)} %get-tuple-element.190.before_ref, f32[128,512]{1,0:T(8,128)S(1)} %collective-permute-done.25.refs_0_, ...), custom_call_target="tpu_custom_call", output_to_operand_aliasing={{}: (2, {})} | custom-call | tf_op jit(solution)/shard_map/update_other/pallas_call | solution.py:425
  (9 shorter events, 0.0 us)
Async XLA Ops:
  0.0 15.3 %copy-start.1 = (f32[4096,128]{1,0:T(8,128)S(1)}, f32[4096,128]{1,0:T(8,128)}, u32[]{:S(2)}) copy-start(f32[4096,128]{1,0:T(8,128)} %change_ref.1) | copy-start | bytes 6291460
  0.0 15.3 %copy-start.3 = (s32[128]{0:T(128)S(1)}, s32[128]{0:T(128)}, u32[]{:S(2)}) copy-start(s32[128]{0:T(128)} %param.8) | copy-start | bytes 1540
  4.3 5.4 %collective-permute-start.12 = (f32[16,1152]{1,0:T(8,128)}, f32[16,1152]{1,0:T(8,128)S(1)}, u32[]{:S(2)}, u32[]{:S(2)}) collective-permute-start(f32[16,1152]{1,0:T(8,128)} %get-tuple-element.175), channel_id=1, source_target_pairs={{0,8},{4,12},{8,16},{12,20},{16,24},{20,28},{24,0},{28,4},{32,40},... | collective-permute-start | bytes 221192 | tf_op jit(solution)/shard_map/ppermute | solution.py:465
  5.5 5.0 %collective-permute-start.13 = (f32[16,1152]{1,0:T(8,128)}, f32[16,1152]{1,0:T(8,128)S(1)}, u32[]{:S(2)}, u32[]{:S(2)}) collective-permute-start(f32[16,1152]{1,0:T(8,128)} %get-tuple-element.176), channel_id=1, source_target_pairs={{0,16},{4,20},{8,24},{12,28},{16,0},{20,4},{24,8},{28,12},{32,48},... | collective-permute-start | bytes 221192 | tf_op jit(solution)/shard_map/ppermute | solution.py:465
  6.3 6.4 %collective-permute-start.14 = (f32[16,1152]{1,0:T(8,128)}, f32[16,1152]{1,0:T(8,128)S(1)}, u32[]{:S(2)}, u32[]{:S(2)}) collective-permute-start(f32[16,1152]{1,0:T(8,128)} %get-tuple-element.177), channel_id=1, source_target_pairs={{0,24},{4,28},{8,0},{12,4},{16,8},{20,12},{24,16},{28,20},{32,56},... | collective-permute-start | bytes 221192 | tf_op jit(solution)/shard_map/ppermute | solution.py:465
  8.3 7.0 %collective-permute-start.15 = (f32[16,1152]{1,0:T(8,128)S(1)}, f32[16,1152]{1,0:T(8,128)S(1)}, u32[]{:S(2)}, u32[]{:S(2)}) collective-permute-start(f32[16,1152]{1,0:T(8,128)S(1)} %get-tuple-element.174), channel_id=1, source_target_pairs={{0,4},{4,0},{8,12},{12,8},{16,20},{20,16},{24,28},{28,24},{32,36},... | collective-permute-start | bytes 221192 | tf_op jit(solution)/shard_map/ppermute | solution.py:466
  9.7 5.6 %collective-permute-start.16 = (f32[16,1152]{1,0:T(8,128)S(1)}, f32[16,1152]{1,0:T(8,128)S(1)}, u32[]{:S(2)}, u32[]{:S(2)}) collective-permute-start(f32[16,1152]{1,0:T(8,128)S(1)} %collective-permute-done.12), channel_id=1, source_target_pairs={{0,4},{4,0},{8,12},{12,8},{16,20},{20,16},{24,28},{28,24},{32,36},... | collective-permute-start | bytes 221192 | tf_op jit(solution)/shard_map/ppermute | solution.py:466
  10.5 4.8 %collective-permute-start.17 = (f32[16,1152]{1,0:T(8,128)S(1)}, f32[16,1152]{1,0:T(8,128)S(1)}, u32[]{:S(2)}, u32[]{:S(2)}) collective-permute-start(f32[16,1152]{1,0:T(8,128)S(1)} %collective-permute-done.13), channel_id=1, source_target_pairs={{0,4},{4,0},{8,12},{12,8},{16,20},{20,16},{24,28},{28,24},{32,36},... | collective-permute-start | bytes 221192 | tf_op jit(solution)/shard_map/ppermute | solution.py:466
  12.8 2.5 %collective-permute-start.18 = (f32[16,1152]{1,0:T(8,128)S(1)}, f32[16,1152]{1,0:T(8,128)S(1)}, u32[]{:S(2)}, u32[]{:S(2)}) collective-permute-start(f32[16,1152]{1,0:T(8,128)S(1)} %collective-permute-done.14), channel_id=1, source_target_pairs={{0,4},{4,0},{8,12},{12,8},{16,20},{20,16},{24,28},{28,24},{32,36},... | collective-permute-start | bytes 221192 | tf_op jit(solution)/shard_map/ppermute | solution.py:466
  16.8 24.4 %all-to-all-start = ((f32[8,24,640]{2,1,0:T(8,128)}), f32[8,24,640]{2,1,0:T(8,128)S(1)}, u32[]{:S(2)}, u32[]{:S(2)}) async-start(f32[8,24,640]{2,1,0:T(8,128)} %plane_slots.2), calls=%async_computation | async-start | bytes 983040 | tf_op jit(solution)/shard_map/cond/branch_0_fun/all_to_all | solution.py:473
  28.3 8.2 %collective-permute-start.2 = (f32[256,128]{1,0:T(8,128)}, f32[256,128]{1,0:T(8,128)}, u32[]{:S(2)}, u32[]{:S(2)}) collective-permute-start(f32[256,128]{1,0:T(8,128)} %respond.3), channel_id=1, source_target_pairs={{0,3},{1,0},{2,1},{3,2},{4,7},{5,4},{6,5},{7,6},{8,11},{9,8},{10,9... | collective-permute-start | bytes 393224 | tf_op jit(solution)/shard_map/cond/branch_0_fun/ppermute | solution.py:463
  31.1 6.0 %collective-permute-start.1 = (f32[256,128]{1,0:T(8,128)}, f32[256,128]{1,0:T(8,128)}, u32[]{:S(2)}, u32[]{:S(2)}) collective-permute-start(f32[256,128]{1,0:T(8,128)} %respond.3), channel_id=1, source_target_pairs={{0,2},{1,3},{2,0},{3,1},{4,6},{5,7},{6,4},{7,5},{8,10},{9,11},{10,... | collective-permute-start | bytes 393224 | tf_op jit(solution)/shard_map/cond/branch_0_fun/ppermute | solution.py:463
  31.5 9.7 %collective-permute-start = (f32[256,128]{1,0:T(8,128)}, f32[256,128]{1,0:T(8,128)}, u32[]{:S(2)}, u32[]{:S(2)}) collective-permute-start(f32[256,128]{1,0:T(8,128)} %respond.3), channel_id=1, source_target_pairs={{0,1},{1,2},{2,3},{3,0},{4,5},{5,6},{6,7},{7,4},{8,9},{9,10},{10,1... | collective-permute-start | bytes 393224 | tf_op jit(solution)/shard_map/cond/branch_0_fun/ppermute | solution.py:463
  42.6 7.8 %collective-permute-start.24 = (f32[128,128]{1,0:T(8,128)S(1)}, f32[128,128]{1,0:T(8,128)S(1)}, u32[]{:S(2)}, u32[]{:S(2)}) collective-permute-start(f32[128,128]{1,0:T(8,128)S(1)} %get-tuple-element.179.refs_0_), channel_id=1, source_target_pairs={{0,3},{1,0},{2,1},{3,2},{4,7},{5,4},{6,5},{7,6},{8,11},{9,8},{10,9... | collective-permute-start | bytes 196616 | tf_op jit(solution)/shard_map/ppermute | solution.py:463
  45.4 17.1 %collective-permute-start.21 = (f32[128,512]{1,0:T(8,128)S(1)}, f32[128,512]{1,0:T(8,128)S(1)}, u32[]{:S(2)}, u32[]{:S(2)}) collective-permute-start(f32[128,512]{1,0:T(8,128)S(1)} %get-tuple-element.181.refs_0_), channel_id=1, source_target_pairs={{0,24},{4,28},{8,0},{12,4},{16,8},{20,12},{24,16},{28,20},{32,56},... | collective-permute-start | bytes 786440 | tf_op jit(solution)/shard_map/ppermute | solution.py:515
  46.5 16.0 %collective-permute-start.20 = (f32[128,512]{1,0:T(8,128)S(1)}, f32[128,512]{1,0:T(8,128)S(1)}, u32[]{:S(2)}, u32[]{:S(2)}) collective-permute-start(f32[128,512]{1,0:T(8,128)S(1)} %get-tuple-element.181.refs_0_), channel_id=1, source_target_pairs={{0,16},{4,20},{8,24},{12,28},{16,0},{20,4},{24,8},{28,12},{32,48},... | collective-permute-start | bytes 786440 | tf_op jit(solution)/shard_map/ppermute | solution.py:515
  47.9 14.6 %collective-permute-start.19 = (f32[128,512]{1,0:T(8,128)S(1)}, f32[128,512]{1,0:T(8,128)S(1)}, u32[]{:S(2)}, u32[]{:S(2)}) collective-permute-start(f32[128,512]{1,0:T(8,128)S(1)} %get-tuple-element.181.refs_0_), channel_id=1, source_target_pairs={{0,8},{4,12},{8,16},{12,20},{16,24},{20,28},{24,0},{28,4},{32,40},... | collective-permute-start | bytes 786440 | tf_op jit(solution)/shard_map/ppermute | solution.py:515
  50.0 4.7 %collective-permute-start.23 = (f32[128,128]{1,0:T(8,128)S(1)}, f32[128,128]{1,0:T(8,128)S(1)}, u32[]{:S(2)}, u32[]{:S(2)}) collective-permute-start(f32[128,128]{1,0:T(8,128)S(1)} %get-tuple-element.179.refs_0_), channel_id=1, source_target_pairs={{0,2},{1,3},{2,0},{3,1},{4,6},{5,7},{6,4},{7,5},{8,10},{9,11},{10,... | collective-permute-start | bytes 196616 | tf_op jit(solution)/shard_map/ppermute | solution.py:463
  50.4 5.0 %collective-permute-start.22 = (f32[128,128]{1,0:T(8,128)S(1)}, f32[128,128]{1,0:T(8,128)S(1)}, u32[]{:S(2)}, u32[]{:S(2)}) collective-permute-start(f32[128,128]{1,0:T(8,128)S(1)} %get-tuple-element.179.refs_0_), channel_id=1, source_target_pairs={{0,1},{1,2},{2,3},{3,0},{4,5},{5,6},{6,7},{7,4},{8,9},{9,10},{10,1... | collective-permute-start | bytes 196616 | tf_op jit(solution)/shard_map/ppermute | solution.py:463
  55.3 10.6 %copy-start = (f32[256,4096]{1,0:T(8,128)S(1)}, f32[256,4096]{1,0:T(8,128)}, u32[]{:S(2)}) copy-start(f32[256,4096]{1,0:T(8,128)} %g_ref.5) | copy-start | bytes 12582916
  62.5 6.6 %collective-permute-start.25 = (f32[128,512]{1,0:T(8,128)S(1)}, f32[128,512]{1,0:T(8,128)S(1)}, u32[]{:S(2)}, u32[]{:S(2)}) collective-permute-start(f32[128,512]{1,0:T(8,128)S(1)} %get-tuple-element.181.refs_0_), channel_id=1, source_target_pairs={{0,4},{4,0},{8,12},{12,8},{16,20},{20,16},{24,28},{28,24},{32,36},... | collective-permute-start | bytes 786440 | tf_op jit(solution)/shard_map/ppermute | solution.py:518
  65.4 3.8 %collective-permute-start.26 = (f32[128,512]{1,0:T(8,128)S(1)}, f32[128,512]{1,0:T(8,128)S(1)}, u32[]{:S(2)}, u32[]{:S(2)}) collective-permute-start(f32[128,512]{1,0:T(8,128)S(1)} %collective-permute-done.19.refs_1_), channel_id=1, source_target_pairs={{0,4},{4,0},{8,12},{12,8},{16,20},{20,16},{24,28},{28,24},{32,36},... | collective-permute-start | bytes 786440 | tf_op jit(solution)/shard_map/ppermute | solution.py:518
  65.5 3.7 %collective-permute-start.27 = (f32[128,512]{1,0:T(8,128)S(1)}, f32[128,512]{1,0:T(8,128)S(1)}, u32[]{:S(2)}, u32[]{:S(2)}) collective-permute-start(f32[128,512]{1,0:T(8,128)S(1)} %collective-permute-done.20.refs_2_), channel_id=1, source_target_pairs={{0,4},{4,0},{8,12},{12,8},{16,20},{20,16},{24,28},{28,24},{32,36},... | collective-permute-start | bytes 786440 | tf_op jit(solution)/shard_map/ppermute | solution.py:518
  65.9 3.3 %collective-permute-start.28 = (f32[128,512]{1,0:T(8,128)S(1)}, f32[128,512]{1,0:T(8,128)S(1)}, u32[]{:S(2)}, u32[]{:S(2)}) collective-permute-start(f32[128,512]{1,0:T(8,128)S(1)} %collective-permute-done.21.refs_3_), channel_id=1, source_target_pairs={{0,4},{4,0},{8,12},{12,8},{16,20},{20,16},{24,28},{28,24},{32,36},... | collective-permute-start | bytes 786440 | tf_op jit(solution)/shard_map/ppermute | solution.py:518

commit v6 on v5

--- a/solution.py
+++ b/solution.py
@@ -340,10 +340,15 @@
     return normal
 
 
-def invert_kernel(*refs):
-    out_ref = refs[-1]
-    touched = refs[0][...]
-    for ref in refs[1:-1]:
+def solve_kernel(narrow, *refs):
+    left_ref, buffer_ref, sem = refs[-3:]
+    touched_refs, response_refs = refs[:-3 - narrow], refs[-3 - narrow:-3]
+    copies = []
+    for i, ref in enumerate(response_refs):
+        copies.append(pltpu.make_async_copy(ref, buffer_ref.at[i], sem.at[i]))
+        copies[i].start()
+    touched = touched_refs[0][...]
+    for ref in touched_refs[1:]:
         touched = touched + ref[...]
     count = touched.shape[0]
     row = lax.broadcasted_iota(jnp.int32, (count, count), 0)
@@ -352,20 +357,33 @@
     normal = lax.dot_general(
         capacitance, capacitance, (((1,), (1,)), ((), ())), precision=HIGHEST, preferred_element_type=jnp.float32
     )
-    out_ref[...] = jnp.dot(spd_inverse(normal), capacitance, precision=HIGHEST, preferred_element_type=jnp.float32)
-
-
-def invert(parts):
+    inverse = jnp.dot(spd_inverse(normal), capacitance, precision=HIGHEST, preferred_element_type=jnp.float32)
+    for copy in copies:
+        copy.wait()
+    response = buffer_ref[0]
+    for i in range(1, narrow):
+        response = response + buffer_ref[i]
+    solved = lax.dot_general(
+        response, inverse, (((1,), (1,)), ((), ())), precision=HIGHEST, preferred_element_type=jnp.float32
+    )
+    s_high, s_low = split(solved)
+    left_ref[...] = jnp.concatenate([s_high, s_low, s_high], axis=1)
+
+
+def solve(touched, response):
+    rows, count = response[0].shape
+    narrow = len(response)
     vmem = pl.BlockSpec(memory_space=pltpu.VMEM)
     return pl.pallas_call(
-        invert_kernel,
-        out_shape=jax.ShapeDtypeStruct(parts[0].shape, jnp.float32),
-        in_specs=[vmem] * len(parts),
+        functools.partial(solve_kernel, narrow),
+        out_shape=jax.ShapeDtypeStruct((rows, 3 * count), jnp.bfloat16),
+        in_specs=[vmem] * len(touched) + [pl.BlockSpec(memory_space=pl.ANY)] * narrow,
         out_specs=vmem,
+        scratch_shapes=[pltpu.VMEM((narrow, rows, count), jnp.float32), pltpu.SemaphoreType.DMA((narrow,))],
         cost_estimate=pl.CostEstimate(flops=2_000_000_000, bytes_accessed=8_000_000, transcendentals=0),
         compiler_params=pltpu.CompilerParams(vmem_limit_bytes=16 * 1024 * 1024),
-        name="invert_capacitance",
-    )(*parts)
+        name="solve",
+    )(*touched, *response)
 
 
 def places(core, part):
@@ -385,18 +403,9 @@
         copy.wait()
 
 
-def update_own_kernel(inverse_ref, g_ref, *refs):
-    pieces, response_refs, (out_ref, left_ref, buffer_ref, sem) = refs[:XS], refs[XS:-4], refs[-4:]
-    response = response_refs[0][...]
-    for ref in response_refs[1:]:
-        response = response + ref[...]
-    solved = lax.dot_general(
-        response, inverse_ref[...], (((1,), (1,)), ((), ())), precision=HIGHEST, preferred_element_type=jnp.float32
-    )
-    s_high, s_low = split(solved)
-    left = jnp.concatenate([s_high, s_low, s_high], axis=1)
-    left_ref[...] = left
-    write_blocks(left, g_ref, pieces, out_ref, buffer_ref, sem, lax.axis_index("wide") % CORES)
+def update_own_kernel(left_ref, g_ref, *refs):
+    pieces, (out_ref, buffer_ref, sem) = refs[:XS], refs[XS:]
+    write_blocks(left_ref[...], g_ref, pieces, out_ref, buffer_ref, sem, lax.axis_index("wide") % CORES)
 
 
 def update_other_kernel(left_ref, g_ref, before_ref, *refs):
@@ -404,24 +413,24 @@
     write_blocks(left_ref[...], g_ref, pieces, out_ref, buffer_ref, sem, 1 - lax.axis_index("wide") % CORES)
 
 
-def update(gebhart, inverse, response, pieces, swapped):
+def update(gebhart, left, pieces, swapped):
     rows, nodes = gebhart.shape
-    count, part = pieces[0].shape
+    part = pieces[0].shape[1]
     vmem = pl.BlockSpec(memory_space=pltpu.VMEM)
     hbm = pl.BlockSpec(memory_space=pl.ANY)
     whole = jax.ShapeDtypeStruct((rows, nodes), jnp.float32)
     scratch = [pltpu.VMEM((XS, rows, part), jnp.float32), pltpu.SemaphoreType.DMA((XS,))]
     params = pltpu.CompilerParams(vmem_limit_bytes=16 * 1024 * 1024)
-    own, left = pl.pallas_call(
+    own = pl.pallas_call(
         update_own_kernel,
-        out_shape=(whole, jax.ShapeDtypeStruct((rows, 3 * count), jnp.bfloat16)),
-        in_specs=[vmem] * (2 + XS + len(response)),
-        out_specs=(hbm, vmem),
+        out_shape=whole,
+        in_specs=[vmem] * (2 + XS),
+        out_specs=hbm,
         scratch_shapes=scratch,
         cost_estimate=pl.CostEstimate(flops=1_000_000_000, bytes_accessed=6_000_000, transcendentals=0),
         compiler_params=params,
         name="update_own",
-    )(inverse, gebhart, *pieces, *response)
+    )(left, gebhart, *pieces)
     return pl.pallas_call(
         update_other_kernel,
         out_shape=whole,
@@ -513,9 +522,14 @@
     rows, touched, *response = lax.switch(table[2, 0], paths, gebhart, change, moved_nodes, own + other, table)
 
     pieces = [rows] + [lax.ppermute(rows, "wide", shift_x[d]) for d in range(1, XS)]
-    inverse = invert([touched] + received(touched))
-    pieces, inverse = lax.optimization_barrier((pieces, inverse))
-    return update(gebhart, inverse, response, pieces, [lax.ppermute(piece, "wide", swap) for piece in pieces])
+    step = 1
+    while step < narrow:
+        parts = [touched, lax.ppermute(touched, "narrow", [(i, i ^ step) for i in range(narrow)])]
+        touched = parts[0] + parts[1]
+        step *= 2
+    left = solve(parts, response)
+    pieces, left = lax.optimization_barrier((pieces, left))
+    return update(gebhart, left, pieces, [lax.ppermute(piece, "wide", swap) for piece in pieces])
 
 
 def solution(mesh):

time: 71.2 us -> 68.6 us (0.963)
  waiting for transfers between devices: 13.9 us -> 11.8 us
    ppermute x6 -> x3, waiting for transfers between devices: 13.3 us -> 8.81 us  [received(): return [lax.ppermute(value, 'narrow', shift_y[d]) for d in range(1, narrow)]]
    ppermute x0 -> x2, starting transfers between devices: none -> 4.09 us  [body(): lax.ppermute(touched, 'narrow', [(i, i ^ step) for i in range(narrow)])]
    ppermute x6 -> x3, starting transfers between devices: 7.71 us -> 3.86 us  [received(): return [lax.ppermute(value, 'narrow', shift_y[d]) for d in range(1, narrow)]]
    ppermute x0 -> x2, waiting for transfers between devices: none -> 2 us  [body(): lax.ppermute(touched, 'narrow', [(i, i ^ step) for i in range(narrow)])]
    pallas_call x2, Pallas kernels: 10.3 us -> 9.58 us  [the longest x1 7.93 us: solve(): pl.pallas_call(functools.partial(solve_kernel, narrow), out_shape=jax.Sha...]
  transfers between devices with their start and end apart: 21 -> 20, of which waited for: 7 -> 6; matrix products, arithmetic and copies ran while one was open for 1% -> 1% of each run, Pallas kernels for 21% -> 20%
where the time goes in v6:
time: 68.6 us; the launch traced here: 68.3 us
  starting transfers between devices  32.3 us (47%)
  Pallas kernels  22.5 us (33%)
  waiting for transfers between devices  11.8 us (17%)
  between operations  0.99 us (1%)
    ppermute x3, waiting for transfers between devices, received(): return [lax.ppermute(value, 'narrow', shift_y[d]) for d in range(1, narrow)]  8.81 us
    pallas_call x1, Pallas kernels, solve(): pl.pallas_call(functools.partial(solve_kernel, narrow), out_shape=jax.Sha...  7.93 us
    all_to_all x1, starting transfers between devices, spread(): slots = lax.all_to_all(slots, 'wide', 0, 0, axis_index_groups=z_groups)  7.14 us
    ppermute x4, starting transfers between devices, body(): other = [lax.ppermute(slots, 'wide', swap) for slots in own]  4.98 us
    ppermute x3, starting transfers between devices, body(): lax.ppermute(rows, 'wide', shift_x[d])  4.81 us
    pallas_call x1, Pallas kernels, pick_slots(): pl.pallas_call(pick_kernel, out_shape=(jax.ShapeDtypeStruct((SLOTS, nodes...  4.38 us
    pallas_call x1, Pallas kernels, respond(): pl.pallas_call(respond_kernel, out_shape=jax.ShapeDtypeStruct((rows, coun...  4.29 us
    ppermute x2, starting transfers between devices, body(): lax.ppermute(touched, 'narrow', [(i, i ^ step) for i in range(narrow)])  4.09 us
  transfers between devices with their start and end apart: 20, of which 6 were waited for; matrix products, arithmetic and copies ran while one was open for 1% of the time, Pallas kernels for 20%

profile of v6, /device:TPU:3, one launch (start us, length us, event | category | flops | bytes accessed | tf_op | source)
XLA Modules:
  0.0 68.3 jit_solution(5504532057735248556)
XLA Ops:
  0.0 4.4 %pick_slots.1 = (f32[16,1152]{1,0:T(8,128)S(1)}, f32[16,1152]{1,0:T(8,128)}, f32[16,1152]{1,0:T(8,128)}, f32[16,1152]{1,0:T(8,128)}, s32[8,128]{1,0:T(8,128)S(1)}) custom-call(s32[1,128]{1,0:T(1,128)} %bitcast.11, f32[256,4096]{1,0:T(8,128)} %g_ref.5, f32[4096,128]{1,0:T(8,128)} %change_ref.1), custom_call_target="tpu_custom_call" | custom-call | tf_op jit(solution)/shard_map/pick_slots/pallas_call | solution.py:98
  4.4 1.2 %collective-permute-start.12 = (f32[16,1152]{1,0:T(8,128)}, f32[16,1152]{1,0:T(8,128)S(1)}, u32[]{:S(2)}, u32[]{:S(2)}) collective-permute-start(f32[16,1152]{1,0:T(8,128)} %get-tuple-element.173), channel_id=1, source_target_pairs={{0,8},{4,12},{8,16},{12,20},{16,24},{20,28},{24,0},{28,4},{32,40},... | collective-permute-start | bytes 221192 | tf_op jit(solution)/shard_map/ppermute | solution.py:474
  5.6 0.8 %collective-permute-start.13 = (f32[16,1152]{1,0:T(8,128)}, f32[16,1152]{1,0:T(8,128)S(1)}, u32[]{:S(2)}, u32[]{:S(2)}) collective-permute-start(f32[16,1152]{1,0:T(8,128)} %get-tuple-element.174), channel_id=1, source_target_pairs={{0,16},{4,20},{8,24},{12,28},{16,0},{20,4},{24,8},{28,12},{32,48},... | collective-permute-start | bytes 221192 | tf_op jit(solution)/shard_map/ppermute | solution.py:474
  6.4 2.0 %collective-permute-start.14 = (f32[16,1152]{1,0:T(8,128)}, f32[16,1152]{1,0:T(8,128)S(1)}, u32[]{:S(2)}, u32[]{:S(2)}) collective-permute-start(f32[16,1152]{1,0:T(8,128)} %get-tuple-element.175), channel_id=1, source_target_pairs={{0,24},{4,28},{8,0},{12,4},{16,8},{20,12},{24,16},{28,20},{32,56},... | collective-permute-start | bytes 221192 | tf_op jit(solution)/shard_map/ppermute | solution.py:474
  8.4 1.4 %collective-permute-start.15 = (f32[16,1152]{1,0:T(8,128)S(1)}, f32[16,1152]{1,0:T(8,128)S(1)}, u32[]{:S(2)}, u32[]{:S(2)}) collective-permute-start(f32[16,1152]{1,0:T(8,128)S(1)} %get-tuple-element.172), channel_id=1, source_target_pairs={{0,4},{4,0},{8,12},{12,8},{16,20},{20,16},{24,28},{28,24},{32,36},... | collective-permute-start | bytes 221192 | tf_op jit(solution)/shard_map/ppermute | solution.py:475
  9.8 0.0 collective-permute-done.12
  9.8 0.1 collective-permute-start.16
  10.0 0.7 collective-permute-done.13
  10.6 2.2 %collective-permute-start.17 = (f32[16,1152]{1,0:T(8,128)S(1)}, f32[16,1152]{1,0:T(8,128)S(1)}, u32[]{:S(2)}, u32[]{:S(2)}) collective-permute-start(f32[16,1152]{1,0:T(8,128)S(1)} %collective-permute-done.13), channel_id=1, source_target_pairs={{0,4},{4,0},{8,12},{12,8},{16,20},{20,16},{24,28},{28,24},{32,36},... | collective-permute-start | bytes 221192 | tf_op jit(solution)/shard_map/ppermute | solution.py:475
  12.8 0.0 collective-permute-done.14
  12.8 1.2 %collective-permute-start.18 = (f32[16,1152]{1,0:T(8,128)S(1)}, f32[16,1152]{1,0:T(8,128)S(1)}, u32[]{:S(2)}, u32[]{:S(2)}) collective-permute-start(f32[16,1152]{1,0:T(8,128)S(1)} %collective-permute-done.14), channel_id=1, source_target_pairs={{0,4},{4,0},{8,12},{12,8},{16,20},{20,16},{24,28},{28,24},{32,36},... | collective-permute-start | bytes 221192 | tf_op jit(solution)/shard_map/ppermute | solution.py:475
  14.0 0.5 slice.13
  15.2 0.0 collective-permute-done.15
  15.2 0.0 collective-permute-done.16
  15.2 0.0 collective-permute-done.17
  15.2 0.0 collective-permute-done.18
  15.3 27.2 %conditional.1 = (f32[128,512]{1,0:T(8,128)S(1)}, f32[128,128]{1,0:T(8,128)S(1)}, f32[256,128]{1,0:T(8,128)}, f32[256,128]{1,0:T(8,128)}, f32[256,128]{1,0:T(8,128)}, /*index=5*/f32[256,128]{1,0:T(8,128)}) conditional(s32[]{:T(128)} %bitcast.5, (s32[8,128]{1,0:T(8,128)S(1)}, f32[16,1152]{1,0:T(8,128)S(1)}, f32[16,1152]{1,0:T(8,128)S(1)}, ...), branch_computations={%region_0.1_spmd, %region_1.2_spmd, %region_2.5_spmd} | conditional | flops 852039744 | bytes 34458876 | solution.py:522
  15.3 1.5 %plane_slots.2 = f32[8,24,640]{2,1,0:T(8,128)} custom-call(s32[8,128]{1,0:T(8,128)S(1)} %get-tuple-element.117.table_ref.token_ref, f32[16,1152]{1,0:T(8,128)S(1)} %get-tuple-element.108.refs_0_, f32[16,1152]{1,0:T(8,128)S(1)} %get-tuple-element.109.refs_1_, f32[16,1152]{1,0:T(8,128)S(1)} %get-tuple-element.110.refs_2_, ...), custom_call_target="tpu_custom_call" | custom-call | tf_op jit(solution)/shard_map/cond/branch_0_fun/plane_slots/pallas_call | solution.py:188
  16.8 7.1 %all-to-all-start = ((f32[8,24,640]{2,1,0:T(8,128)}), f32[8,24,640]{2,1,0:T(8,128)S(1)}, u32[]{:S(2)}, u32[]{:S(2)}) async-start(f32[8,24,640]{2,1,0:T(8,128)} %plane_slots.2), calls=%async_computation | async-start | bytes 983040 | tf_op jit(solution)/shard_map/cond/branch_0_fun/all_to_all | solution.py:482
  23.9 4.3 %respond.3 = f32[256,128]{1,0:T(8,128)} custom-call(s32[8,128]{1,0:T(8,128)S(1)} %get-tuple-element.117.table_ref.token_ref, f32[256,4096]{1,0:T(8,128)} %get-tuple-element.118.g_ref, f32[4096,128]{1,0:T(8,128)S(1)} %get-tuple-element.119.change_ref), custom_call_target="tpu_custom_call" | custom-call | flops 800000000 | bytes 8000000 | tf_op jit(solution)/shard_map/cond/branch_0_fun/respond/pallas_call | solution.py:148
  28.2 2.8 %collective-permute-start.2 = (f32[256,128]{1,0:T(8,128)}, f32[256,128]{1,0:T(8,128)}, u32[]{:S(2)}, u32[]{:S(2)}) collective-permute-start(f32[256,128]{1,0:T(8,128)} %respond.3), channel_id=1, source_target_pairs={{0,3},{1,0},{2,1},{3,2},{4,7},{5,4},{6,5},{7,6},{8,11},{9,8},{10,9... | collective-permute-start | bytes 393224 | tf_op jit(solution)/shard_map/cond/branch_0_fun/ppermute | solution.py:472
  31.0 0.4 collective-permute-start.1
  31.4 0.7 %collective-permute-start = (f32[256,128]{1,0:T(8,128)}, f32[256,128]{1,0:T(8,128)}, u32[]{:S(2)}, u32[]{:S(2)}) collective-permute-start(f32[256,128]{1,0:T(8,128)} %respond.3), channel_id=1, source_target_pairs={{0,1},{1,2},{2,3},{3,0},{4,5},{5,6},{6,7},{7,4},{8,9},{9,10},{10,1... | collective-permute-start | bytes 393224 | tf_op jit(solution)/shard_map/cond/branch_0_fun/ppermute | solution.py:472
  32.1 4.2 %collective-permute-done.2 = f32[256,128]{1,0:T(8,128)} collective-permute-done((f32[256,128]{1,0:T(8,128)}, f32[256,128]{1,0:T(8,128)}, u32[]{:S(2)}, u32[]{:S(2)}) %collective-permute-start.2) | collective-permute-done | bytes 131104 | tf_op jit(solution)/shard_map/cond/branch_0_fun/ppermute | solution.py:472
  36.3 0.5 collective-permute-done.1
  36.8 4.1 %collective-permute-done = f32[256,128]{1,0:T(8,128)} collective-permute-done((f32[256,128]{1,0:T(8,128)}, f32[256,128]{1,0:T(8,128)}, u32[]{:S(2)}, u32[]{:S(2)}) %collective-permute-start) | collective-permute-done | bytes 131104 | tf_op jit(solution)/shard_map/cond/branch_0_fun/ppermute | solution.py:472
  40.9 0.3 all-to-all-done
  41.2 1.1 %order_rows.2 = (f32[128,512]{1,0:T(8,128)S(1)}, f32[128,128]{1,0:T(8,128)S(1)}) custom-call(s32[8,128]{1,0:T(8,128)S(1)} %get-tuple-element.117.table_ref.token_ref, f32[192,640]{1,0:T(8,128)S(1)} %bitcast.8), custom_call_target="tpu_custom_call" | custom-call | tf_op jit(solution)/shard_map/cond/branch_0_fun/order_rows/pallas_call | solution.py:215
  42.5 1.4 %collective-permute-start.22 = (f32[128,128]{1,0:T(8,128)S(1)}, f32[128,128]{1,0:T(8,128)S(1)}, u32[]{:S(2)}, u32[]{:S(2)}) collective-permute-start(f32[128,128]{1,0:T(8,128)S(1)} %get-tuple-element.177), channel_id=1, source_target_pairs={{0,1},{1,0},{2,3},{3,2},{4,5},{5,4},{6,7},{7,6},{8,9},{9,8},{10,11... | collective-permute-start | bytes 196616 | tf_op jit(solution)/shard_map/ppermute | solution.py:527
  43.9 1.3 %collective-permute-start.21 = (f32[128,512]{1,0:T(8,128)S(1)}, f32[128,512]{1,0:T(8,128)S(1)}, u32[]{:S(2)}, u32[]{:S(2)}) collective-permute-start(f32[128,512]{1,0:T(8,128)S(1)} %get-tuple-element.183.refs_0_), channel_id=1, source_target_pairs={{0,24},{4,28},{8,0},{12,4},{16,8},{20,12},{24,16},{28,20},{32,56},... | collective-permute-start | bytes 786440 | tf_op jit(solution)/shard_map/ppermute | solution.py:524
  45.1 1.5 %collective-permute-start.20 = (f32[128,512]{1,0:T(8,128)S(1)}, f32[128,512]{1,0:T(8,128)S(1)}, u32[]{:S(2)}, u32[]{:S(2)}) collective-permute-start(f32[128,512]{1,0:T(8,128)S(1)} %get-tuple-element.183.refs_0_), channel_id=1, source_target_pairs={{0,16},{4,20},{8,24},{12,28},{16,0},{20,4},{24,8},{28,12},{32,48},... | collective-permute-start | bytes 786440 | tf_op jit(solution)/shard_map/ppermute | solution.py:524
  46.6 2.1 %collective-permute-start.19 = (f32[128,512]{1,0:T(8,128)S(1)}, f32[128,512]{1,0:T(8,128)S(1)}, u32[]{:S(2)}, u32[]{:S(2)}) collective-permute-start(f32[128,512]{1,0:T(8,128)S(1)} %get-tuple-element.183.refs_0_), channel_id=1, source_target_pairs={{0,8},{4,12},{8,16},{12,20},{16,24},{20,28},{24,0},{28,4},{32,40},... | collective-permute-start | bytes 786440 | tf_op jit(solution)/shard_map/ppermute | solution.py:524
  48.7 0.0 collective-permute-done.22
  48.7 2.7 %collective-permute-start.23 = (f32[128,128]{1,0:T(8,128)S(1)}, f32[128,128]{1,0:T(8,128)S(1)}, u32[]{:S(2)}, u32[]{:S(2)}) collective-permute-start(f32[128,128]{1,0:T(8,128)S(1)} %add.49.refs_0_), channel_id=1, source_target_pairs={{0,2},{1,3},{2,0},{3,1},{4,6},{5,7},{6,4},{7,5},{8,10},{9,11},{10,... | collective-permute-start | bytes 196616 | tf_op jit(solution)/shard_map/ppermute | solution.py:527
  51.4 2.0 %collective-permute-done.23.refs_1_ = f32[128,128]{1,0:T(8,128)S(1)} collective-permute-done((f32[128,128]{1,0:T(8,128)S(1)}, f32[128,128]{1,0:T(8,128)S(1)}, u32[]{:S(2)}, u32[]{:S(2)}) %collective-permute-start.23) | collective-permute-done | bytes 65568 | tf_op jit(solution)/shard_map/ppermute | solution.py:527
  53.4 7.9 %solve.1.left_ref = bf16[256,384]{1,0:T(8,128)(2,1)S(1)} custom-call(f32[128,128]{1,0:T(8,128)S(1)} %add.49.refs_0_, f32[128,128]{1,0:T(8,128)S(1)} %collective-permute-done.23.refs_1_, f32[256,128]{1,0:T(8,128)} %get-tuple-element.178.refs_2_, f32[256,128]{1,0:T(8,128)} %get-tuple-element.179.refs_3_, f32[256,128]{1,0:T(8,128)} %get-tuple-element.180.refs_4_, ...), custom_call_target="tpu_custom_call" | custom-call | flops 2000000000 | bytes 8000000 | tf_op jit(solution)/shard_map/solve/pallas_call | solution.py:377
  61.3 0.0 collective-permute-done.21.refs_3_
  61.3 0.0 collective-permute-done.20.refs_2_
  61.4 0.0 collective-permute-done.19.refs_1_
  61.4 2.8 %collective-permute-start.24 = (f32[128,512]{1,0:T(8,128)S(1)}, f32[128,512]{1,0:T(8,128)S(1)}, u32[]{:S(2)}, u32[]{:S(2)}) collective-permute-start(f32[128,512]{1,0:T(8,128)S(1)} %get-tuple-element.183.refs_0_), channel_id=1, source_target_pairs={{0,4},{4,0},{8,12},{12,8},{16,20},{20,16},{24,28},{28,24},{32,36},... | collective-permute-start | bytes 786440 | tf_op jit(solution)/shard_map/ppermute | solution.py:532
  64.2 0.1 collective-permute-start.25
  64.3 0.4 collective-permute-start.26
  64.7 0.1 collective-permute-start.27
  64.8 1.6 %update_own.1.before_ref = f32[256,4096]{1,0:T(8,128)} custom-call(bf16[256,384]{1,0:T(8,128)(2,1)S(1)} %solve.1.left_ref, f32[256,4096]{1,0:T(8,128)S(1)} %copy-done, f32[128,512]{1,0:T(8,128)S(1)} %get-tuple-element.183.refs_0_, f32[128,512]{1,0:T(8,128)S(1)} %collective-permute-done.19.refs_1_, f32[128,512]{1,0:T(8,128)S(1)} %collective-permute-done.20.refs_2_, ...), custom_call_target="tpu_custom_call" | custom-call | flops 1000000000 | bytes 6000000 | tf_op jit(solution)/shard_map/update_own/pallas_call | solution.py:424
  66.5 0.0 collective-permute-done.24.refs_0_
  66.5 0.0 collective-permute-done.25.refs_1_
  66.5 0.0 collective-permute-done.27.refs_3_
  66.5 1.6 %update_other.1 = f32[256,4096]{1,0:T(8,128)} custom-call(bf16[256,384]{1,0:T(8,128)(2,1)S(1)} %solve.1.left_ref, f32[256,4096]{1,0:T(8,128)S(1)} %copy-done, f32[256,4096]{1,0:T(8,128)} %update_own.1.before_ref, f32[128,512]{1,0:T(8,128)S(1)} %collective-permute-done.24.refs_0_, ...), custom_call_target="tpu_custom_call", output_to_operand_aliasing={{}: (2, {})} | custom-call | tf_op jit(solution)/shard_map/update_other/pallas_call | solution.py:434
  (8 shorter events, 0.0 us)
Async XLA Ops:
  0.0 15.3 %copy-start.1 = (f32[4096,128]{1,0:T(8,128)S(1)}, f32[4096,128]{1,0:T(8,128)}, u32[]{:S(2)}) copy-start(f32[4096,128]{1,0:T(8,128)} %change_ref.1) | copy-start | bytes 6291460
  0.0 15.3 %copy-start.3 = (s32[128]{0:T(128)S(1)}, s32[128]{0:T(128)}, u32[]{:S(2)}) copy-start(s32[128]{0:T(128)} %param.8) | copy-start | bytes 1540
  4.4 5.4 %collective-permute-start.12 = (f32[16,1152]{1,0:T(8,128)}, f32[16,1152]{1,0:T(8,128)S(1)}, u32[]{:S(2)}, u32[]{:S(2)}) collective-permute-start(f32[16,1152]{1,0:T(8,128)} %get-tuple-element.173), channel_id=1, source_target_pairs={{0,8},{4,12},{8,16},{12,20},{16,24},{20,28},{24,0},{28,4},{32,40},... | collective-permute-start | bytes 221192 | tf_op jit(solution)/shard_map/ppermute | solution.py:474
  5.6 5.0 %collective-permute-start.13 = (f32[16,1152]{1,0:T(8,128)}, f32[16,1152]{1,0:T(8,128)S(1)}, u32[]{:S(2)}, u32[]{:S(2)}) collective-permute-start(f32[16,1152]{1,0:T(8,128)} %get-tuple-element.174), channel_id=1, source_target_pairs={{0,16},{4,20},{8,24},{12,28},{16,0},{20,4},{24,8},{28,12},{32,48},... | collective-permute-start | bytes 221192 | tf_op jit(solution)/shard_map/ppermute | solution.py:474
  6.4 6.4 %collective-permute-start.14 = (f32[16,1152]{1,0:T(8,128)}, f32[16,1152]{1,0:T(8,128)S(1)}, u32[]{:S(2)}, u32[]{:S(2)}) collective-permute-start(f32[16,1152]{1,0:T(8,128)} %get-tuple-element.175), channel_id=1, source_target_pairs={{0,24},{4,28},{8,0},{12,4},{16,8},{20,12},{24,16},{28,20},{32,56},... | collective-permute-start | bytes 221192 | tf_op jit(solution)/shard_map/ppermute | solution.py:474
  8.4 6.8 %collective-permute-start.15 = (f32[16,1152]{1,0:T(8,128)S(1)}, f32[16,1152]{1,0:T(8,128)S(1)}, u32[]{:S(2)}, u32[]{:S(2)}) collective-permute-start(f32[16,1152]{1,0:T(8,128)S(1)} %get-tuple-element.172), channel_id=1, source_target_pairs={{0,4},{4,0},{8,12},{12,8},{16,20},{20,16},{24,28},{28,24},{32,36},... | collective-permute-start | bytes 221192 | tf_op jit(solution)/shard_map/ppermute | solution.py:475
  9.8 5.4 %collective-permute-start.16 = (f32[16,1152]{1,0:T(8,128)S(1)}, f32[16,1152]{1,0:T(8,128)S(1)}, u32[]{:S(2)}, u32[]{:S(2)}) collective-permute-start(f32[16,1152]{1,0:T(8,128)S(1)} %collective-permute-done.12), channel_id=1, source_target_pairs={{0,4},{4,0},{8,12},{12,8},{16,20},{20,16},{24,28},{28,24},{32,36},... | collective-permute-start | bytes 221192 | tf_op jit(solution)/shard_map/ppermute | solution.py:475
  10.6 4.6 %collective-permute-start.17 = (f32[16,1152]{1,0:T(8,128)S(1)}, f32[16,1152]{1,0:T(8,128)S(1)}, u32[]{:S(2)}, u32[]{:S(2)}) collective-permute-start(f32[16,1152]{1,0:T(8,128)S(1)} %collective-permute-done.13), channel_id=1, source_target_pairs={{0,4},{4,0},{8,12},{12,8},{16,20},{20,16},{24,28},{28,24},{32,36},... | collective-permute-start | bytes 221192 | tf_op jit(solution)/shard_map/ppermute | solution.py:475
  12.8 2.4 %collective-permute-start.18 = (f32[16,1152]{1,0:T(8,128)S(1)}, f32[16,1152]{1,0:T(8,128)S(1)}, u32[]{:S(2)}, u32[]{:S(2)}) collective-permute-start(f32[16,1152]{1,0:T(8,128)S(1)} %collective-permute-done.14), channel_id=1, source_target_pairs={{0,4},{4,0},{8,12},{12,8},{16,20},{20,16},{24,28},{28,24},{32,36},... | collective-permute-start | bytes 221192 | tf_op jit(solution)/shard_map/ppermute | solution.py:475
  16.8 24.4 %all-to-all-start = ((f32[8,24,640]{2,1,0:T(8,128)}), f32[8,24,640]{2,1,0:T(8,128)S(1)}, u32[]{:S(2)}, u32[]{:S(2)}) async-start(f32[8,24,640]{2,1,0:T(8,128)} %plane_slots.2), calls=%async_computation | async-start | bytes 983040 | tf_op jit(solution)/shard_map/cond/branch_0_fun/all_to_all | solution.py:482
  28.2 8.1 %collective-permute-start.2 = (f32[256,128]{1,0:T(8,128)}, f32[256,128]{1,0:T(8,128)}, u32[]{:S(2)}, u32[]{:S(2)}) collective-permute-start(f32[256,128]{1,0:T(8,128)} %respond.3), channel_id=1, source_target_pairs={{0,3},{1,0},{2,1},{3,2},{4,7},{5,4},{6,5},{7,6},{8,11},{9,8},{10,9... | collective-permute-start | bytes 393224 | tf_op jit(solution)/shard_map/cond/branch_0_fun/ppermute | solution.py:472
  31.0 5.7 %collective-permute-start.1 = (f32[256,128]{1,0:T(8,128)}, f32[256,128]{1,0:T(8,128)}, u32[]{:S(2)}, u32[]{:S(2)}) collective-permute-start(f32[256,128]{1,0:T(8,128)} %respond.3), channel_id=1, source_target_pairs={{0,2},{1,3},{2,0},{3,1},{4,6},{5,7},{6,4},{7,5},{8,10},{9,11},{10,... | collective-permute-start | bytes 393224 | tf_op jit(solution)/shard_map/cond/branch_0_fun/ppermute | solution.py:472
  31.4 9.5 %collective-permute-start = (f32[256,128]{1,0:T(8,128)}, f32[256,128]{1,0:T(8,128)}, u32[]{:S(2)}, u32[]{:S(2)}) collective-permute-start(f32[256,128]{1,0:T(8,128)} %respond.3), channel_id=1, source_target_pairs={{0,1},{1,2},{2,3},{3,0},{4,5},{5,6},{6,7},{7,4},{8,9},{9,10},{10,1... | collective-permute-start | bytes 393224 | tf_op jit(solution)/shard_map/cond/branch_0_fun/ppermute | solution.py:472
  42.5 6.2 %collective-permute-start.22 = (f32[128,128]{1,0:T(8,128)S(1)}, f32[128,128]{1,0:T(8,128)S(1)}, u32[]{:S(2)}, u32[]{:S(2)}) collective-permute-start(f32[128,128]{1,0:T(8,128)S(1)} %get-tuple-element.177), channel_id=1, source_target_pairs={{0,1},{1,0},{2,3},{3,2},{4,5},{5,4},{6,7},{7,6},{8,9},{9,8},{10,11... | collective-permute-start | bytes 196616 | tf_op jit(solution)/shard_map/ppermute | solution.py:527
  43.9 17.5 %collective-permute-start.21 = (f32[128,512]{1,0:T(8,128)S(1)}, f32[128,512]{1,0:T(8,128)S(1)}, u32[]{:S(2)}, u32[]{:S(2)}) collective-permute-start(f32[128,512]{1,0:T(8,128)S(1)} %get-tuple-element.183.refs_0_), channel_id=1, source_target_pairs={{0,24},{4,28},{8,0},{12,4},{16,8},{20,12},{24,16},{28,20},{32,56},... | collective-permute-start | bytes 786440 | tf_op jit(solution)/shard_map/ppermute | solution.py:524
  45.1 16.2 %collective-permute-start.20 = (f32[128,512]{1,0:T(8,128)S(1)}, f32[128,512]{1,0:T(8,128)S(1)}, u32[]{:S(2)}, u32[]{:S(2)}) collective-permute-start(f32[128,512]{1,0:T(8,128)S(1)} %get-tuple-element.183.refs_0_), channel_id=1, source_target_pairs={{0,16},{4,20},{8,24},{12,28},{16,0},{20,4},{24,8},{28,12},{32,48},... | collective-permute-start | bytes 786440 | tf_op jit(solution)/shard_map/ppermute | solution.py:524
  46.6 14.8 %collective-permute-start.19 = (f32[128,512]{1,0:T(8,128)S(1)}, f32[128,512]{1,0:T(8,128)S(1)}, u32[]{:S(2)}, u32[]{:S(2)}) collective-permute-start(f32[128,512]{1,0:T(8,128)S(1)} %get-tuple-element.183.refs_0_), channel_id=1, source_target_pairs={{0,8},{4,12},{8,16},{12,20},{16,24},{20,28},{24,0},{28,4},{32,40},... | collective-permute-start | bytes 786440 | tf_op jit(solution)/shard_map/ppermute | solution.py:524
  48.7 4.7 %collective-permute-start.23 = (f32[128,128]{1,0:T(8,128)S(1)}, f32[128,128]{1,0:T(8,128)S(1)}, u32[]{:S(2)}, u32[]{:S(2)}) collective-permute-start(f32[128,128]{1,0:T(8,128)S(1)} %add.49.refs_0_), channel_id=1, source_target_pairs={{0,2},{1,3},{2,0},{3,1},{4,6},{5,7},{6,4},{7,5},{8,10},{9,11},{10,... | collective-permute-start | bytes 196616 | tf_op jit(solution)/shard_map/ppermute | solution.py:527
  53.4 11.4 %copy-start = (f32[256,4096]{1,0:T(8,128)S(1)}, f32[256,4096]{1,0:T(8,128)}, u32[]{:S(2)}) copy-start(f32[256,4096]{1,0:T(8,128)} %g_ref.5) | copy-start | bytes 12582916
  61.4 5.1 %collective-permute-start.24 = (f32[128,512]{1,0:T(8,128)S(1)}, f32[128,512]{1,0:T(8,128)S(1)}, u32[]{:S(2)}, u32[]{:S(2)}) collective-permute-start(f32[128,512]{1,0:T(8,128)S(1)} %get-tuple-element.183.refs_0_), channel_id=1, source_target_pairs={{0,4},{4,0},{8,12},{12,8},{16,20},{20,16},{24,28},{28,24},{32,36},... | collective-permute-start | bytes 786440 | tf_op jit(solution)/shard_map/ppermute | solution.py:532
  64.2 2.3 %collective-permute-start.25 = (f32[128,512]{1,0:T(8,128)S(1)}, f32[128,512]{1,0:T(8,128)S(1)}, u32[]{:S(2)}, u32[]{:S(2)}) collective-permute-start(f32[128,512]{1,0:T(8,128)S(1)} %collective-permute-done.19.refs_1_), channel_id=1, source_target_pairs={{0,4},{4,0},{8,12},{12,8},{16,20},{20,16},{24,28},{28,24},{32,36},... | collective-permute-start | bytes 786440 | tf_op jit(solution)/shard_map/ppermute | solution.py:532
  64.3 2.2 %collective-permute-start.26 = (f32[128,512]{1,0:T(8,128)S(1)}, f32[128,512]{1,0:T(8,128)S(1)}, u32[]{:S(2)}, u32[]{:S(2)}) collective-permute-start(f32[128,512]{1,0:T(8,128)S(1)} %collective-permute-done.20.refs_2_), channel_id=1, source_target_pairs={{0,4},{4,0},{8,12},{12,8},{16,20},{20,16},{24,28},{28,24},{32,36},... | collective-permute-start | bytes 786440 | tf_op jit(solution)/shard_map/ppermute | solution.py:532
  64.7 1.8 %collective-permute-start.27 = (f32[128,512]{1,0:T(8,128)S(1)}, f32[128,512]{1,0:T(8,128)S(1)}, u32[]{:S(2)}, u32[]{:S(2)}) collective-permute-start(f32[128,512]{1,0:T(8,128)S(1)} %collective-permute-done.21.refs_3_), channel_id=1, source_target_pairs={{0,4},{4,0},{8,12},{12,8},{16,20},{20,16},{24,28},{28,24},{32,36},... | collective-permute-start | bytes 786440 | tf_op jit(solution)/shard_map/ppermute | solution.py:532

commit v7 on v6

--- a/solution.py
+++ b/solution.py
@@ -157,7 +157,7 @@
             pltpu.SemaphoreType.DMA((chunks,)),
         ],
         cost_estimate=pl.CostEstimate(flops=800_000_000, bytes_accessed=8_000_000, transcendentals=0),
-        compiler_params=pltpu.CompilerParams(vmem_limit_bytes=24 * 1024 * 1024),
+        compiler_params=pltpu.CompilerParams(vmem_limit_bytes=60 * 1024 * 1024),
         name="respond",
     )(token, gebhart, change)
 
@@ -524,7 +524,7 @@
     pieces = [rows] + [lax.ppermute(rows, "wide", shift_x[d]) for d in range(1, XS)]
     step = 1
     while step < narrow:
-        parts = [touched, lax.ppermute(touched, "narrow", [(i, i ^ step) for i in range(narrow)])]
+        parts = [touched, lax.ppermute(touched, "narrow", [(i, i ^ (2 * step - 1)) for i in range(narrow)])]
         touched = parts[0] + parts[1]
         step *= 2
     left = solve(parts, response)

time: 68.6 us -> 68.2 us (level)
  starting transfers between devices: 32.3 us -> 31.6 us
    ppermute x2, starting transfers between devices: 4.09 us -> 3.37 us  [body(): lax.ppermute(touched, 'narrow', [(i, i ^ 2 * step - 1) for i in range(nar...]
where the time goes in v7:
time: 68.2 us; the launch traced here: 68 us
  starting transfers between devices  31.6 us (46%)
  Pallas kernels  22.4 us (33%)
  waiting for transfers between devices  12.3 us (18%)
  between operations  0.99 us (1%)
    ppermute x3, waiting for transfers between devices, received(): return [lax.ppermute(value, 'narrow', shift_y[d]) for d in range(1, narrow)]  8.81 us
    pallas_call x1, Pallas kernels, solve(): pl.pallas_call(functools.partial(solve_kernel, narrow), out_shape=jax.Sha...  7.93 us
    all_to_all x1, starting transfers between devices, spread(): slots = lax.all_to_all(slots, 'wide', 0, 0, axis_index_groups=z_groups)  7.24 us
    ppermute x4, starting transfers between devices, body(): other = [lax.ppermute(slots, 'wide', swap) for slots in own]  4.85 us
    ppermute x3, starting transfers between devices, body(): lax.ppermute(rows, 'wide', shift_x[d])  4.77 us
    pallas_call x1, Pallas kernels, pick_slots(): pl.pallas_call(pick_kernel, out_shape=(jax.ShapeDtypeStruct((SLOTS, nodes...  4.31 us
    pallas_call x1, Pallas kernels, respond(): pl.pallas_call(respond_kernel, out_shape=jax.ShapeDtypeStruct((rows, coun...  4.3 us
    ppermute x3, starting transfers between devices, body(): lax.ppermute(picked[d], 'wide', shift_x[d])  4.06 us
  transfers between devices with their start and end apart: 20, of which 6 were waited for; matrix products, arithmetic and copies ran while one was open for 1% of the time, Pallas kernels for 20%

profile of v7, /device:TPU:3, one launch (start us, length us, event | category | flops | bytes accessed | tf_op | source)
XLA Modules:
  0.0 68.0 jit_solution(11730529365202360463)
XLA Ops:
  0.0 4.3 %pick_slots.1 = (f32[16,1152]{1,0:T(8,128)S(1)}, f32[16,1152]{1,0:T(8,128)}, f32[16,1152]{1,0:T(8,128)}, f32[16,1152]{1,0:T(8,128)}, s32[8,128]{1,0:T(8,128)S(1)}) custom-call(s32[1,128]{1,0:T(1,128)} %bitcast.11, f32[256,4096]{1,0:T(8,128)} %g_ref.5, f32[4096,128]{1,0:T(8,128)} %change_ref.1), custom_call_target="tpu_custom_call" | custom-call | tf_op jit(solution)/shard_map/pick_slots/pallas_call | solution.py:98
  4.3 1.3 %collective-permute-start.12 = (f32[16,1152]{1,0:T(8,128)}, f32[16,1152]{1,0:T(8,128)S(1)}, u32[]{:S(2)}, u32[]{:S(2)}) collective-permute-start(f32[16,1152]{1,0:T(8,128)} %get-tuple-element.173), channel_id=1, source_target_pairs={{0,8},{4,12},{8,16},{12,20},{16,24},{20,28},{24,0},{28,4},{32,40},... | collective-permute-start | bytes 221192 | tf_op jit(solution)/shard_map/ppermute | solution.py:474
  5.6 0.8 %collective-permute-start.13 = (f32[16,1152]{1,0:T(8,128)}, f32[16,1152]{1,0:T(8,128)S(1)}, u32[]{:S(2)}, u32[]{:S(2)}) collective-permute-start(f32[16,1152]{1,0:T(8,128)} %get-tuple-element.174), channel_id=1, source_target_pairs={{0,16},{4,20},{8,24},{12,28},{16,0},{20,4},{24,8},{28,12},{32,48},... | collective-permute-start | bytes 221192 | tf_op jit(solution)/shard_map/ppermute | solution.py:474
  6.4 2.0 %collective-permute-start.14 = (f32[16,1152]{1,0:T(8,128)}, f32[16,1152]{1,0:T(8,128)S(1)}, u32[]{:S(2)}, u32[]{:S(2)}) collective-permute-start(f32[16,1152]{1,0:T(8,128)} %get-tuple-element.175), channel_id=1, source_target_pairs={{0,24},{4,28},{8,0},{12,4},{16,8},{20,12},{24,16},{28,20},{32,56},... | collective-permute-start | bytes 221192 | tf_op jit(solution)/shard_map/ppermute | solution.py:474
  8.4 1.4 %collective-permute-start.15 = (f32[16,1152]{1,0:T(8,128)S(1)}, f32[16,1152]{1,0:T(8,128)S(1)}, u32[]{:S(2)}, u32[]{:S(2)}) collective-permute-start(f32[16,1152]{1,0:T(8,128)S(1)} %get-tuple-element.172), channel_id=1, source_target_pairs={{0,4},{4,0},{8,12},{12,8},{16,20},{20,16},{24,28},{28,24},{32,36},... | collective-permute-start | bytes 221192 | tf_op jit(solution)/shard_map/ppermute | solution.py:475
  9.8 0.0 collective-permute-done.12
  9.8 0.1 collective-permute-start.16
  9.9 0.7 %collective-permute-done.13 = f32[16,1152]{1,0:T(8,128)S(1)} collective-permute-done((f32[16,1152]{1,0:T(8,128)}, f32[16,1152]{1,0:T(8,128)S(1)}, u32[]{:S(2)}, u32[]{:S(2)}) %collective-permute-start.13) | collective-permute-done | bytes 73760 | tf_op jit(solution)/shard_map/ppermute | solution.py:474
  10.6 2.2 %collective-permute-start.17 = (f32[16,1152]{1,0:T(8,128)S(1)}, f32[16,1152]{1,0:T(8,128)S(1)}, u32[]{:S(2)}, u32[]{:S(2)}) collective-permute-start(f32[16,1152]{1,0:T(8,128)S(1)} %collective-permute-done.13), channel_id=1, source_target_pairs={{0,4},{4,0},{8,12},{12,8},{16,20},{20,16},{24,28},{28,24},{32,36},... | collective-permute-start | bytes 221192 | tf_op jit(solution)/shard_map/ppermute | solution.py:475
  12.8 0.0 collective-permute-done.14
  12.8 1.2 %collective-permute-start.18 = (f32[16,1152]{1,0:T(8,128)S(1)}, f32[16,1152]{1,0:T(8,128)S(1)}, u32[]{:S(2)}, u32[]{:S(2)}) collective-permute-start(f32[16,1152]{1,0:T(8,128)S(1)} %collective-permute-done.14), channel_id=1, source_target_pairs={{0,4},{4,0},{8,12},{12,8},{16,20},{20,16},{24,28},{28,24},{32,36},... | collective-permute-start | bytes 221192 | tf_op jit(solution)/shard_map/ppermute | solution.py:475
  14.0 0.5 slice.13
  15.1 0.0 collective-permute-done.15
  15.2 0.0 collective-permute-done.16
  15.2 0.0 collective-permute-done.17
  15.2 0.0 collective-permute-done.18
  15.2 27.3 %conditional.1 = (f32[128,512]{1,0:T(8,128)S(1)}, f32[128,128]{1,0:T(8,128)S(1)}, f32[256,128]{1,0:T(8,128)}, f32[256,128]{1,0:T(8,128)}, f32[256,128]{1,0:T(8,128)}, /*index=5*/f32[256,128]{1,0:T(8,128)}) conditional(s32[]{:T(128)} %bitcast.5, (s32[8,128]{1,0:T(8,128)S(1)}, f32[16,1152]{1,0:T(8,128)S(1)}, f32[16,1152]{1,0:T(8,128)S(1)}, ...), branch_computations={%region_0.1_spmd, %region_1.2_spmd, %region_2.5_spmd} | conditional | flops 852039744 | bytes 34458876 | solution.py:522
  15.2 1.5 %plane_slots.2 = f32[8,24,640]{2,1,0:T(8,128)} custom-call(s32[8,128]{1,0:T(8,128)S(1)} %get-tuple-element.117.table_ref.token_ref, f32[16,1152]{1,0:T(8,128)S(1)} %get-tuple-element.108.refs_0_, f32[16,1152]{1,0:T(8,128)S(1)} %get-tuple-element.109.refs_1_, f32[16,1152]{1,0:T(8,128)S(1)} %get-tuple-element.110.refs_2_, ...), custom_call_target="tpu_custom_call" | custom-call | tf_op jit(solution)/shard_map/cond/branch_0_fun/plane_slots/pallas_call | solution.py:188
  16.7 7.2 %all-to-all-start = ((f32[8,24,640]{2,1,0:T(8,128)}), f32[8,24,640]{2,1,0:T(8,128)S(1)}, u32[]{:S(2)}, u32[]{:S(2)}) async-start(f32[8,24,640]{2,1,0:T(8,128)} %plane_slots.2), calls=%async_computation | async-start | bytes 983040 | tf_op jit(solution)/shard_map/cond/branch_0_fun/all_to_all | solution.py:482
  23.9 4.3 %respond.3 = f32[256,128]{1,0:T(8,128)} custom-call(s32[8,128]{1,0:T(8,128)S(1)} %get-tuple-element.117.table_ref.token_ref, f32[256,4096]{1,0:T(8,128)} %get-tuple-element.118.g_ref, f32[4096,128]{1,0:T(8,128)S(1)} %get-tuple-element.119.change_ref), custom_call_target="tpu_custom_call" | custom-call | flops 800000000 | bytes 8000000 | tf_op jit(solution)/shard_map/cond/branch_0_fun/respond/pallas_call | solution.py:148
  28.2 2.8 %collective-permute-start.2 = (f32[256,128]{1,0:T(8,128)}, f32[256,128]{1,0:T(8,128)}, u32[]{:S(2)}, u32[]{:S(2)}) collective-permute-start(f32[256,128]{1,0:T(8,128)} %respond.3), channel_id=1, source_target_pairs={{0,3},{1,0},{2,1},{3,2},{4,7},{5,4},{6,5},{7,6},{8,11},{9,8},{10,9... | collective-permute-start | bytes 393224 | tf_op jit(solution)/shard_map/cond/branch_0_fun/ppermute | solution.py:472
  31.1 0.4 collective-permute-start.1
  31.4 0.7 %collective-permute-start = (f32[256,128]{1,0:T(8,128)}, f32[256,128]{1,0:T(8,128)}, u32[]{:S(2)}, u32[]{:S(2)}) collective-permute-start(f32[256,128]{1,0:T(8,128)} %respond.3), channel_id=1, source_target_pairs={{0,1},{1,2},{2,3},{3,0},{4,5},{5,6},{6,7},{7,4},{8,9},{9,10},{10,1... | collective-permute-start | bytes 393224 | tf_op jit(solution)/shard_map/cond/branch_0_fun/ppermute | solution.py:472
  32.1 4.2 %collective-permute-done.2 = f32[256,128]{1,0:T(8,128)} collective-permute-done((f32[256,128]{1,0:T(8,128)}, f32[256,128]{1,0:T(8,128)}, u32[]{:S(2)}, u32[]{:S(2)}) %collective-permute-start.2) | collective-permute-done | bytes 131104 | tf_op jit(solution)/shard_map/cond/branch_0_fun/ppermute | solution.py:472
  36.3 0.5 collective-permute-done.1
  36.8 4.1 %collective-permute-done = f32[256,128]{1,0:T(8,128)} collective-permute-done((f32[256,128]{1,0:T(8,128)}, f32[256,128]{1,0:T(8,128)}, u32[]{:S(2)}, u32[]{:S(2)}) %collective-permute-start) | collective-permute-done | bytes 131104 | tf_op jit(solution)/shard_map/cond/branch_0_fun/ppermute | solution.py:472
  40.9 0.3 all-to-all-done
  41.2 1.1 %order_rows.2 = (f32[128,512]{1,0:T(8,128)S(1)}, f32[128,128]{1,0:T(8,128)S(1)}) custom-call(s32[8,128]{1,0:T(8,128)S(1)} %get-tuple-element.117.table_ref.token_ref, f32[192,640]{1,0:T(8,128)S(1)} %bitcast.8), custom_call_target="tpu_custom_call" | custom-call | tf_op jit(solution)/shard_map/cond/branch_0_fun/order_rows/pallas_call | solution.py:215
  42.5 1.4 %collective-permute-start.22 = (f32[128,128]{1,0:T(8,128)S(1)}, f32[128,128]{1,0:T(8,128)S(1)}, u32[]{:S(2)}, u32[]{:S(2)}) collective-permute-start(f32[128,128]{1,0:T(8,128)S(1)} %get-tuple-element.177), channel_id=1, source_target_pairs={{0,1},{1,0},{2,3},{3,2},{4,5},{5,4},{6,7},{7,6},{8,9},{9,8},{10,11... | collective-permute-start | bytes 196616 | tf_op jit(solution)/shard_map/ppermute | solution.py:527
  43.9 1.2 %collective-permute-start.21 = (f32[128,512]{1,0:T(8,128)S(1)}, f32[128,512]{1,0:T(8,128)S(1)}, u32[]{:S(2)}, u32[]{:S(2)}) collective-permute-start(f32[128,512]{1,0:T(8,128)S(1)} %get-tuple-element.183.refs_0_), channel_id=1, source_target_pairs={{0,24},{4,28},{8,0},{12,4},{16,8},{20,12},{24,16},{28,20},{32,56},... | collective-permute-start | bytes 786440 | tf_op jit(solution)/shard_map/ppermute | solution.py:524
  45.1 1.5 %collective-permute-start.20 = (f32[128,512]{1,0:T(8,128)S(1)}, f32[128,512]{1,0:T(8,128)S(1)}, u32[]{:S(2)}, u32[]{:S(2)}) collective-permute-start(f32[128,512]{1,0:T(8,128)S(1)} %get-tuple-element.183.refs_0_), channel_id=1, source_target_pairs={{0,16},{4,20},{8,24},{12,28},{16,0},{20,4},{24,8},{28,12},{32,48},... | collective-permute-start | bytes 786440 | tf_op jit(solution)/shard_map/ppermute | solution.py:524
  46.6 2.1 %collective-permute-start.19 = (f32[128,512]{1,0:T(8,128)S(1)}, f32[128,512]{1,0:T(8,128)S(1)}, u32[]{:S(2)}, u32[]{:S(2)}) collective-permute-start(f32[128,512]{1,0:T(8,128)S(1)} %get-tuple-element.183.refs_0_), channel_id=1, source_target_pairs={{0,8},{4,12},{8,16},{12,20},{16,24},{20,28},{24,0},{28,4},{32,40},... | collective-permute-start | bytes 786440 | tf_op jit(solution)/shard_map/ppermute | solution.py:524
  48.7 0.0 collective-permute-done.22
  48.7 2.0 %collective-permute-start.23 = (f32[128,128]{1,0:T(8,128)S(1)}, f32[128,128]{1,0:T(8,128)S(1)}, u32[]{:S(2)}, u32[]{:S(2)}) collective-permute-start(f32[128,128]{1,0:T(8,128)S(1)} %add.49.refs_0_), channel_id=1, source_target_pairs={{0,3},{1,2},{2,1},{3,0},{4,7},{5,6},{6,5},{7,4},{8,11},{9,10},{10,... | collective-permute-start | bytes 196616 | tf_op jit(solution)/shard_map/ppermute | solution.py:527
  50.7 2.4 %collective-permute-done.23.refs_1_ = f32[128,128]{1,0:T(8,128)S(1)} collective-permute-done((f32[128,128]{1,0:T(8,128)S(1)}, f32[128,128]{1,0:T(8,128)S(1)}, u32[]{:S(2)}, u32[]{:S(2)}) %collective-permute-start.23) | collective-permute-done | bytes 65568 | tf_op jit(solution)/shard_map/ppermute | solution.py:527
  53.1 7.9 %solve.1.left_ref = bf16[256,384]{1,0:T(8,128)(2,1)S(1)} custom-call(f32[128,128]{1,0:T(8,128)S(1)} %add.49.refs_0_, f32[128,128]{1,0:T(8,128)S(1)} %collective-permute-done.23.refs_1_, f32[256,128]{1,0:T(8,128)} %get-tuple-element.178.refs_2_, f32[256,128]{1,0:T(8,128)} %get-tuple-element.179.refs_3_, f32[256,128]{1,0:T(8,128)} %get-tuple-element.180.refs_4_, ...), custom_call_target="tpu_custom_call" | custom-call | flops 2000000000 | bytes 8000000 | tf_op jit(solution)/shard_map/solve/pallas_call | solution.py:377
  61.0 0.0 collective-permute-done.21.refs_3_
  61.0 0.0 collective-permute-done.20.refs_2_
  61.1 0.0 collective-permute-done.19.refs_1_
  61.1 2.8 %collective-permute-start.24 = (f32[128,512]{1,0:T(8,128)S(1)}, f32[128,512]{1,0:T(8,128)S(1)}, u32[]{:S(2)}, u32[]{:S(2)}) collective-permute-start(f32[128,512]{1,0:T(8,128)S(1)} %get-tuple-element.183.refs_0_), channel_id=1, source_target_pairs={{0,4},{4,0},{8,12},{12,8},{16,20},{20,16},{24,28},{28,24},{32,36},... | collective-permute-start | bytes 786440 | tf_op jit(solution)/shard_map/ppermute | solution.py:532
  63.9 0.1 collective-permute-start.25
  64.0 0.4 collective-permute-start.26
  64.4 0.1 collective-permute-start.27
  64.5 1.6 %update_own.1.before_ref = f32[256,4096]{1,0:T(8,128)} custom-call(bf16[256,384]{1,0:T(8,128)(2,1)S(1)} %solve.1.left_ref, f32[256,4096]{1,0:T(8,128)S(1)} %copy-done, f32[128,512]{1,0:T(8,128)S(1)} %get-tuple-element.183.refs_0_, f32[128,512]{1,0:T(8,128)S(1)} %collective-permute-done.19.refs_1_, f32[128,512]{1,0:T(8,128)S(1)} %collective-permute-done.20.refs_2_, ...), custom_call_target="tpu_custom_call" | custom-call | flops 1000000000 | bytes 6000000 | tf_op jit(solution)/shard_map/update_own/pallas_call | solution.py:424
  66.2 0.0 collective-permute-done.24.refs_0_
  66.2 0.0 collective-permute-done.25.refs_1_
  66.2 0.0 collective-permute-done.27.refs_3_
  66.2 1.6 %update_other.1 = f32[256,4096]{1,0:T(8,128)} custom-call(bf16[256,384]{1,0:T(8,128)(2,1)S(1)} %solve.1.left_ref, f32[256,4096]{1,0:T(8,128)S(1)} %copy-done, f32[256,4096]{1,0:T(8,128)} %update_own.1.before_ref, f32[128,512]{1,0:T(8,128)S(1)} %collective-permute-done.24.refs_0_, ...), custom_call_target="tpu_custom_call", output_to_operand_aliasing={{}: (2, {})} | custom-call | tf_op jit(solution)/shard_map/update_other/pallas_call | solution.py:434
  (8 shorter events, 0.0 us)
Async XLA Ops:
  0.0 15.2 %copy-start.1 = (f32[4096,128]{1,0:T(8,128)S(1)}, f32[4096,128]{1,0:T(8,128)}, u32[]{:S(2)}) copy-start(f32[4096,128]{1,0:T(8,128)} %change_ref.1) | copy-start | bytes 6291460
  0.0 15.2 %copy-start.3 = (s32[128]{0:T(128)S(1)}, s32[128]{0:T(128)}, u32[]{:S(2)}) copy-start(s32[128]{0:T(128)} %param.8) | copy-start | bytes 1540
  4.3 5.4 %collective-permute-start.12 = (f32[16,1152]{1,0:T(8,128)}, f32[16,1152]{1,0:T(8,128)S(1)}, u32[]{:S(2)}, u32[]{:S(2)}) collective-permute-start(f32[16,1152]{1,0:T(8,128)} %get-tuple-element.173), channel_id=1, source_target_pairs={{0,8},{4,12},{8,16},{12,20},{16,24},{20,28},{24,0},{28,4},{32,40},... | collective-permute-start | bytes 221192 | tf_op jit(solution)/shard_map/ppermute | solution.py:474
  5.6 5.0 %collective-permute-start.13 = (f32[16,1152]{1,0:T(8,128)}, f32[16,1152]{1,0:T(8,128)S(1)}, u32[]{:S(2)}, u32[]{:S(2)}) collective-permute-start(f32[16,1152]{1,0:T(8,128)} %get-tuple-element.174), channel_id=1, source_target_pairs={{0,16},{4,20},{8,24},{12,28},{16,0},{20,4},{24,8},{28,12},{32,48},... | collective-permute-start | bytes 221192 | tf_op jit(solution)/shard_map/ppermute | solution.py:474
  6.4 6.4 %collective-permute-start.14 = (f32[16,1152]{1,0:T(8,128)}, f32[16,1152]{1,0:T(8,128)S(1)}, u32[]{:S(2)}, u32[]{:S(2)}) collective-permute-start(f32[16,1152]{1,0:T(8,128)} %get-tuple-element.175), channel_id=1, source_target_pairs={{0,24},{4,28},{8,0},{12,4},{16,8},{20,12},{24,16},{28,20},{32,56},... | collective-permute-start | bytes 221192 | tf_op jit(solution)/shard_map/ppermute | solution.py:474
  8.4 6.8 %collective-permute-start.15 = (f32[16,1152]{1,0:T(8,128)S(1)}, f32[16,1152]{1,0:T(8,128)S(1)}, u32[]{:S(2)}, u32[]{:S(2)}) collective-permute-start(f32[16,1152]{1,0:T(8,128)S(1)} %get-tuple-element.172), channel_id=1, source_target_pairs={{0,4},{4,0},{8,12},{12,8},{16,20},{20,16},{24,28},{28,24},{32,36},... | collective-permute-start | bytes 221192 | tf_op jit(solution)/shard_map/ppermute | solution.py:475
  9.8 5.4 %collective-permute-start.16 = (f32[16,1152]{1,0:T(8,128)S(1)}, f32[16,1152]{1,0:T(8,128)S(1)}, u32[]{:S(2)}, u32[]{:S(2)}) collective-permute-start(f32[16,1152]{1,0:T(8,128)S(1)} %collective-permute-done.12), channel_id=1, source_target_pairs={{0,4},{4,0},{8,12},{12,8},{16,20},{20,16},{24,28},{28,24},{32,36},... | collective-permute-start | bytes 221192 | tf_op jit(solution)/shard_map/ppermute | solution.py:475
  10.6 4.5 %collective-permute-start.17 = (f32[16,1152]{1,0:T(8,128)S(1)}, f32[16,1152]{1,0:T(8,128)S(1)}, u32[]{:S(2)}, u32[]{:S(2)}) collective-permute-start(f32[16,1152]{1,0:T(8,128)S(1)} %collective-permute-done.13), channel_id=1, source_target_pairs={{0,4},{4,0},{8,12},{12,8},{16,20},{20,16},{24,28},{28,24},{32,36},... | collective-permute-start | bytes 221192 | tf_op jit(solution)/shard_map/ppermute | solution.py:475
  12.8 2.4 %collective-permute-start.18 = (f32[16,1152]{1,0:T(8,128)S(1)}, f32[16,1152]{1,0:T(8,128)S(1)}, u32[]{:S(2)}, u32[]{:S(2)}) collective-permute-start(f32[16,1152]{1,0:T(8,128)S(1)} %collective-permute-done.14), channel_id=1, source_target_pairs={{0,4},{4,0},{8,12},{12,8},{16,20},{20,16},{24,28},{28,24},{32,36},... | collective-permute-start | bytes 221192 | tf_op jit(solution)/shard_map/ppermute | solution.py:475
  16.7 24.5 %all-to-all-start = ((f32[8,24,640]{2,1,0:T(8,128)}), f32[8,24,640]{2,1,0:T(8,128)S(1)}, u32[]{:S(2)}, u32[]{:S(2)}) async-start(f32[8,24,640]{2,1,0:T(8,128)} %plane_slots.2), calls=%async_computation | async-start | bytes 983040 | tf_op jit(solution)/shard_map/cond/branch_0_fun/all_to_all | solution.py:482
  28.2 8.1 %collective-permute-start.2 = (f32[256,128]{1,0:T(8,128)}, f32[256,128]{1,0:T(8,128)}, u32[]{:S(2)}, u32[]{:S(2)}) collective-permute-start(f32[256,128]{1,0:T(8,128)} %respond.3), channel_id=1, source_target_pairs={{0,3},{1,0},{2,1},{3,2},{4,7},{5,4},{6,5},{7,6},{8,11},{9,8},{10,9... | collective-permute-start | bytes 393224 | tf_op jit(solution)/shard_map/cond/branch_0_fun/ppermute | solution.py:472
  31.1 5.7 %collective-permute-start.1 = (f32[256,128]{1,0:T(8,128)}, f32[256,128]{1,0:T(8,128)}, u32[]{:S(2)}, u32[]{:S(2)}) collective-permute-start(f32[256,128]{1,0:T(8,128)} %respond.3), channel_id=1, source_target_pairs={{0,2},{1,3},{2,0},{3,1},{4,6},{5,7},{6,4},{7,5},{8,10},{9,11},{10,... | collective-permute-start | bytes 393224 | tf_op jit(solution)/shard_map/cond/branch_0_fun/ppermute | solution.py:472
  31.4 9.5 %collective-permute-start = (f32[256,128]{1,0:T(8,128)}, f32[256,128]{1,0:T(8,128)}, u32[]{:S(2)}, u32[]{:S(2)}) collective-permute-start(f32[256,128]{1,0:T(8,128)} %respond.3), channel_id=1, source_target_pairs={{0,1},{1,2},{2,3},{3,0},{4,5},{5,6},{6,7},{7,4},{8,9},{9,10},{10,1... | collective-permute-start | bytes 393224 | tf_op jit(solution)/shard_map/cond/branch_0_fun/ppermute | solution.py:472
  42.5 6.2 %collective-permute-start.22 = (f32[128,128]{1,0:T(8,128)S(1)}, f32[128,128]{1,0:T(8,128)S(1)}, u32[]{:S(2)}, u32[]{:S(2)}) collective-permute-start(f32[128,128]{1,0:T(8,128)S(1)} %get-tuple-element.177), channel_id=1, source_target_pairs={{0,1},{1,0},{2,3},{3,2},{4,5},{5,4},{6,7},{7,6},{8,9},{9,8},{10,11... | collective-permute-start | bytes 196616 | tf_op jit(solution)/shard_map/ppermute | solution.py:527
  43.9 17.1 %collective-permute-start.21 = (f32[128,512]{1,0:T(8,128)S(1)}, f32[128,512]{1,0:T(8,128)S(1)}, u32[]{:S(2)}, u32[]{:S(2)}) collective-permute-start(f32[128,512]{1,0:T(8,128)S(1)} %get-tuple-element.183.refs_0_), channel_id=1, source_target_pairs={{0,24},{4,28},{8,0},{12,4},{16,8},{20,12},{24,16},{28,20},{32,56},... | collective-permute-start | bytes 786440 | tf_op jit(solution)/shard_map/ppermute | solution.py:524
  45.1 15.9 %collective-permute-start.20 = (f32[128,512]{1,0:T(8,128)S(1)}, f32[128,512]{1,0:T(8,128)S(1)}, u32[]{:S(2)}, u32[]{:S(2)}) collective-permute-start(f32[128,512]{1,0:T(8,128)S(1)} %get-tuple-element.183.refs_0_), channel_id=1, source_target_pairs={{0,16},{4,20},{8,24},{12,28},{16,0},{20,4},{24,8},{28,12},{32,48},... | collective-permute-start | bytes 786440 | tf_op jit(solution)/shard_map/ppermute | solution.py:524
  46.6 14.5 %collective-permute-start.19 = (f32[128,512]{1,0:T(8,128)S(1)}, f32[128,512]{1,0:T(8,128)S(1)}, u32[]{:S(2)}, u32[]{:S(2)}) collective-permute-start(f32[128,512]{1,0:T(8,128)S(1)} %get-tuple-element.183.refs_0_), channel_id=1, source_target_pairs={{0,8},{4,12},{8,16},{12,20},{16,24},{20,28},{24,0},{28,4},{32,40},... | collective-permute-start | bytes 786440 | tf_op jit(solution)/shard_map/ppermute | solution.py:524
  48.7 4.4 %collective-permute-start.23 = (f32[128,128]{1,0:T(8,128)S(1)}, f32[128,128]{1,0:T(8,128)S(1)}, u32[]{:S(2)}, u32[]{:S(2)}) collective-permute-start(f32[128,128]{1,0:T(8,128)S(1)} %add.49.refs_0_), channel_id=1, source_target_pairs={{0,3},{1,2},{2,1},{3,0},{4,7},{5,6},{6,5},{7,4},{8,11},{9,10},{10,... | collective-permute-start | bytes 196616 | tf_op jit(solution)/shard_map/ppermute | solution.py:527
  53.1 11.4 %copy-start = (f32[256,4096]{1,0:T(8,128)S(1)}, f32[256,4096]{1,0:T(8,128)}, u32[]{:S(2)}) copy-start(f32[256,4096]{1,0:T(8,128)} %g_ref.5) | copy-start | bytes 12582916
  61.1 5.1 %collective-permute-start.24 = (f32[128,512]{1,0:T(8,128)S(1)}, f32[128,512]{1,0:T(8,128)S(1)}, u32[]{:S(2)}, u32[]{:S(2)}) collective-permute-start(f32[128,512]{1,0:T(8,128)S(1)} %get-tuple-element.183.refs_0_), channel_id=1, source_target_pairs={{0,4},{4,0},{8,12},{12,8},{16,20},{20,16},{24,28},{28,24},{32,36},... | collective-permute-start | bytes 786440 | tf_op jit(solution)/shard_map/ppermute | solution.py:532
  63.9 2.3 %collective-permute-start.25 = (f32[128,512]{1,0:T(8,128)S(1)}, f32[128,512]{1,0:T(8,128)S(1)}, u32[]{:S(2)}, u32[]{:S(2)}) collective-permute-start(f32[128,512]{1,0:T(8,128)S(1)} %collective-permute-done.19.refs_1_), channel_id=1, source_target_pairs={{0,4},{4,0},{8,12},{12,8},{16,20},{20,16},{24,28},{28,24},{32,36},... | collective-permute-start | bytes 786440 | tf_op jit(solution)/shard_map/ppermute | solution.py:532
  64.0 2.2 %collective-permute-start.26 = (f32[128,512]{1,0:T(8,128)S(1)}, f32[128,512]{1,0:T(8,128)S(1)}, u32[]{:S(2)}, u32[]{:S(2)}) collective-permute-start(f32[128,512]{1,0:T(8,128)S(1)} %collective-permute-done.20.refs_2_), channel_id=1, source_target_pairs={{0,4},{4,0},{8,12},{12,8},{16,20},{20,16},{24,28},{28,24},{32,36},... | collective-permute-start | bytes 786440 | tf_op jit(solution)/shard_map/ppermute | solution.py:532
  64.4 1.8 %collective-permute-start.27 = (f32[128,512]{1,0:T(8,128)S(1)}, f32[128,512]{1,0:T(8,128)S(1)}, u32[]{:S(2)}, u32[]{:S(2)}) collective-permute-start(f32[128,512]{1,0:T(8,128)S(1)} %collective-permute-done.21.refs_3_), channel_id=1, source_target_pairs={{0,4},{4,0},{8,12},{12,8},{16,20},{20,16},{24,28},{28,24},{32,36},... | collective-permute-start | bytes 786440 | tf_op jit(solution)/shard_map/ppermute | solution.py:532
